TPU v7x, 32 devices: a whole 2x2x4 slice. The times are simulated.
32 devices in a mesh: seq: 8 (over z, x), fsdp: 4 (over y, core).
Axes of the slice: x: 2, y: 2, z: 4, core: 2. Of those that a mesh axis runs over, the one named last changes fastest.
Arguments:
- x_in: bfloat16 [4, 1024, 2048], P('fsdp', 'seq'), may hold values from -6 to 6
- cotangent: bfloat16 [4, 1024, 2048], P('fsdp', 'seq'), may hold values from -6 to 6
- doc_lengths: int32 [4, 8], P('fsdp'), may hold values from 1 to 897, 1024 in all within a row
- norm_gain: bfloat16 [2048], P('fsdp'), may hold values from 0.099609375 to 1.8984375
- in_weight: bfloat16 [2048, 8192], P('fsdp'), may hold values from -0.125 to 0.125
- conv_weight: bfloat16 [4096, 4], P('fsdp'), may hold values from -3 to 3
- conv_bias: bfloat16 [4096], P('fsdp'), may hold values from -1 to 1
- x_weight: bfloat16 [4096, 160], P('fsdp'), may hold values from -0.09375 to 0.09375
- dt_weight: bfloat16 [4096, 128], P('fsdp'), may hold values from -0.5 to 0.5
- dt_bias: bfloat16 [4096], P('fsdp'), may hold values from -5.5 to -3.5
- a_log: bfloat16 [4096, 16], P('fsdp'), may hold values from -9.1 to 1.4
- skip_weight: bfloat16 [4096], P('fsdp'), may hold values from 0.5 to 1.5
- out_weight: bfloat16 [4096, 2048], P('fsdp'), may hold values from -0.1875 to 0.1875
Outputs:
- block_out: bfloat16 [4, 1024, 2048], P('fsdp', 'seq')
- x_grad: float32 [4, 1024, 2048], P('fsdp', 'seq')
- gain_grad: float32 [2048], P(('seq', 'fsdp'))
- in_grad: float32 [2048, 8192], P(('seq', 'fsdp'))
- conv_w_grad: float32 [4096, 4], P(('seq', 'fsdp'))
- conv_b_grad: float32 [4096], P(('seq', 'fsdp'))
- x_proj_grad: float32 [4096, 160], P(('seq', 'fsdp'))
- dt_grad: float32 [4096, 128], P(('seq', 'fsdp'))
- bias_dt_grad: float32 [4096], P(('seq', 'fsdp'))
- a_log_grad: float32 [4096, 16], P(('seq', 'fsdp'))
- skip_grad: float32 [4096], P(('seq', 'fsdp'))
- out_grad: float32 [4096, 2048], P(('seq', 'fsdp'))
Inputs may be any that keep to these rules, and one draw needn't show every extreme that they name: `doc_lengths`: each row lists 8 document lengths in order that sum to 1024; one is exactly 897.
All inputs are finite; a program needn't handle non-finite values.
Results may differ from a plain program's by a relative error of at most 0.009.
Values may be sent and summed in bfloat16 or wider, within the bound.
No kernel may reach another device: no remote copies, remote signals or barrier semaphores. Data moves between devices by JAX's collectives and lax.ppermute only.
A program may use at most 448 MiB of HBM per device.

v0:
```python
import jax
import jax.numpy as jnp
from jax import lax
from jax.sharding import PartitionSpec as P

INNER = 4096
STATE = 16
DT_RANK = 128
CONV = 4
GROUP = 16


NORM_EPS = 1e-05


def from_behind(array, axis, by):
    size = lax.axis_size(axis)
    pairs = [(i, i + by) for i in range(size) if 0 <= i + by < size]
    return lax.ppermute(array, axis, pairs)


def prefix(array, axis, join, neutral):
    place = lax.axis_index(axis)
    gathered = jax.tree.map(
        lambda a, kind: lax.all_gather(a.astype(kind), axis), array, (jnp.bfloat16, jnp.bfloat16)
    )
    state = jax.tree.map(lambda a, e: jnp.zeros_like(a) + jnp.asarray(e, a.dtype), array, neutral)

    def one(step, state):
        return join(
            state,
            jax.tree.map(
                lambda a, own: lax.dynamic_index_in_dim(a, step, 0, False).astype(own.dtype),
                gathered,
                array,
            ),
        )

    return lax.fori_loop(0, place, one, state)


def prefix_2(part, axis, combine, identity):
    count = lax.axis_size(axis)
    place = lax.axis_index(axis)
    ahead = count - 1 - place
    gathered = jax.tree.map(lambda a: lax.all_gather(a, axis), part)
    state = jax.tree.map(lambda a, e: jnp.zeros_like(a) + jnp.asarray(e, a.dtype), part, identity)

    def one(step, state):
        source = count - 1 - step
        return combine(
            state, jax.tree.map(lambda a: lax.dynamic_index_in_dim(a, source, 0, False), gathered)
        )

    return lax.fori_loop(0, ahead, one, state)


def group_step(decay_rate, carry_state, pieces):
    step_c, b_c, c_c, act_c, keep_c = pieces
    running = carry_state
    outputs = []
    for token_place in range(GROUP):
        decay_now = jnp.exp(step_c[token_place][:, None] * decay_rate) * keep_c[token_place]
        drive_now = (step_c[token_place] * act_c[token_place])[:, None] * b_c[token_place][None, :]
        running = decay_now * running + drive_now
        outputs.append(jnp.sum(running * c_c[token_place][None, :], axis=1))
    return (running, jnp.stack(outputs))


def run_scan(start_state, decay_rate, step_size, b_in, c_out, activated, keep_state):
    blocks = step_size.shape[0] // GROUP
    pieces = (
        step_size.reshape(blocks, GROUP, -1),
        b_in.reshape(blocks, GROUP, -1),
        c_out.reshape(blocks, GROUP, -1),
        activated.reshape(blocks, GROUP, -1),
        keep_state.reshape(blocks, GROUP),
    )
    checked = jax.checkpoint(group_step)

    def advance(carry_state, one_piece):
        return checked(decay_rate, carry_state, one_piece)

    final_state, outputs = lax.scan(advance, start_state, pieces)
    return (final_state, outputs.reshape(step_size.shape[0], -1))


def doc_masks(lengths, positions):
    doc_ends = jnp.cumsum(lengths)
    doc_starts = doc_ends - lengths

    def segment_of(places):
        return jnp.sum((doc_starts[None, :] <= places[:, None]).astype(jnp.int32), axis=1)

    own_doc = segment_of(positions)
    valid_taps = []
    for offset in range(CONV):
        source = positions - (CONV - 1 - offset)
        valid_taps.append(((source >= 0) & (segment_of(source) == own_doc)).astype(jnp.float32))
    begins = jnp.any(doc_starts[None, :] == positions[:, None], axis=1)
    keep_state = 1.0 - begins.astype(jnp.float32)
    return (jnp.stack(valid_taps), keep_state)


def combine_maps(earlier, later):
    return (earlier[0] * later[0], later[0] * earlier[1] + later[1])


def silu_slope(values):
    sigmoid_val = jax.nn.sigmoid(values)
    return sigmoid_val * (1.0 + values * (1.0 - sigmoid_val))


def contract_rows(left_mat, right_mat):
    return lax.dot_general(
        left_mat, right_mat, (((0,), (0,)), ((), ())), preferred_element_type=jnp.float32
    )


def contract_cols(left_mat, right_mat):
    return lax.dot_general(
        left_mat, right_mat, (((1,), (1,)), ((), ())), preferred_element_type=jnp.float32
    )


def local(
    x_in,
    cotangent,
    doc_lengths,
    norm_gain,
    in_weight,
    conv_weight,
    conv_bias,
    x_weight,
    dt_weight,
    dt_bias,
    a_log,
    skip_weight,
    out_weight,
):
    gathered = (
        lax.all_gather(norm_gain, "fsdp", axis=0, tiled=True),
        lax.all_gather(in_weight, "fsdp", axis=0, tiled=True),
        lax.all_gather(conv_weight, "fsdp", axis=0, tiled=True),
        lax.all_gather(conv_bias, "fsdp", axis=0, tiled=True),
        lax.all_gather(x_weight, "fsdp", axis=0, tiled=True),
        lax.all_gather(dt_weight, "fsdp", axis=0, tiled=True),
        lax.all_gather(dt_bias, "fsdp", axis=0, tiled=True),
        lax.all_gather(a_log, "fsdp", axis=0, tiled=True),
        lax.all_gather(skip_weight, "fsdp", axis=0, tiled=True),
        lax.all_gather(out_weight, "fsdp", axis=0, tiled=True),
    )
    gain_vec, w_in, conv_w, conv_b, w_x, w_dt, bias_dt, log_rate, skip_vec, w_out = gathered
    tokens = x_in.shape[1]
    x_row = x_in[0].astype(jnp.float32)
    places = lax.axis_index("seq") * tokens + jnp.arange(tokens, dtype=jnp.int32)
    valid_taps, keep_state = doc_masks(doc_lengths[0], places)
    inv_rms = lax.rsqrt(jnp.mean(x_row * x_row, axis=1, keepdims=True) + NORM_EPS)
    normed = x_row * inv_rms
    gain_f = gain_vec.astype(jnp.float32)
    lowered = (normed * gain_f).astype(jnp.bfloat16)
    projected = jnp.dot(lowered, w_in, preferred_element_type=jnp.float32)
    conv_in = projected[:, :INNER].astype(jnp.bfloat16)
    gate_z = projected[:, INNER:]
    edge_rows = from_behind(conv_in[tokens - (CONV - 1) :], "seq", 1)
    extended = jnp.concatenate([edge_rows, conv_in], axis=0).astype(jnp.float32)
    conv_wf = conv_w.astype(jnp.float32)
    conv_out = conv_b.astype(jnp.float32)[None, :]
    for offset in range(CONV):
        conv_out = (
            conv_out
            + conv_wf[:, offset] * extended[offset : offset + tokens] * valid_taps[offset][:, None]
        )
    activated = jax.nn.silu(conv_out).astype(jnp.bfloat16)
    act_f = activated.astype(jnp.float32)
    mixed_proj = jnp.dot(activated, w_x, preferred_element_type=jnp.float32)
    low_rank = mixed_proj[:, :DT_RANK].astype(jnp.bfloat16)
    b_in = mixed_proj[:, DT_RANK : DT_RANK + STATE]
    c_out = mixed_proj[:, DT_RANK + STATE :]
    pre_step = contract_cols(low_rank, w_dt) + bias_dt.astype(jnp.float32)
    step_size = jax.nn.softplus(pre_step)
    decay_rate = -jnp.exp(log_rate.astype(jnp.float32))
    through = jnp.exp(decay_rate * jnp.sum(step_size, axis=0)[:, None]) * jnp.prod(keep_state)
    zero_state = jnp.zeros((INNER, STATE), jnp.float32)
    unit_state = jnp.ones((INNER, STATE), jnp.float32)
    local_last, unused = run_scan(zero_state, decay_rate, step_size, b_in, c_out, act_f, keep_state)
    unused_prod, state_in = prefix(
        (through, local_last), "seq", combine_maps, (unit_state, zero_state)
    )

    def scan_part(start_state, rate_in, steps_in, b_part, c_part, act_part):
        return run_scan(start_state, rate_in, steps_in, b_part, c_part, act_part, keep_state)

    (final_state, scan_y), scan_back = jax.vjp(
        scan_part, state_in, decay_rate, step_size, b_in, c_out, act_f
    )
    skip_f = skip_vec.astype(jnp.float32)
    y_total = scan_y + skip_f * act_f
    gate_act = jax.nn.silu(gate_z)
    branch = (y_total * gate_act).astype(jnp.bfloat16)
    block_out = (x_row + jnp.dot(branch, w_out, preferred_element_type=jnp.float32)).astype(
        jnp.bfloat16
    )
    regathered = (
        lax.all_gather(norm_gain, "fsdp", axis=0, tiled=True),
        lax.all_gather(in_weight, "fsdp", axis=0, tiled=True),
        lax.all_gather(conv_weight, "fsdp", axis=0, tiled=True),
        lax.all_gather(conv_bias, "fsdp", axis=0, tiled=True),
        lax.all_gather(x_weight, "fsdp", axis=0, tiled=True),
        lax.all_gather(dt_weight, "fsdp", axis=0, tiled=True),
        lax.all_gather(dt_bias, "fsdp", axis=0, tiled=True),
        lax.all_gather(a_log, "fsdp", axis=0, tiled=True),
        lax.all_gather(skip_weight, "fsdp", axis=0, tiled=True),
        lax.all_gather(out_weight, "fsdp", axis=0, tiled=True),
    )
    gain_vec, w_in, conv_w, conv_b, w_x, w_dt, bias_dt, log_rate, skip_vec, w_out = regathered
    gain_f = gain_vec.astype(jnp.float32)
    conv_wf = conv_w.astype(jnp.float32)
    skip_f = skip_vec.astype(jnp.float32)
    cot_low = cotangent[0]
    cot_f = cot_low.astype(jnp.float32)
    d_branch = contract_cols(cot_low, w_out)
    out_grad = contract_rows(branch, cot_low)
    d_y = d_branch * gate_act
    d_gate = d_branch * y_total * silu_slope(gate_z)
    skip_grad = jnp.sum(d_y * act_f, axis=0)
    local_adj = scan_back((zero_state, d_y))[0]
    unused_prod, adj_in = prefix_2(
        (through, local_adj), "seq", combine_maps, (unit_state, zero_state)
    )
    unused_start, rate_grad, d_step, d_b, d_c, d_act_scan = scan_back((adj_in, d_y))
    a_log_grad = rate_grad * decay_rate
    d_pre = d_step * jax.nn.sigmoid(pre_step)
    bias_dt_grad = jnp.sum(d_pre, axis=0)
    d_pre_low = d_pre.astype(jnp.bfloat16)
    dt_grad = contract_rows(d_pre_low, low_rank)
    d_low_rank = jnp.dot(d_pre_low, w_dt, preferred_element_type=jnp.float32)
    d_mixed = jnp.concatenate([d_low_rank, d_b, d_c], axis=1).astype(jnp.bfloat16)
    x_proj_grad = contract_rows(activated, d_mixed)
    d_act = d_y * skip_f + d_act_scan + contract_cols(d_mixed, w_x)
    d_conv = d_act * silu_slope(conv_out)
    conv_b_grad = jnp.sum(d_conv, axis=0)
    d_extended = jnp.zeros((tokens + CONV - 1, INNER), jnp.float32)
    conv_columns = []
    for offset in range(CONV):
        masked = d_conv * valid_taps[offset][:, None]
        conv_columns.append(jnp.sum(masked * extended[offset : offset + tokens], axis=0))
        d_extended = d_extended + jnp.pad(
            masked * conv_wf[:, offset], ((offset, CONV - 1 - offset), (0, 0))
        )
    conv_w_grad = jnp.stack(conv_columns, axis=1)
    spill_rows = from_behind(d_extended[: CONV - 1].astype(jnp.bfloat16), "seq", -1).astype(
        jnp.float32
    )
    d_conv_in = d_extended[CONV - 1 :] + jnp.concatenate(
        [jnp.zeros((tokens - CONV + 1, INNER), jnp.float32), spill_rows], axis=0
    )
    d_proj = jnp.concatenate([d_conv_in, d_gate], axis=1).astype(jnp.bfloat16)
    d_lowered = contract_cols(d_proj, w_in)
    gain_grad = jnp.sum(d_lowered * normed, axis=0)
    d_norm = d_lowered * gain_f
    x_grad = cot_f + inv_rms * (d_norm - normed * jnp.mean(d_norm * normed, axis=1, keepdims=True))
    in_grad = lax.psum_scatter(
        contract_rows(lowered, d_proj), ("seq", "fsdp"), scatter_dimension=0, tiled=True
    )
    rest_sums = (
        lax.psum_scatter(gain_grad, ("seq", "fsdp"), scatter_dimension=0, tiled=True),
        lax.psum_scatter(conv_w_grad, ("seq", "fsdp"), scatter_dimension=0, tiled=True),
        lax.psum_scatter(conv_b_grad, ("seq", "fsdp"), scatter_dimension=0, tiled=True),
        lax.psum_scatter(x_proj_grad, ("seq", "fsdp"), scatter_dimension=0, tiled=True),
        lax.psum_scatter(dt_grad, ("seq", "fsdp"), scatter_dimension=0, tiled=True),
        lax.psum_scatter(bias_dt_grad, ("seq", "fsdp"), scatter_dimension=0, tiled=True),
        lax.psum_scatter(a_log_grad, ("seq", "fsdp"), scatter_dimension=0, tiled=True),
        lax.psum_scatter(skip_grad, ("seq", "fsdp"), scatter_dimension=0, tiled=True),
        lax.psum_scatter(out_grad, ("seq", "fsdp"), scatter_dimension=0, tiled=True),
    )
    return (
        block_out[None],
        x_grad[None],
        rest_sums[0],
        in_grad,
        rest_sums[1],
        rest_sums[2],
        rest_sums[3],
        rest_sums[4],
        rest_sums[5],
        rest_sums[6],
        rest_sums[7],
        rest_sums[8],
    )


def solution(mesh):
    in_specs = (
        P("fsdp", "seq", None),
        P("fsdp", "seq", None),
        P("fsdp", None),
        P("fsdp"),
        P("fsdp", None),
        P("fsdp", None),
        P("fsdp"),
        P("fsdp", None),
        P("fsdp", None),
        P("fsdp"),
        P("fsdp", None),
        P("fsdp"),
        P("fsdp", None),
    )
    out_specs = (
        P("fsdp", "seq", None),
        P("fsdp", "seq", None),
        P(("seq", "fsdp")),
        P(("seq", "fsdp"), None),
        P(("seq", "fsdp"), None),
        P(("seq", "fsdp")),
        P(("seq", "fsdp"), None),
        P(("seq", "fsdp"), None),
        P(("seq", "fsdp")),
        P(("seq", "fsdp"), None),
        P(("seq", "fsdp")),
        P(("seq", "fsdp"), None),
    )
    return jax.shard_map(local, mesh=mesh, in_specs=in_specs, out_specs=out_specs, check_vma=False)
```

profile of v0, /device:TPU:0, one launch (start us, length us, event | category | flops | bytes accessed | tf_op | source)
XLA Modules:
  0.0 3135.3 jit_solution(8494408623290402037)
XLA Ops:
  23.1 190.8 %all-gather.14.cloned.1.call-done = bf16[2048,8192]{1,0:T(8,128)(2,1)} async-done(((bf16[512,8192]{1,0:T(8,128)(2,1)}), bf16[2048,8192]{1,0:T(8,128)(2,1)}) %all-gather.14.cloned.1.call-update) | async-done | bytes 33554448 | tf_op jit(solution)/shard_map/all_gather | solution.py:143
  213.8 18.9 fusion.128
  257.8 64.3 %all-gather.20.cloned.1.call-done = bf16[4096,2048]{1,0:T(8,128)(2,1)} async-done(((bf16[1024,2048]{1,0:T(8,128)(2,1)}), bf16[4096,2048]{1,0:T(8,128)(2,1)}) %all-gather.20.cloned.1.call-update) | async-done | bytes 16777232 | tf_op jit(solution)/shard_map/all_gather | solution.py:151
  322.2 15.1 multiply_reduce_fusion.80
  343.8 16.3 all-gather.18.cloned.1.call-done
  368.6 140.0 %while.94 = (s32[]{:T(128)}, f32[4096,16]{0,1:T(8,128)S(1)}, f32[8,16,4096]{2,1,0:T(8,128)}, f32[4096,16]{0,1:T(8,128)S(1)}, f32[8,16]{1,0:T(8,128)}, /*index=5*...) while((s32[]{:T(128)}, f32[4096,16]{0,1:T(8,128)S(1)}, ...), condition=%wide.region_10.11_spmd.clone, body=%wide.region_9.10_spmd.clone.sunk | while | flops 5373970 | bytes 3149663 | solution.py:84
  516.0 118.4 %while.95 = (s32[]{:T(128)}, f32[4096,16]{0,1:T(8,128)S(1)}, f32[8,16,4096]{2,1,0:T(8,128)}, f32[8,16,16]{2,1,0:T(8,128)}, f32[8,16]{1,0:T(8,128)}, /*index=5*/f...) while((s32[]{:T(128)}, f32[4096,16]{0,1:T(8,128)S(1)}, ...), condition=%wide.region_32.33_spmd.clone, body=%wide.region_31.32_spmd.clone.sunk | while | flops 5308420 | bytes 3937743 | solution.py:84
  640.8 232.5 %while.92 = (s32[]{:T(128)}, f32[4096,16]{0,1:T(8,128)S(1)}, f32[8,16,4096]{2,1,0:T(8,128)}, f32[8,4096,16]{1,2,0:T(8,128)}, f32[8,16,4096]{2,1,0:T(8,128)}, /*i...) while((s32[]{:T(128)}, f32[4096,16]{0,1:T(8,128)S(1)}, ...), condition=%wide.region_30.31_spmd, body=%wide.region_13.30_spmd.sunk | while | flops 11272209 | bytes 8265381 | solution.py:84
  650.1 11.8 multiply_reduce_fusion.104
  707.8 11.8 multiply_reduce_fusion.104
  737.0 11.8 multiply_reduce_fusion.104
  766.0 11.8 multiply_reduce_fusion.104
  795.3 11.8 multiply_reduce_fusion.104
  881.6 21.5 while.93
  907.4 602.1 %while.96 = (s32[]{:T(128)}, f32[4096,16]{0,1:T(8,128)}, f32[4096,16]{0,1:T(8,128)S(1)}, f32[8,16,4096]{2,1,0:T(8,128)}, bf16[8,16,16]{2,1,0:T(8,128)(2,1)}, /*i...) while((s32[]{:T(128)}, f32[4096,16]{0,1:T(8,128)}, ...), condition=%wide.region_100.101_spmd.clone, body=%wide.region_35.100_spmd.clone.sunk | while | flops 47324164 | bytes 31624040 | solution.py:84
  953.3 12.2 select_add_fusion.2
  1028.5 12.2 select_add_fusion.2
  1103.7 12.2 select_add_fusion.2
  1178.9 12.2 select_add_fusion.2
  1254.1 12.2 select_add_fusion.2
  1329.3 12.2 select_add_fusion.2
  1404.6 12.2 select_add_fusion.2
  1479.8 12.2 select_add_fusion.2
  1536.2 13.1 fusion.95
  1560.9 23.6 fusion.85
  1593.5 16.3 fusion.93
  1609.8 37.7 %all-reduce.89 = (f32[2048]{0:T(1024)S(1)}, f32[4096]{0:T(1024)S(1)}, f32[4096]{0:T(1024)S(1)}, f32[4096]{0:T(1024)S(1)}) all-reduce(f32[2048]{0:T(1024)S(1)} %get-tuple-element.1033, f32[4096]{0:T(1024)S(1)} %copy-done.24, f32[4096]{0:T(1024)S(1)} %copy-done.20, ...), channel_id=6, replica_groups=mesh['seq'=8,'fsdp'=4] {'seq','fsdp'}, use_global_device_ids=true, to_apply=%region_103.104.clone | all-reduce | flops 14336 | bytes 114688
  1663.7 131.0 %reduce-scatter.15.cloned.1.call-done = f32[128,16]{0,1:T(8,128)} async-done(((f32[4096,16]{0,1:T(8,128)}), f32[128,16]{0,1:T(8,128)}) %reduce-scatter.15.cloned.1.call-update) | async-done | bytes 8208 | tf_op jit(solution)/shard_map/reduce_scatter | solution.py:273
  1794.7 135.5 %reduce-scatter.13.cloned.1.call-done = f32[128,128]{1,0:T(8,128)} async-done(((f32[4096,128]{1,0:T(8,128)}), f32[128,128]{1,0:T(8,128)}) %reduce-scatter.13.cloned.1.call-update) | async-done | bytes 65552 | tf_op jit(solution)/shard_map/reduce_scatter | solution.py:271
  1930.2 136.3 %reduce-scatter.11.cloned.1.call-done = f32[128,160]{0,1:T(8,128)} async-done(((f32[4096,160]{0,1:T(8,128)}), f32[128,160]{0,1:T(8,128)}) %reduce-scatter.11.cloned.1.call-update) | async-done | bytes 81936 | tf_op jit(solution)/shard_map/reduce_scatter | solution.py:270
  2066.5 352.9 %reduce-scatter.17.cloned.1.call-done = f32[128,2048]{1,0:T(8,128)} async-done(((f32[4096,2048]{1,0:T(8,128)}), f32[128,2048]{1,0:T(8,128)}) %reduce-scatter.17.cloned.1.call-update) | async-done | bytes 1048592 | tf_op jit(solution)/shard_map/reduce_scatter | solution.py:275
  2419.4 708.8 %reduce-scatter.9.cloned.1.call-done = f32[64,8192]{1,0:T(8,128)} async-done(((f32[2048,8192]{1,0:T(8,128)}), f32[64,8192]{1,0:T(8,128)}) %reduce-scatter.9.cloned.1.call-update) | async-done | bytes 2097168 | tf_op jit(solution)/shard_map/reduce_scatter | solution.py:263
  (1108 shorter events, 1096.8 us)
Async XLA Ops:
  7.2 206.7 %all-gather.14.cloned.1.call-start = ((), (), s32[]{:S(2)}) async-start(), calls=%async_computation.6 | async-start | bytes 41943040 | tf_op jit(solution)/shard_map/all_gather | solution.py:143
  8.0 314.2 %all-gather.20.cloned.1.call-start = ((), (), s32[]{:S(2)}) async-start(), calls=%async_computation.9 | async-start | bytes 20971520 | tf_op jit(solution)/shard_map/all_gather | solution.py:151
  8.7 333.2 %all-gather.16.cloned.1.call-start = ((), (), s32[]{:S(2)}) async-start(), calls=%async_computation.7 | async-start | bytes 1638400 | tf_op jit(solution)/shard_map/all_gather | solution.py:146
  9.4 350.7 %all-gather.18.cloned.1.call-start = ((), (), s32[]{:S(2)}) async-start(), calls=%async_computation.8 | async-start | bytes 1310720 | tf_op jit(solution)/shard_map/all_gather | solution.py:147
  10.0 625.2 %all-gather.22.cloned.1.call-start = ((), (), s32[]{:S(2)}) async-start(), calls=%async_computation.15 | async-start | bytes 1179648 | tf_op jit(solution)/shard_map/all_gather | solution.py:25
  10.1 312.1 %copy-start.45 = (f32[128]{0:T(128)}, f32[128]{0:T(128)S(1)}, u32[]{:S(2)}) copy-start(f32[128]{0:T(128)S(1)} %compare_convert_fusion) | copy-start | bytes 1540
  16.3 216.4 %copy-start.16 = (f32[4,1,512]{2,1,0:T(1,128)}, f32[4,1,512]{2,1,0:T(1,128)S(1)}, u32[]{:S(2)}) copy-start(f32[4,1,512]{2,1,0:T(1,128)S(1)} %convert_element_type.161) | copy-start | bytes 24580
  22.0 300.1 %copy-start.25 = (f32[4096,1]{0,1:T(1,128)}, f32[4096,1]{0,1:T(1,128)S(1)}, u32[]{:S(2)}) copy-start(f32[4096,1]{0,1:T(1,128)S(1)} %get-tuple-element.1572) | copy-start | bytes 49156
  22.0 300.1 %copy-start.27 = (f32[4096,1]{0,1:T(1,128)}, f32[4096,1]{0,1:T(1,128)S(1)}, u32[]{:S(2)}) copy-start(f32[4096,1]{0,1:T(1,128)S(1)} %get-tuple-element.1573) | copy-start | bytes 49156
  22.0 300.1 %copy-start.29 = (f32[4096,1]{0,1:T(1,128)}, f32[4096,1]{0,1:T(1,128)S(1)}, u32[]{:S(2)}) copy-start(f32[4096,1]{0,1:T(1,128)S(1)} %get-tuple-element.1574) | copy-start | bytes 49156
  22.0 300.1 %copy-start.31 = (f32[4096,1]{0,1:T(1,128)}, f32[4096,1]{0,1:T(1,128)S(1)}, u32[]{:S(2)}) copy-start(f32[4096,1]{0,1:T(1,128)S(1)} %get-tuple-element.1575) | copy-start | bytes 49156
  23.1 299.1 %copy-start.38 = (f32[128]{0:T(128)}, f32[128]{0:T(128)S(1)}, u32[]{:S(2)}) copy-start(f32[128]{0:T(128)S(1)} %get-tuple-element.1579) | copy-start | bytes 1540
  23.1 299.1 %copy-start.40 = (f32[128]{0:T(128)}, f32[128]{0:T(128)S(1)}, u32[]{:S(2)}) copy-start(f32[128]{0:T(128)S(1)} %get-tuple-element.1580) | copy-start | bytes 1540
  23.1 299.1 %copy-start.42 = (f32[128]{0:T(128)}, f32[128]{0:T(128)S(1)}, u32[]{:S(2)}) copy-start(f32[128]{0:T(128)S(1)} %get-tuple-element.1581) | copy-start | bytes 1540
  213.8 23.6 copy-start.22
  213.8 29.7 copy-start.34
  213.8 34.9 %copy-start.35 = (bf16[1024]{0:T(1024)(128)(2,1)S(1)}, bf16[1024]{0:T(1024)(128)(2,1)}, u32[]{:S(2)}) copy-start(bf16[1024]{0:T(1024)(128)(2,1)} %param.34) | copy-start | bytes 6148
  234.1 22.0 collective-permute-start
  256.1 66.1 %copy-start.12 = (bf16[1,128,2048]{2,1,0:T(8,128)(2,1)S(1)}, bf16[1,128,2048]{2,1,0:T(8,128)(2,1)}, u32[]{:S(2)}) copy-start(bf16[1,128,2048]{2,1,0:T(8,128)(2,1)} %param.26) | copy-start | bytes 1572868
  343.8 21.1 copy-start.18
  366.3 270.2 %all-gather.24.cloned.1.call-start = ((), (), s32[]{:S(2)}) async-start(), calls=%async_computation.16 | async-start | bytes 1179648 | tf_op jit(solution)/shard_map/all_gather | solution.py:25
  368.6 140.8 %copy-start.36 = (bf16[1024]{0:T(1024)(128)(2,1)S(1)}, bf16[1024]{0:T(1024)(128)(2,1)}, u32[]{:S(2)}) copy-start(bf16[1024]{0:T(1024)(128)(2,1)} %param.36) | copy-start | bytes 6148
  509.3 364.0 %all-gather.26.cloned.1.call-start = ((), (), s32[]{:S(2)}) async-start(), calls=%async_computation.17 | async-start | bytes 2359296 | tf_op jit(solution)/shard_map/all_gather | solution.py:46
  515.9 361.6 %all-gather.28.cloned.1.call-start = ((), (), s32[]{:S(2)}) async-start(), calls=%async_computation.18 | async-start | bytes 2359296 | tf_op jit(solution)/shard_map/all_gather | solution.py:46
  635.1 1027.1 %reduce-scatter.19.cloned.1.call-start = ((), (), s32[]{:S(2)}) async-start(), calls=%async_computation.19 | async-start | bytes 2162688
  1529.1 265.6 %reduce-scatter.15.cloned.1.call-start = ((), (), s32[]{:S(2)}) async-start(), calls=%async_computation.13 | async-start | bytes 270336 | tf_op jit(solution)/shard_map/reduce_scatter | solution.py:273
  1530.0 400.2 %reduce-scatter.13.cloned.1.call-start = ((), (), s32[]{:S(2)}) async-start(), calls=%async_computation.12 | async-start | bytes 2162688 | tf_op jit(solution)/shard_map/reduce_scatter | solution.py:271
  1533.1 533.4 %reduce-scatter.11.cloned.1.call-start = ((), (), s32[]{:S(2)}) async-start(), calls=%async_computation.11 | async-start | bytes 2703360 | tf_op jit(solution)/shard_map/reduce_scatter | solution.py:270
  1535.2 884.3 %reduce-scatter.17.cloned.1.call-start = ((), (), s32[]{:S(2)}) async-start(), calls=%async_computation.14 | async-start | bytes 34603008 | tf_op jit(solution)/shard_map/reduce_scatter | solution.py:275
  1549.4 1578.9 %reduce-scatter.9.cloned.1.call-start = ((), (), s32[]{:S(2)}) async-start(), calls=%async_computation.10 | async-start | bytes 69206016 | tf_op jit(solution)/shard_map/reduce_scatter | solution.py:263
  1553.7 5.9 collective-permute-start.1
  1593.5 16.3 copy-start.24
  (46 other events, 283.7 us)
Sparse Core Ops, SparseCore 0:
  9.6 204.2 all-gather.13
  215.4 106.7 all-gather.19
  323.7 18.1 all-gather.15
  343.4 16.7 all-gather.17
  366.4 40.1 all-gather.21
  509.4 40.1 all-gather.23
  552.4 48.0 all-gather.25
  635.3 49.3 all-gather.27
  1529.2 132.9 reduce-scatter.18
  1664.9 129.7 reduce-scatter.14
  1797.5 132.5 reduce-scatter.12
  1933.0 133.4 reduce-scatter.10
  2069.5 349.9 reduce-scatter.16
  2422.3 705.8 reduce-scatter.8
where the time goes:
time: 3160 us; the launch traced here: 3140 us
  waiting for transfers between devices  1760 us (56%)
  other arithmetic  913 us (29%)
  local copies, waits for them, and re-layouts  252 us (8%)
  matrix products  114 us (4%)
  blocking collectives  71.1 us (2%)
    reduce_scatter x1, waiting for transfers between devices, local(): lax.psum_scatter(contract_rows(lowered, d_proj), ('seq', 'fsdp'), scatter...  709 us
    reduce_scatter x1, waiting for transfers between devices, local(): lax.psum_scatter(out_grad, ('seq', 'fsdp'), scatter_dimension=0, tiled=True)  353 us
    reduce_sum x48, other arithmetic, group_step(): outputs.append(jnp.sum(running * c_c[token_place][None, :], axis=1))  258 us
    reduce_sum x64, other arithmetic, group_step(): step_c[token_place][:, None] * decay_rate  243 us
    all_gather x1, waiting for transfers between devices, local(): lax.all_gather(in_weight, 'fsdp', axis=0, tiled=True)  191 us
    reduce_scatter x1, waiting for transfers between devices, local(): lax.psum_scatter(x_proj_grad, ('seq', 'fsdp'), scatter_dimension=0, tiled...  136 us
    reduce_scatter x1, waiting for transfers between devices, local(): lax.psum_scatter(dt_grad, ('seq', 'fsdp'), scatter_dimension=0, tiled=True)  135 us
    reduce_scatter x1, waiting for transfers between devices, local(): lax.psum_scatter(a_log_grad, ('seq', 'fsdp'), scatter_dimension=0, tiled=...  131 us
  transfers between devices with their start and end apart: 16, of which 11 were waited for; matrix products, arithmetic and copies ran while one was open for 20% of the time, Pallas kernels for 0%

commit v1 on v0

v1 whole, which is shorter than its diff:
```python
import jax
import jax.numpy as jnp
from jax import lax
from jax.experimental import pallas as pl
from jax.experimental.pallas import tpu as pltpu
from jax.sharding import PartitionSpec as P

INNER = 4096
STATE = 16
DT_RANK = 128
CONV = 4
MIXED = DT_RANK + 2 * STATE
NORM_EPS = 1e-05
LOG2E = 1.4426950408889634
BLOCK = 128
WIDE = 256
GROUP = 16
RESET = 1e30
VMEM = 56 << 20
F32, BF16 = jnp.float32, jnp.bfloat16


def dot_nn(a, b):
    return lax.dot_general(a, b, (((1,), (0,)), ((), ())), preferred_element_type=F32)


def dot_tn(a, b):
    return lax.dot_general(a, b, (((0,), (0,)), ((), ())), preferred_element_type=F32)


def dot_nt(a, b):
    return lax.dot_general(a, b, (((1,), (1,)), ((), ())), preferred_element_type=F32)


def silu_slope(values):
    sig = jax.nn.sigmoid(values)
    return sig * (1.0 + values * (1.0 - sig))


def softplus(values):
    return jnp.maximum(values, 0.0) + jnp.log1p(jnp.exp(-jnp.abs(values)))


def sigmoid(values):
    return 1.0 / (1.0 + jnp.exp(-values))


ANY = pl.BlockSpec(memory_space=pl.ANY)


def ordered_kernel(*refs):
    pass


def after(value, *others):
    return pl.pallas_call(
        ordered_kernel,
        in_specs=[ANY] * (1 + len(others)),
        out_specs=ANY,
        out_shape=jax.ShapeDtypeStruct(value.shape, value.dtype),
        input_output_aliases={0: 0},
        name="after",
    )(value, *others)


def doc_masks(lengths, count):
    docs = lengths.shape[0]
    order = jnp.arange(docs, dtype=jnp.int32)
    starts = jnp.sum(jnp.where(order[None, :] < order[:, None], lengths[None, :], 0), axis=1)
    places = jnp.arange(count, dtype=jnp.int32)

    def segment_of(at):
        return jnp.sum((starts[None, :] <= at[:, None]).astype(jnp.int32), axis=1)

    own = segment_of(places)
    columns = []
    for k in range(CONV):
        source = places - (CONV - 1 - k)
        columns.append(((source >= 0) & (segment_of(source) == own)).astype(F32))
    columns.append(jnp.any(starts[None, :] == places[:, None], axis=1).astype(F32))
    columns += [jnp.zeros_like(columns[0])] * (8 - len(columns))
    return jnp.stack(columns, axis=1)


ROW_LOG, ROW_CONV, ROW_CONV_B, ROW_DT_B, ROW_SKIP = 0, 16, 20, 21, 22


def assemble_kernel(slots_ref, *refs):
    n = slots_ref.shape[0]
    pieces, (w_ref, gain_ref, gains_ref, w_sem, gain_sem) = refs[:n], refs[n:]
    deep = w_ref.shape[0] // n
    copies = []
    for k, piece in enumerate(pieces):
        slot = slots_ref[k]
        at = pl.multiple_of(slot * deep, deep)
        copies.append(pltpu.make_async_copy(piece.at[:deep], w_ref.at[pl.ds(at, deep)], w_sem.at[k]))
        copies.append(pltpu.make_async_copy(piece.at[deep : deep + GROUP], gains_ref.at[slot], gain_sem.at[k]))
    for copy in copies:
        copy.start()
    for copy in copies:
        copy.wait()
    parts = []
    for i in range(n):
        gains = gains_ref[i].astype(F32)
        lanes = min(deep, gains.shape[1])
        parts += [gains[r : r + 1, :lanes] for r in range(deep // lanes)]
    gain_ref[...] = jnp.concatenate(parts, axis=1)


def assemble(pieces, slots, deep):
    n, columns = len(pieces), pieces[0].shape[1]
    return pl.pallas_call(
        assemble_kernel,
        in_specs=[pl.BlockSpec(memory_space=pltpu.SMEM), *[ANY] * n],
        out_specs=[pl.BlockSpec(memory_space=pltpu.VMEM)] * 2,
        out_shape=[jax.ShapeDtypeStruct((n * deep, columns), BF16), jax.ShapeDtypeStruct((1, n * deep), F32)],
        scratch_shapes=[
            pltpu.VMEM((n, GROUP, columns), BF16),
            pltpu.SemaphoreType.DMA((n,)),
            pltpu.SemaphoreType.DMA((n,)),
        ],
        compiler_params=pltpu.CompilerParams(vmem_limit_bytes=VMEM),
        name="assemble",
    )(slots, *pieces)


def project_kernel(slots_ref, w_in_ref, gain_ref, w_xt_ref, table_ref, mask_ref, *refs):
    n = slots_ref.shape[0]
    pieces = refs[:n]
    (lowered_ref, conv_in_ref, conv_out_ref, act_ref, gate_ref, mixed_ref, line_ref, x_ref, x_sem) = refs[n:]
    rows, width = conv_in_ref.shape
    block = pl.program_id(0)
    tokens = pieces[0].shape[0]

    @pl.when(block == 0)
    def _():
        for k, piece in enumerate(pieces):
            slot = slots_ref[k]
            pltpu.make_async_copy(piece, x_ref.at[slot], x_sem.at[slot]).start()
        line_ref[:8] = jnp.zeros((8, width), F32)

    @pl.when(block > 0)
    def _():
        line_ref[:8] = line_ref[rows:]

    per = rows // tokens
    for i in range(per):
        slot = block * per + i
        pltpu.make_async_copy(pieces[0], x_ref.at[slot], x_sem.at[slot]).wait()
    x = jnp.concatenate([x_ref[block * per + i] for i in range(per)], axis=0).astype(F32)
    inv = lax.rsqrt(jnp.mean(x * x, axis=1, keepdims=True) + NORM_EPS)
    lowered_ref[...] = (x * inv * gain_ref[...]).astype(BF16)
    projected = dot_nn(lowered_ref[...], w_in_ref[...])
    conv_in = projected[:, :width].astype(BF16)
    gate_ref[...] = projected[:, width:]
    conv_in_ref[...] = conv_in
    line_ref[8:] = conv_in.astype(F32)
    conv_out = table_ref[ROW_CONV_B : ROW_CONV_B + 1, :]
    for k in range(CONV):
        taps = table_ref[ROW_CONV + k : ROW_CONV + k + 1, :]
        conv_out = conv_out + taps * line_ref[5 + k : 5 + k + rows] * mask_ref[:, k : k + 1]
    conv_out_ref[...] = conv_out
    act = (conv_out * sigmoid(conv_out)).astype(BF16)
    act_ref[...] = act
    mixed = dot_nt(w_xt_ref[...], act).astype(BF16)
    for i in range(rows // BLOCK):
        mixed_ref[i] = mixed[:, i * BLOCK : (i + 1) * BLOCK]


def rows_spec(width, index=lambda i: i, rows=BLOCK):
    return pl.BlockSpec((rows, width), lambda i: (index(i), 0))


def whole_spec(shape):
    return pl.BlockSpec(shape, lambda i: (0,) * len(shape))


def project(pieces, slots, w_rows, gain, w_xt, table, mask):
    tokens, model = pieces[0].shape
    count = tokens * len(pieces)
    width = w_xt.shape[1]

    def rows(columns):
        return rows_spec(columns, rows=WIDE)

    return pl.pallas_call(
        project_kernel,
        grid=(count // WIDE,),
        in_specs=[
            pl.BlockSpec(memory_space=pltpu.SMEM), whole_spec(w_rows.shape), whole_spec(gain.shape),
            whole_spec(w_xt.shape), whole_spec(table.shape), rows(8), *[ANY] * len(pieces),
        ],
        out_specs=[
            rows(model), rows(width), rows(width), rows(width), rows(width),
            pl.BlockSpec((WIDE // BLOCK, MIXED, BLOCK), lambda i: (i, 0, 0)),
        ],
        out_shape=[
            jax.ShapeDtypeStruct((count, model), BF16),
            jax.ShapeDtypeStruct((count, width), BF16),
            jax.ShapeDtypeStruct((count, width), F32),
            jax.ShapeDtypeStruct((count, width), BF16),
            jax.ShapeDtypeStruct((count, width), F32),
            jax.ShapeDtypeStruct((count // BLOCK, MIXED, BLOCK), BF16),
        ],
        scratch_shapes=[
            pltpu.VMEM((WIDE + 8, width), F32),
            pltpu.VMEM((len(pieces), tokens, model), BF16),
            pltpu.SemaphoreType.DMA((len(pieces),)),
        ],
        compiler_params=pltpu.CompilerParams(vmem_limit_bytes=VMEM),
        cost_estimate=pl.CostEstimate(flops=2 * count * model * 2 * width, bytes_accessed=20 << 20, transcendentals=0),
        name="project",
    )(slots, w_rows, gain, w_xt, table, mask, *pieces)


def spread_groups(values):
    state = lax.broadcasted_iota(jnp.int32, (STATE, GROUP * STATE), 0)
    column = lax.broadcasted_iota(jnp.int32, (STATE, GROUP * STATE), 1)
    pick = jnp.where((column & (STATE - 1)) == state, 1.0, 0.0).astype(BF16)
    tiled = dot_tn(values, pick)
    token = lax.broadcasted_iota(jnp.int32, (BLOCK, GROUP * STATE), 0)
    column = lax.broadcasted_iota(jnp.int32, (BLOCK, GROUP * STATE), 1)
    return jnp.where((token & (GROUP - 1)) == (column >> 4), tiled, 0.0).astype(BF16)


def spread_lanes(values, own_ref, out_ref):
    ones = jnp.ones((BLOCK, BLOCK), BF16)
    for g in range(BLOCK // GROUP):
        here = slice(g * GROUP * STATE, (g + 1) * GROUP * STATE)
        out_ref[here] = dot_nn(jnp.concatenate([values] * GROUP, axis=0) * own_ref[here], ones)


def wide(values, width):
    lanes = values.shape[1]
    return values[:, :width] if width < lanes else jnp.concatenate([values] * (width // lanes), axis=1)


def owns():
    row, column = (lax.broadcasted_iota(jnp.int32, (BLOCK * STATE, BLOCK), i) for i in (0, 1))
    ahead = column - row // STATE
    return (ahead == 0).astype(BF16), ahead[: GROUP * STATE]


def forward_kernel(mixed_ref, act_ref, gate_ref, mask_ref, w_dtt_ref, table_ref, own_ref, _,
                   branch_ref, y_ref, states_ref, _out, h_ref, stepd_ref, drive_ref, b_ref):
    @pl.when(pl.program_id(0) == 0)
    def _():
        h_ref[...] = jnp.zeros_like(h_ref)

    width = act_ref.shape[1]
    act = act_ref[...].astype(F32)
    pre = dot_tn(mixed_ref[0, :DT_RANK], w_dtt_ref[...]) + table_ref[ROW_DT_B : ROW_DT_B + 1, :]
    step = softplus(pre)
    stepd_ref[...] = jnp.where(mask_ref[:, CONV : CONV + 1] > 0.0, RESET, step)
    drive_ref[...] = step * act
    spread_lanes(mixed_ref[0, DT_RANK : DT_RANK + STATE], own_ref, b_ref)
    rate = -jnp.exp(table_ref[ROW_LOG : ROW_LOG + STATE, :]) * LOG2E

    def group(g, h):
        r0 = pl.multiple_of(g * GROUP, GROUP)
        stepd = stepd_ref[pl.ds(r0, GROUP), :]
        drive = drive_ref[pl.ds(r0, GROUP), :]
        for j in range(GROUP):
            at = pl.multiple_of((r0 + j) * STATE, STATE)
            b = wide(b_ref[pl.ds(at, STATE), :], width)
            h = jnp.exp2(stepd[j : j + 1, :] * rate) * h + drive[j : j + 1, :] * b
            states_ref[pl.ds(at, STATE), :] = h.astype(BF16)
        return h

    h_ref[...] = lax.fori_loop(0, BLOCK // GROUP, group, h_ref[...])
    c = spread_groups(mixed_ref[0, DT_RANK + STATE :])
    for g in range(BLOCK // GROUP):
        at = g * GROUP
        y_ref[at : at + GROUP, :] = dot_nn(c[at : at + GROUP], states_ref[at * STATE : (at + GROUP) * STATE])
    y_total = y_ref[...] + table_ref[ROW_SKIP : ROW_SKIP + 1, :] * act
    y_ref[...] = y_total
    gate = gate_ref[...]
    branch_ref[...] = (y_total * (gate * sigmoid(gate))).astype(BF16)


def scan_forward(mixed, act, gate, mask, w_dtt, table, own, w_out):
    count, width = act.shape
    return pl.pallas_call(
        forward_kernel,
        grid=(count // BLOCK,),
        in_specs=[
            pl.BlockSpec((1, MIXED, BLOCK), lambda i: (i, 0, 0)), rows_spec(width), rows_spec(width), rows_spec(8),
            whole_spec(w_dtt.shape), whole_spec(table.shape), whole_spec(own.shape), ANY,
        ],
        out_specs=[rows_spec(width), rows_spec(width), pl.BlockSpec((BLOCK * STATE, width), lambda i: (i, 0)), ANY],
        out_shape=[
            jax.ShapeDtypeStruct((count, width), BF16),
            jax.ShapeDtypeStruct((count, width), F32),
            jax.ShapeDtypeStruct((count * STATE, width), BF16),
            jax.ShapeDtypeStruct(w_out.shape, w_out.dtype),
        ],
        input_output_aliases={7: 3},
        scratch_shapes=[
            pltpu.VMEM((STATE, width), F32),
            pltpu.VMEM((BLOCK, width), F32),
            pltpu.VMEM((BLOCK, width), F32),
            pltpu.VMEM((BLOCK * STATE, BLOCK), F32),
        ],
        compiler_params=pltpu.CompilerParams(vmem_limit_bytes=VMEM),
        cost_estimate=pl.CostEstimate(flops=8 * count * width * STATE * 16, bytes_accessed=64 << 20, transcendentals=0),
        name="scan_forward",
    )(mixed, act, gate, mask, w_dtt, table, own, w_out)


def backward_kernel(mixed_ref, act_ref, gate_ref, d_branch_ref, mask_ref, states_ref, ahead_ref,
                    w_dtt_ref, table_ref, own_ref, offset_ref,
                    d_mixed_ref, d_act_ref, sums_ref, dt_grad_ref,
                    p_ref, dy_ref, stepd_ref, c_ref, s1_ref, s2_ref, bg_ref, dyt_ref, sat_ref, d_b_ref, d_c_ref,
                    adj_a_ref, adj_b_ref, rq_a_ref, rq_b_ref):
    first = pl.program_id(0) == 0
    width = act_ref.shape[1]

    @pl.when(first)
    def _():
        p_ref[...] = jnp.zeros_like(p_ref)
        sums_ref[...] = jnp.zeros_like(sums_ref)
        dt_grad_ref[...] = jnp.zeros_like(dt_grad_ref)
        adj_b_ref[...] = jnp.zeros_like(adj_b_ref)
        rq_b_ref[...] = jnp.zeros_like(rq_b_ref)
        d_b_ref[...] = jnp.zeros_like(d_b_ref)
        d_c_ref[...] = jnp.zeros_like(d_c_ref)
        bg_ref[BLOCK:] = jnp.zeros((GROUP, GROUP * STATE), BF16)

    act = act_ref[...].astype(F32)
    gate = gate_ref[...]
    sig = sigmoid(gate)
    d_branch = d_branch_ref[...]
    dy = d_branch * (gate * sig)
    pre = dot_tn(mixed_ref[0, :DT_RANK], w_dtt_ref[...]) + table_ref[ROW_DT_B : ROW_DT_B + 1, :]
    step = softplus(pre)
    dy_ref[...] = dy
    stepd_ref[...] = jnp.where(mask_ref[:, CONV : CONV + 1] > 0.0, RESET, step)
    dyt_ref[...] = dy.T.astype(BF16)
    sat_ref[...] = (step * act).T.astype(BF16)
    spread_lanes(mixed_ref[0, DT_RANK + STATE :], own_ref, c_ref)
    bg_ref[:BLOCK] = spread_groups(mixed_ref[0, DT_RANK : DT_RANK + STATE])
    raw = -jnp.exp(table_ref[ROW_LOG : ROW_LOG + STATE, :])
    rate = raw * LOG2E
    groups = BLOCK // GROUP
    per = GROUP * STATE
    token = lax.broadcasted_iota(jnp.int32, (GROUP, per), 0)
    column = lax.broadcasted_iota(jnp.int32, (GROUP, per), 1)
    ones = jnp.where(token == (column >> 4), 1.0, 0.0).astype(BF16)
    pick = jnp.where(token == (column & (STATE - 1)), 1.0, 0.0).astype(BF16)

    def steps(g, p, total, adj_ref, rq_ref):
        r0 = pl.multiple_of(g * GROUP, GROUP)
        dy_g = dy_ref[pl.ds(r0, GROUP), :]
        stepd_g = stepd_ref[pl.ds(r0, GROUP), :]
        for j in reversed(range(GROUP)):
            at = pl.multiple_of((r0 + j) * STATE, STATE)
            if j:
                behind = pl.multiple_of((r0 + j - 1) * STATE, STATE)
                before = states_ref[pl.ds(behind, STATE), :]
            else:
                behind = pl.multiple_of(jnp.maximum(r0 - 1, 0) * STATE, STATE)
                before = jnp.where(g > 0, states_ref[pl.ds(behind, STATE), :], ahead_ref[...])
            adj = dy_g[j : j + 1, :] * wide(c_ref[pl.ds(at, STATE), :], width) + p
            adj_ref[j * STATE : (j + 1) * STATE] = adj.astype(BF16)
            p = jnp.exp2(stepd_g[j : j + 1, :] * rate) * adj
            rq = raw * (p * before.astype(F32))
            rq_ref[j * STATE : (j + 1) * STATE] = rq.astype(BF16)
            total = total + stepd_g[j : j + 1, :] * rq
        return p, total

    def sums(g, state_rows, adj_ref, rq_ref):
        r0 = pl.multiple_of(g * GROUP, GROUP)
        adj = adj_ref[...]
        s1_ref[pl.ds(r0, GROUP), :] = dot_nn(bg_ref[pl.ds(r0, GROUP), :], adj)
        s2_ref[pl.ds(r0, GROUP), :] = dot_nn(ones, rq_ref[...])
        here = offset_ref[...] == r0
        d_b_ref[...] = jnp.where(here, dot_nn(adj, sat_ref[...]), d_b_ref[...])
        states = states_ref[pl.ds(state_rows, per), :]
        d_c_ref[...] = jnp.where(here, dot_nn(states, dyt_ref[...]), d_c_ref[...])

    def pair(i, carry):
        p, total = carry
        high = groups - 1 - 2 * i
        low = high - 1
        rows = pl.multiple_of(jnp.minimum(low + 2, groups - 1) * per, per)
        sums(low + 2, rows, adj_b_ref, rq_b_ref)
        p, total = steps(high, p, total, adj_a_ref, rq_a_ref)
        sums(high, pl.multiple_of(high * per, per), adj_a_ref, rq_a_ref)
        return steps(low, p, total, adj_b_ref, rq_b_ref)

    p, total = lax.fori_loop(0, groups // 2, pair, (p_ref[...], sums_ref[:STATE]))
    sums(0, 0, adj_b_ref, rq_b_ref)
    p_ref[...] = p
    sums_ref[:STATE] = total
    d_mixed_ref[0, DT_RANK : DT_RANK + STATE] = dot_nn(pick, d_b_ref[...].astype(BF16)).astype(BF16)
    d_mixed_ref[0, DT_RANK + STATE :] = dot_nn(pick, d_c_ref[...].astype(BF16)).astype(BF16)

    s1, s2 = s1_ref[:BLOCK], s2_ref[:BLOCK]
    d_act_ref[...] = dy * table_ref[ROW_SKIP : ROW_SKIP + 1, :] + step * s1
    d_pre = (act * s1 + s2) * jnp.exp(pre - step)
    sums_ref[STATE : STATE + 1] += jnp.sum(dy * act, axis=0, keepdims=True)
    sums_ref[STATE + 1 : STATE + 2] += jnp.sum(d_pre, axis=0, keepdims=True)
    d_pre = d_pre.astype(BF16)
    dt_grad_ref[...] += dot_nn(mixed_ref[0, :DT_RANK], d_pre)
    d_mixed_ref[0, :DT_RANK] = dot_nt(w_dtt_ref[...], d_pre).astype(BF16)


def scan_backward(mixed, act, gate, d_branch, mask, states, w_dtt, table, own, offsets):
    count, width = act.shape
    blocks = count // BLOCK
    last = blocks - 1
    rows = rows_spec(width, lambda i: last - i)
    mixed_spec = pl.BlockSpec((1, MIXED, BLOCK), lambda i: (last - i, 0, 0))
    per = GROUP * STATE
    return pl.pallas_call(
        backward_kernel,
        grid=(blocks,),
        in_specs=[
            mixed_spec, rows, rows, rows, rows_spec(8, lambda i: last - i),
            pl.BlockSpec((BLOCK * STATE, width), lambda i: (last - i, 0)),
            pl.BlockSpec((STATE, width), lambda i: (jnp.maximum((last - i) * BLOCK - 1, 0), 0)),
            whole_spec(w_dtt.shape), whole_spec(table.shape), whole_spec(own.shape), whole_spec(offsets.shape),
        ],
        out_specs=[mixed_spec, rows, whole_spec((24, width)), whole_spec((DT_RANK, width))],
        out_shape=[
            jax.ShapeDtypeStruct((blocks, MIXED, BLOCK), BF16),
            jax.ShapeDtypeStruct((count, width), F32),
            jax.ShapeDtypeStruct((24, width), F32),
            jax.ShapeDtypeStruct((DT_RANK, width), F32),
        ],
        scratch_shapes=[
            pltpu.VMEM((STATE, width), F32),
            pltpu.VMEM((BLOCK, width), F32),
            pltpu.VMEM((BLOCK, width), F32),
            pltpu.VMEM((BLOCK * STATE, BLOCK), F32),
            pltpu.VMEM((BLOCK + GROUP, width), F32),
            pltpu.VMEM((BLOCK + GROUP, width), F32),
            pltpu.VMEM((BLOCK + GROUP, per), BF16),
            pltpu.VMEM((width, BLOCK), BF16),
            pltpu.VMEM((width, BLOCK), BF16),
            pltpu.VMEM((per, BLOCK), F32),
            pltpu.VMEM((per, BLOCK), F32),
            pltpu.VMEM((per, width), BF16),
            pltpu.VMEM((per, width), BF16),
            pltpu.VMEM((per, width), BF16),
            pltpu.VMEM((per, width), BF16),
        ],
        compiler_params=pltpu.CompilerParams(vmem_limit_bytes=VMEM),
        cost_estimate=pl.CostEstimate(flops=8 * count * width * STATE * 32, bytes_accessed=96 << 20, transcendentals=0),
        name="scan_backward",
    )(mixed, act, gate, d_branch, mask, states, states, w_dtt, table, own, offsets)


def finish_kernel(mixed_ref, d_act_ref, conv_out_ref, conv_in_ref, ahead_ref, act_ref, d_gate_ref, mask_ref, w_xt_ref,
                  table_ref, d_proj_ref, x_grad_ref, sums_ref, line_ref, masked_ref):
    first = pl.program_id(0) == 0
    rows, width = act_ref.shape

    @pl.when(first)
    def _():
        x_grad_ref[...] = jnp.zeros_like(x_grad_ref)
        sums_ref[...] = jnp.zeros_like(sums_ref)
        for k in range(CONV - 1):
            masked_ref[k, rows:] = jnp.zeros((8, width), F32)

    @pl.when(jnp.logical_not(first))
    def _():
        for k in range(CONV - 1):
            masked_ref[k, rows:] = masked_ref[k, :8]

    mixed = jnp.concatenate([mixed_ref[i] for i in range(rows // BLOCK)], axis=1)
    x_grad_ref[...] += dot_nn(mixed, act_ref[...])
    d_act = d_act_ref[...] + dot_tn(mixed, w_xt_ref[...])
    conv_out = conv_out_ref[...]
    sig = sigmoid(conv_out)
    d_conv = d_act * (sig * (1.0 + conv_out * (1.0 - sig)))
    sums_ref[CONV : CONV + 1] += jnp.sum(d_conv, axis=0, keepdims=True)
    line_ref[:8] = ahead_ref[...].astype(F32)[8:]
    line_ref[8:] = conv_in_ref[...].astype(F32)
    d_conv_in = jnp.zeros((rows, width), F32)
    for k in range(CONV):
        masked = d_conv * mask_ref[:, k : k + 1]
        sums_ref[k : k + 1] += jnp.sum(masked * line_ref[5 + k : 5 + k + rows], axis=0, keepdims=True)
        if k < CONV - 1:
            masked_ref[k, :rows] = masked
            masked = masked_ref[k, CONV - 1 - k : CONV - 1 - k + rows]
        d_conv_in = d_conv_in + table_ref[ROW_CONV + k : ROW_CONV + k + 1, :] * masked
    d_proj_ref[:, :width] = d_conv_in.astype(BF16)
    d_proj_ref[:, width:] = d_gate_ref[...]


def finish(mixed, d_act, conv_out, conv_in, act, d_gate, mask, w_xt, table):
    count, width = act.shape
    blocks = count // WIDE
    last = blocks - 1

    def rows(columns):
        return rows_spec(columns, lambda i: last - i, WIDE)

    per = WIDE // GROUP
    return pl.pallas_call(
        finish_kernel,
        grid=(blocks,),
        in_specs=[
            pl.BlockSpec((WIDE // BLOCK, MIXED, BLOCK), lambda i: (last - i, 0, 0)), rows(width), rows(width), rows(width),
            pl.BlockSpec((GROUP, width), lambda i: (jnp.maximum((last - i) * per - 1, 0), 0)),
            rows(width), rows(width), rows(8), whole_spec(w_xt.shape), whole_spec(table.shape),
        ],
        out_specs=[rows(2 * width), whole_spec((MIXED, width)), whole_spec((8, width))],
        out_shape=[
            jax.ShapeDtypeStruct((count, 2 * width), BF16),
            jax.ShapeDtypeStruct((MIXED, width), F32),
            jax.ShapeDtypeStruct((8, width), F32),
        ],
        scratch_shapes=[pltpu.VMEM((WIDE + 8, width), F32), pltpu.VMEM((CONV - 1, WIDE + 8, width), F32)],
        compiler_params=pltpu.CompilerParams(vmem_limit_bytes=VMEM),
        cost_estimate=pl.CostEstimate(flops=1 << 31, bytes_accessed=12 << 20, transcendentals=0),
        name="finish",
    )(mixed, d_act, conv_out, conv_in, conv_in, act, d_gate, mask, w_xt, table)


def lower_kernel(where_ref, d_proj_ref, w_ref, _, *out_refs):
    row, column = where_ref[0], where_ref[1]
    tokens = out_refs[0].shape[0]
    mine, theirs = out_refs[:4], out_refs[4:]
    for i, k in enumerate((1, 2, 3, 0)):
        at = lax.rem(row - k + 4, 4) * 2
        parts = [d_proj_ref[pl.ds(pl.multiple_of((at + column) * tokens, tokens), tokens), :]]
        if i:
            parts.append(d_proj_ref[pl.ds(pl.multiple_of((at + 1 - column) * tokens, tokens), tokens), :])
        out = dot_nt(jnp.concatenate(parts, axis=0), w_ref[...]).astype(BF16)
        mine[i][...] = out[:tokens]
        if i:
            theirs[i - 1][...] = out[tokens:]


def lower(where, d_proj, w_rows, first):
    tokens, model = first.shape
    vmem = pl.BlockSpec(memory_space=pltpu.VMEM)
    out = pl.pallas_call(
        lower_kernel,
        in_specs=[pl.BlockSpec(memory_space=pltpu.SMEM), vmem, vmem, ANY],
        out_specs=[vmem] * 7,
        out_shape=[jax.ShapeDtypeStruct((tokens, model), BF16)] * 7,
        compiler_params=pltpu.CompilerParams(vmem_limit_bytes=VMEM),
        cost_estimate=pl.CostEstimate(flops=2 * d_proj.size * model, bytes_accessed=12 << 20, transcendentals=0),
        name="lower",
    )(where.astype(jnp.int32), d_proj, w_rows, first)
    return out[:4], out[4:]


def line_ring(seqs):
    return [(i, (i + 2) % seqs) for i in range(seqs)]


def pair_swap(size, bit):
    return [(i, i ^ bit) for i in range(size)]


def gather_all(part, shard):
    seqs, shards = lax.axis_size("seq"), lax.axis_size("fsdp")
    if (seqs, shards) != (8, 4):
        whole, wide = lax.all_gather(part, "seq", axis=0), lax.all_gather(shard, "fsdp", axis=0)
        return (
            [whole[k] for k in range(seqs)], jnp.arange(seqs, dtype=jnp.int32),
            [wide[k] for k in range(shards)], jnp.arange(shards, dtype=jnp.int32),
        )
    place, here = lax.axis_index("seq"), lax.axis_index("fsdp")
    row, column = place // 2, place % 2
    swap, ring = pair_swap(seqs, 1), line_ring(seqs)
    pieces, slots = [], []
    far = lax.ppermute(shard, "fsdp", pair_swap(shards, 2))
    beside = lax.ppermute(shard, "fsdp", pair_swap(shards, 1))
    for k in range(4):
        slot = (row - k + 4) % 4 * 2
        swapped = lax.ppermute(part, "seq", swap)
        pieces += [part, swapped]
        slots += [slot + column, slot + 1 - column]
        if k == 3:
            break
        part = lax.ppermute(part, "seq", ring)
        if k == 0:
            part = after(part, swapped)
        elif k == 1:
            part = after(part, swapped, beside)
            far = after(far, part)
            both = lax.ppermute(far, "fsdp", pair_swap(shards, 1))
        else:
            part = after(part, swapped, both)
    w_slots = jnp.stack([here, here ^ 2, here ^ 1, here ^ 3]).astype(jnp.int32)
    return pieces, jnp.stack(slots).astype(jnp.int32), [shard, far, beside, both], w_slots


def sum_over_seq(part):
    seqs = lax.axis_size("seq")
    shares = part.reshape((seqs, part.shape[0] // seqs) + part.shape[1:])
    shares = lax.all_to_all(shares, "seq", split_axis=0, concat_axis=0, tiled=True)
    total = jnp.sum(shares.astype(F32), axis=0).astype(BF16)
    copies = jnp.broadcast_to(total, shares.shape)
    return lax.all_to_all(copies, "seq", split_axis=0, concat_axis=0, tiled=True).reshape(part.shape), total


def from_owner(shares, owner):
    seqs, shards = lax.axis_size("seq"), lax.axis_size("fsdp")
    here = lax.axis_index("fsdp")
    if (seqs, shards) != (8, 4):
        every = jnp.stack([shares(j) for j in range(shards)])
        every = lax.dynamic_index_in_dim(lax.all_gather(every, "fsdp"), owner, 0, False)
        return [lax.dynamic_index_in_dim(every, here, 0, False)]
    got = [jnp.where(here == owner, shares(here), 0)]
    for j in range(1, shards):
        pairs = [(s * shards + s * shards // seqs, s * shards + (s * shards // seqs ^ j)) for s in range(seqs)]
        got.append(lax.ppermute(shares(here ^ j), ("seq", "fsdp"), pairs))
    return got


def scatter_shards(blocks, kind=BF16):
    shards = lax.axis_size("fsdp")
    if shards != 4 or lax.axis_size("seq") != 8:
        return lax.psum_scatter(blocks, "fsdp", scatter_dimension=0)
    here = lax.axis_index("fsdp")
    total = lax.dynamic_index_in_dim(blocks, here, 0, False).astype(F32)
    for j in range(1, shards):
        theirs = lax.dynamic_index_in_dim(blocks, here ^ j, 0, False).astype(kind)
        total = total + lax.ppermute(theirs, "fsdp", pair_swap(shards, j)).astype(F32)
    return total


def local(
    x_in, cotangent, doc_lengths, norm_gain, in_weight, conv_weight, conv_bias,
    x_weight, dt_weight, dt_bias, a_log, skip_weight, out_weight,
):
    seqs, shards = lax.axis_size("seq"), lax.axis_size("fsdp")
    place = lax.axis_index("seq")
    width = INNER // seqs
    tokens, model = x_in.shape[1:]
    count = tokens * seqs
    deep = model // shards

    held = INNER // shards
    owner, offset = place * width // held, place * width % held
    lanes = min(2 * width, deep)
    small = jnp.concatenate(
        [
            dt_weight.T, a_log.T, conv_weight.T, conv_bias[None], dt_bias[None], skip_weight[None],
            jnp.zeros((MIXED - DT_RANK - STATE - CONV - 3, held), BF16),
        ],
        axis=0,
    )
    small = jnp.concatenate(
        [lax.dynamic_slice_in_dim(x_weight.T, offset, width, 1), lax.dynamic_slice_in_dim(small, offset, width, 1)], axis=1
    )
    gain_rows = norm_gain.reshape(-1, lanes)
    gain_rows = jnp.pad(gain_rows, ((0, GROUP - gain_rows.shape[0]), (0, 2 * width - lanes)))
    in_cols = jnp.concatenate(
        [
            lax.dynamic_slice_in_dim(in_weight, place * width, width, 1),
            lax.dynamic_slice_in_dim(in_weight, INNER + place * width, width, 1),
        ],
        axis=1,
    )
    shard = jnp.concatenate([in_cols, gain_rows, small], axis=0)
    pieces, slots, w_pieces, w_slots = gather_all(x_in[0], shard)
    small = sum(jnp.where(w_slots[k] == owner, piece[deep + GROUP :], 0) for k, piece in enumerate(w_pieces))
    w_xt, w_dtt, table = small[:, :width], small[:DT_RANK, width:], small[DT_RANK:, width:].astype(F32)
    cot_all = lax.all_gather(after(cotangent[0], pieces[-2]), "seq", axis=0, tiled=True)
    rows = model // (seqs * shards)
    start = place * shards * rows % deep
    in_got = from_owner(
        lambda j: after(lax.dynamic_slice_in_dim(in_weight, start + j * rows, rows, 0), pieces[2]), owner
    )
    out_rows = after(lax.dynamic_slice_in_dim(out_weight, offset, width, 0), pieces[-2])
    out_got = from_owner(lambda j: out_rows, owner)
    mask = doc_masks(doc_lengths[0], count)

    own, offsets = owns()
    w_rows, gain = assemble(w_pieces, w_slots, deep)
    lowered, conv_in, conv_out, act, gate, mixed = project(pieces, slots, w_rows, gain, w_xt, table, mask)
    mixed, share = sum_over_seq(mixed)
    in_rows = sum(in_got[1:], after(in_got[0], share))
    w_out = sum(out_got[1:], after(out_got[0], share))
    mixed = after(mixed, in_rows)
    branch, y_total, states, w_out = scan_forward(mixed, act, gate, mask, w_dtt, table, own, w_out)
    block_part = dot_nn(branch, w_out).astype(BF16)
    block_sum = lax.psum_scatter(block_part, "seq", scatter_dimension=0, tiled=True)
    block_out = (x_in[0].astype(F32) + block_sum.astype(F32)).astype(BF16)

    d_branch = dot_nt(cot_all, w_out)
    d_gate = (d_branch * y_total * silu_slope(gate)).astype(BF16)
    d_branch = after(d_branch, block_part, d_gate)
    d_mixed, d_act, sums, dt_grad = scan_backward(
        mixed, act, gate, d_branch, mask, states, w_dtt, table, own, offsets
    )
    out_grad = scatter_shards(dot_tn(branch, cot_all).reshape(shards, width // shards, model))

    def shared(part):
        return scatter_shards(part.reshape(seqs, shards, rows, width).transpose(1, 0, 2, 3)).astype(BF16)

    def spread(part):
        part = lax.all_to_all(part, "seq", split_axis=0, concat_axis=0, tiled=True)
        return part.transpose(1, 0, 2).reshape(rows, INNER).astype(F32)

    gate_sum = shared(dot_tn(lowered, d_gate))
    d_mixed, share = sum_over_seq(d_mixed)
    d_mixed = after(d_mixed, block_sum)
    gate_grad = spread(after(gate_sum, share))
    d_proj, x_proj_grad, conv_sums = finish(d_mixed, d_act, conv_out, conv_in, act, d_gate, mask, w_xt, table)

    small = jnp.concatenate([x_proj_grad, dt_grad, sums, conv_sums], axis=0)
    if seqs == 8:
        row, column = place // 2, place % 2
        swap, ring = pair_swap(seqs, 1), line_ring(seqs)
        first = (row + 3) % 4 * 2 + 1 - column
        first = dot_nt(lax.dynamic_slice_in_dim(d_proj, first * tokens, tokens, 0), w_rows).astype(BF16)
        swapped = [lax.ppermute(first, "seq", swap)]
        mine, theirs = lower(jnp.stack([row, column]), d_proj, w_rows, first)
        conv_sum = shared(dot_tn(lowered, after(d_proj, *theirs)[:, :width]))
        swapped += [lax.ppermute(block, "seq", swap) for block in theirs]
        total = mine[0].astype(F32) + swapped[0].astype(F32)
        befores = (theirs, (gate_grad,), (conv_sum,))
        for k in range(3):
            total = after(total.astype(BF16), *befores[k])
            if k == 2:
                small = after(small, total)
            total = lax.ppermute(total, "seq", ring).astype(F32) + mine[k + 1].astype(F32) + swapped[k + 1].astype(F32)
        d_low_own = total
    else:
        conv_sum = shared(dot_tn(lowered, d_proj[:, :width]))
        d_lowered = dot_nt(d_proj, w_rows).astype(BF16)
        d_low_own = lax.psum_scatter(d_lowered, "seq", scatter_dimension=0, tiled=True).astype(F32)
    conv_grad = spread(conv_sum)

    x_own = x_in[0].astype(F32)
    inv_own = lax.rsqrt(jnp.mean(x_own * x_own, axis=1, keepdims=True) + NORM_EPS)
    normed_own = x_own * inv_own
    d_norm = d_low_own * gain
    x_grad = cotangent[0].astype(F32) + inv_own * (
        d_norm - normed_own * jnp.mean(d_norm * normed_own, axis=1, keepdims=True)
    )
    in_grad = jnp.concatenate([conv_grad, gate_grad], axis=1)
    gain_own = lax.dynamic_slice_in_dim(gain[0], (place * shards + lax.axis_index("fsdp")) * rows, rows, 0)
    gain_grad = jnp.sum(in_grad * in_rows.astype(F32), axis=1) / gain_own
    small = small.reshape(-1, shards, width // shards).transpose(1, 0, 2)
    small = scatter_shards(small, F32)
    at = MIXED + DT_RANK
    tail = at + 24
    return (
        block_out[None],
        x_grad[None],
        gain_grad,
        in_grad,
        small[tail : tail + CONV].T,
        small[tail + CONV],
        small[:MIXED].T,
        small[MIXED:at].T,
        small[at + STATE + 1],
        small[at : at + STATE].T,
        small[at + STATE],
        out_grad,
    )


def solution(mesh):
    by_row, by_vec = P("fsdp", None), P("fsdp")
    tok = P("fsdp", "seq", None)
    out_row, out_vec = P(("seq", "fsdp"), None), P(("seq", "fsdp"))
    in_specs = (
        tok, tok, by_row, by_vec, by_row, by_row, by_vec, by_row, by_row, by_vec, by_row, by_vec, by_row,
    )
    out_specs = (
        tok, tok, out_vec, out_row, out_row, out_vec, out_row, out_row, out_vec, out_row, out_vec, out_row,
    )
    return jax.shard_map(local, mesh=mesh, in_specs=in_specs, out_specs=out_specs, check_vma=False)
```

time: 3160 us -> 445 us (0.14)
  waiting for transfers between devices: 1760 us -> 137 us
  other arithmetic: 913 us -> 44.6 us
  local copies, waits for them, and re-layouts: 252 us -> 43.5 us
  Pallas kernels: 0 us -> 95.2 us
  matrix products: 114 us -> 31 us
  blocking collectives: 71.1 us -> 0 us
  starting transfers between devices: 5.35 us -> 72.1 us
    reduce_scatter x5 -> x1, waiting for transfers between devices: 1460 us -> 1.93 us  [local(): lax.psum_scatter(block_part, 'seq', scatter_dimension=0, tiled=True)]
    reduce_sum x155 -> x7, other arithmetic: 572 us -> 2.65 us  [the longest x1 1.79 us: local(): jnp.mean(d_norm * normed_own, axis=1, keepdims=True)]
    all_gather x8 -> x1, waiting for transfers between devices: 276 us -> 0.02 us  [local(): lax.all_gather(after(cotangent[0], pieces[-2]), 'seq', axis=0, tiled=True)]
    mul x434 -> x0, other arithmetic: 104 us -> none  [the longest x16 94.4 us: group_step(): running = decay_now * running + drive_now]
    add_any x8 -> x0, other arithmetic: 98 us -> none  [advance(): return checked(decay_rate, carry_state, one_piece)]
    ppermute x2 -> x35, waiting for transfers between devices: 4.51 us -> 101 us  [the longest x12 35.9 us: scatter_shards(): lax.ppermute(theirs, 'fsdp', pair_swap(shards, j)).astype(F32)]
    pallas_call x0 -> x27, Pallas kernels: none -> 95.2 us  [the longest x1 42 us: scan_backward(): pl.pallas_call(backward_kernel, grid=(blocks,), in_specs=[mixed_spec, row...]
    add x17 -> x5, other arithmetic: 97.1 us -> 13 us  [the longest x1 5.16 us: local(): w_out = sum(out_got[1:], after(out_got[0], share))]
  transfers between devices with their start and end apart: 16 -> 43, of which waited for: 11 -> 19; matrix products, arithmetic and copies ran while one was open for 20% -> 22% of each run, Pallas kernels for 0% -> 22%
where the time goes in v1:
time: 445 us; the launch traced here: 438 us
  waiting for transfers between devices  137 us (31%)
  Pallas kernels  95.2 us (21%)
  starting transfers between devices  72.1 us (16%)
  other arithmetic  44.6 us (10%)
  local copies, waits for them, and re-layouts  43.5 us (10%)
  matrix products  31 us (7%)
  between operations  15.2 us (3%)
    pallas_call x1, Pallas kernels, scan_backward(): pl.pallas_call(backward_kernel, grid=(blocks,), in_specs=[mixed_spec, row...  42 us
    ppermute x12, waiting for transfers between devices, scatter_shards(): lax.ppermute(theirs, 'fsdp', pair_swap(shards, j)).astype(F32)  35.9 us
    all_to_all x2, waiting for transfers between devices, sum_over_seq(): lax.all_to_all(copies, 'seq', split_axis=0, concat_axis=0, tiled=True)  27.5 us
    ppermute x4, waiting for transfers between devices, gather_all(): swapped = lax.ppermute(part, 'seq', swap)  22.7 us
    ppermute x3, waiting for transfers between devices, gather_all(): part = lax.ppermute(part, 'seq', ring)  19.4 us
    pallas_call x1, Pallas kernels, scan_forward(): pl.pallas_call(forward_kernel, grid=(count // BLOCK,), in_specs=[pl.Block...  18.4 us
    ppermute x6, starting transfers between devices, from_owner(): got.append(lax.ppermute(shares(here ^ j), ('seq', 'fsdp'), pairs))  16.9 us
    dot_general x3, matrix products, dot_tn(): lax.dot_general(a, b, (((0,), (0,)), ((), ())), preferred_element_type=F32)  16.1 us
  transfers between devices with their start and end apart: 43, of which 19 were waited for; matrix products, arithmetic and copies ran while one was open for 22% of the time, Pallas kernels for 22%

profile of v1, /device:TPU:0, one launch (start us, length us, event | category | flops | bytes accessed | tf_op | source)
XLA Modules:
  0.0 438.2 jit_solution(15211184709598749244)
XLA Ops:
  22.5 10.3 %collective-permute-done.2.refs_1_ = bf16[128,2048]{1,0:T(8,128)(2,1)} collective-permute-done((bf16[128,2048]{1,0:T(8,128)(2,1)S(1)}, bf16[128,2048]{1,0:T(8,128)(2,1)}, u32[]{:S(2)}, u32[]{:S(2)}) %collective-permute-start.2) | collective-permute-done | bytes 524320 | tf_op jit(solution)/shard_map/ppermute | solution.py:576
  37.3 12.4 %collective-permute-done.4.refs_1_.refs_3_ = bf16[128,2048]{1,0:T(8,128)(2,1)S(1)} collective-permute-done((bf16[128,2048]{1,0:T(8,128)(2,1)}, bf16[128,2048]{1,0:T(8,128)(2,1)S(1)}, u32[]{:S(2)}, u32[]{:S(2)}) %collective-permute-start.4) | collective-permute-done | bytes 524320 | tf_op jit(solution)/shard_map/ppermute | solution.py:576
  53.7 5.1 %constant_dynamic-slice_fusion.8 = (bf16[64,8192]{1,0:T(8,128)(2,1)}, bf16[64,8192]{1,0:T(8,128)(2,1)}, bf16[64,8192]{1,0:T(8,128)(2,1)}, bf16[64,8192]{1,0:T(8,128)(2,1)}) fusion(bf16[512,8192]{1,0:T(8,128)(2,1)} %param.17, s32[]{:T(128)S(6)} %select_n.178, s32[]{:T(128)S(6)} %select_n.176, s32[]{:T(128)S(6)} %select_n.180, s32[]{:T(128)S(6)} %select_n.179), kind=kLoop, calls=%fused_computation.106 | loop fusion | bytes 8388624 | tf_op jit(solution)/shard_map/dynamic_slice | solution.py:670
  60.5 14.4 %collective-permute-done.8.refs_0_ = bf16[128,2048]{1,0:T(8,128)(2,1)S(1)} collective-permute-done((bf16[128,2048]{1,0:T(8,128)(2,1)S(1)}, bf16[128,2048]{1,0:T(8,128)(2,1)S(1)}, u32[]{:S(2)}, u32[]{:S(2)}) %collective-permute-start.8) | collective-permute-done | bytes 524320 | tf_op jit(solution)/shard_map/ppermute | solution.py:581
  96.8 5.1 %assemble.1 = (bf16[2048,1024]{1,0:T(8,128)(2,1)}, f32[1,2048]{1,0:T(1,128)}) custom-call(s32[4]{0:T(128)} %pad_add_fusion.slots_ref, bf16[688,1024]{1,0:T(8,128)(2,1)} %fusion.3.refs_0_, bf16[688,1024]{1,0:T(8,128)(2,1)} %after.23.refs_1_, bf16[688,1024]{1,0:T(8,128)(2,1)} %copy-done.9, bf16[688,1024]{1,0:T(8,128)(2,1)} %copy-done.10), custom_call_target="tpu_custom_call" | custom-call | tf_op jit(solution)/shard_map/assemble/pallas_call | solution.py:112
  103.3 12.8 %project.1 = (bf16[1024,2048]{1,0:T(8,128)(2,1)}, bf16[1024,512]{1,0:T(8,128)(2,1)}, f32[1024,512]{1,0:T(8,128)}, bf16[1024,512]{1,0:T(8,128)(2,1)}, f32[1024,512]{1,0:T(8,128)}, /*index=5*/bf16[8,160,128]{2,1,0:T(8,128)(2,1)}) custom-call(s32[8]{0:T(128)} %stack.70.slots_ref, bf16[2048,1024]{1,0:T(8,128)(2,1)} %get-tuple-element.38.w_in_ref.w_ref, ...), custom_call_target="tpu_custom_call" | custom-call | flops 4294967296 | bytes 20971520 | tf_op jit(solution)/shard_map/project/pallas_call | solution.py:186
  116.1 3.7 all-to-all-start
  133.3 6.6 %all-to-all-done = bf16[8,1,160,128]{3,2,1,0:T(8,128)(2,1)S(1)} async-done(((bf16[8,1,160,128]{3,2,1,0:T(8,128)(2,1)}), bf16[8,1,160,128]{3,2,1,0:T(8,128)(2,1)S(1)}, u32[]{:S(2)}, u32[]{:S(2)}) %all-to-all-start) | async-done | bytes 327712 | tf_op jit(solution)/shard_map/all_to_all | solution.py:597
  147.9 14.1 %all-to-all-done.1 = bf16[8,1,160,128]{3,2,1,0:T(8,128)(2,1)S(1)} async-done(((bf16[8,1,160,128]{3,2,1,0:T(8,128)(2,1)}), bf16[8,1,160,128]{3,2,1,0:T(8,128)(2,1)S(1)}, u32[]{:S(2)}, u32[]{:S(2)}) %all-to-all-start.1) | async-done | bytes 327712 | tf_op jit(solution)/shard_map/all_to_all | solution.py:600
  162.7 6.6 %collective-permute-done.14 = bf16[512,2048]{1,0:T(8,128)(2,1)} collective-permute-done((bf16[512,2048]{1,0:T(8,128)(2,1)}, bf16[512,2048]{1,0:T(8,128)(2,1)}, u32[]{:S(2)}, u32[]{:S(2)}) %collective-permute-start.14) | collective-permute-done | bytes 2097184 | tf_op jit(solution)/shard_map/ppermute | solution.py:613
  169.4 5.2 %add_add_fusion._ = bf16[512,2048]{1,0:T(8,128)(2,1)} fusion(bf16[512,2048]{1,0:T(8,128)(2,1)} %collective-permute-done.15, bf16[512,2048]{1,0:T(8,128)(2,1)} %collective-permute-done.14, bf16[512,2048]{1,0:T(8,128)(2,1)} %after.32, bf16[512,2048]{1,0:T(8,128)(2,1)} %collective-permute-done.13), kind=kLoop, calls=%fused_computation.8 | loop fusion | flops 3145728 | bytes 10485760 | tf_op jit(solution)/shard_map/add | solution.py:681
  174.6 18.4 %scan_forward.1 = (bf16[1024,512]{1,0:T(8,128)(2,1)}, f32[1024,512]{1,0:T(8,128)}, bf16[16384,512]{1,0:T(8,128)(2,1)}, bf16[512,2048]{1,0:T(8,128)(2,1)}) custom-call(bf16[8,160,128]{2,1,0:T(8,128)(2,1)} %after.30.mixed_ref, bf16[1024,512]{1,0:T(8,128)(2,1)} %get-tuple-element.41.act_ref, ...), custom_call_target="tpu_custom_call", output_to_operand_aliasing={{3}: (7, {})} | custom-call | flops 1073741824 | bytes 67108864 | tf_op jit(solution)/shard_map/scan_forward/pallas_call | solution.py:283
  193.0 6.2 %convolution_convert_fusion.refs_1_ = bf16[1024,2048]{1,0:T(8,128)(2,1)} fusion(bf16[1024,512]{1,0:T(8,128)(2,1)} %get-tuple-element.43, bf16[512,2048]{1,0:T(8,128)(2,1)} %get-tuple-element.44), kind=kOutput, calls=%fused_computation.2 | convolution fusion | flops 2149580800 | bytes 7340032 | tf_op jit(solution)/shard_map/dot_general | solution.py:24
  201.6 5.4 %fusion.45.refs_0_ = f32[1024,512]{1,0:T(8,128)S(1)} fusion(bf16[1024,2048]{1,0:T(8,128)(2,1)} %all-gather.2.cloned.1.call-done, bf16[512,2048]{1,0:T(8,128)(2,1)} %get-tuple-element.44), kind=kOutput, calls=%fused_computation.130 | convolution fusion | flops 2147483648 | bytes 8388608 | tf_op jit(solution)/shard_map/dot_general | solution.py:32
  210.4 42.0 %scan_backward.1 = (bf16[8,160,128]{2,1,0:T(8,128)(2,1)}, f32[1024,512]{1,0:T(8,128)}, f32[24,512]{1,0:T(8,128)}, f32[128,512]{1,0:T(8,128)}) custom-call(bf16[8,160,128]{2,1,0:T(8,128)(2,1)} %after.30.mixed_ref, bf16[1024,512]{1,0:T(8,128)(2,1)} %get-tuple-element.41.act_ref, f32[1024,512]{1,0:T(8,128)} %get-tuple-element.42.gate_ref, ...), custom_call_target="tpu_custom_call" | custom-call | flops 2147483648 | bytes 100663296 | tf_op jit(solution)/shard_map/scan_backward/pallas_call | solution.py:415
  252.4 5.2 %all-to-all-start.2 = ((bf16[8,1,160,128]{3,2,1,0:T(8,128)(2,1)}), bf16[8,1,160,128]{3,2,1,0:T(8,128)(2,1)S(1)}, u32[]{:S(2)}, u32[]{:S(2)}) async-start(bf16[8,1,160,128]{3,2,1,0:T(8,128)(2,1)} %bitcast.171), calls=%async_computation.3 | async-start | bytes 655360 | tf_op jit(solution)/shard_map/all_to_all | solution.py:597
  257.5 4.6 %fusion.46 = f32[2048,512]{1,0:T(8,128)S(1)} fusion(bf16[1024,2048]{1,0:T(8,128)(2,1)} %get-tuple-element.57, bf16[1024,512]{1,0:T(8,128)(2,1)S(1)} %copy-done.5), kind=kOutput, calls=%fused_computation.131 | convolution fusion | flops 2147483648 | bytes 9437184 | tf_op jit(solution)/shard_map/dot_general | solution.py:28
  268.8 5.9 %all-to-all-start.3 = ((bf16[8,1,160,128]{3,2,1,0:T(8,128)(2,1)}), bf16[8,1,160,128]{3,2,1,0:T(8,128)(2,1)S(1)}, u32[]{:S(2)}, u32[]{:S(2)}) async-start(bf16[8,1,160,128]{3,2,1,0:T(8,128)(2,1)} %broadcast_in_dim.81), calls=%async_computation.4 | async-start | bytes 655360 | tf_op jit(solution)/shard_map/all_to_all | solution.py:600
  274.7 6.6 %fusion.47 = f32[512,2048]{1,0:T(8,128)} fusion(bf16[1024,512]{1,0:T(8,128)(2,1)S(1)} %copy-done.21, bf16[1024,2048]{1,0:T(8,128)(2,1)} %all-gather.2.cloned.1.call-done), kind=kOutput, calls=%fused_computation.132 | convolution fusion | flops 2147483648 | bytes 9437184 | tf_op jit(solution)/shard_map/dot_general | solution.py:28
  281.3 13.4 %all-to-all-done.3 = bf16[8,1,160,128]{3,2,1,0:T(8,128)(2,1)S(1)} async-done(((bf16[8,1,160,128]{3,2,1,0:T(8,128)(2,1)}), bf16[8,1,160,128]{3,2,1,0:T(8,128)(2,1)S(1)}, u32[]{:S(2)}, u32[]{:S(2)}) %all-to-all-start.3) | async-done | bytes 327712 | tf_op jit(solution)/shard_map/all_to_all | solution.py:600
  296.6 8.2 %finish.1 = (bf16[1024,1024]{1,0:T(8,128)(2,1)}, f32[160,512]{1,0:T(8,128)}, f32[8,512]{1,0:T(8,128)}) custom-call(bf16[8,160,128]{2,1,0:T(8,128)(2,1)} %after.35.mixed_ref, f32[1024,512]{1,0:T(8,128)} %get-tuple-element.48.d_act_ref, f32[1024,512]{1,0:T(8,128)} %get-tuple-element.49.conv_out_ref, bf16[1024,512]{1,0:T(8,128)(2,1)} %get-tuple-element.50.conv_in_ref.ahead_ref, ...), custom_call_target="tpu_custom_call" | custom-call | flops 2147483648 | bytes 12582912 | tf_op jit(solution)/shard_map/finish/pallas_call | solution.py:501
  309.6 8.8 %lower.1 = (bf16[128,2048]{1,0:T(8,128)(2,1)}, bf16[128,2048]{1,0:T(8,128)(2,1)}, bf16[128,2048]{1,0:T(8,128)(2,1)}, bf16[128,2048]{1,0:T(8,128)(2,1)}, bf16[128...) custom-call(s32[2]{0:T(128)} %pad_add_fusion.1.where_ref, ...), custom_call_target="tpu_custom_call" | custom-call | flops 4294967296 | bytes 12582912 | tf_op jit(solution)/shard_map/lower/pallas_call | solution.py:540
  318.4 4.9 %fusion.13 = f32[2048,512]{1,0:T(8,128)S(1)} fusion(bf16[1024,2048]{1,0:T(8,128)(2,1)} %get-tuple-element.57, bf16[1024,1024]{1,0:T(8,128)(2,1)} %after.39), kind=kOutput, calls=%fused_computation.24 | convolution fusion | flops 2147483648 | bytes 9437184 | tf_op jit(solution)/shard_map/dot_general | solution.py:28
  328.0 3.9 all-to-all-start.4
  339.8 7.2 %collective-permute-done.25 = bf16[8,64,512]{2,1,0:T(8,128)(2,1)} collective-permute-done((bf16[8,64,512]{2,1,0:T(8,128)(2,1)}, bf16[8,64,512]{2,1,0:T(8,128)(2,1)}, u32[]{:S(2)}, u32[]{:S(2)}) %collective-permute-start.25) | collective-permute-done | bytes 524320 | tf_op jit(solution)/shard_map/ppermute | solution.py:625
  349.0 8.2 %collective-permute-done.26 = bf16[8,64,512]{2,1,0:T(8,128)(2,1)} collective-permute-done((bf16[8,64,512]{2,1,0:T(8,128)(2,1)}, bf16[8,64,512]{2,1,0:T(8,128)(2,1)}, u32[]{:S(2)}, u32[]{:S(2)}) %collective-permute-start.26) | collective-permute-done | bytes 524320 | tf_op jit(solution)/shard_map/ppermute | solution.py:625
  362.1 4.6 %all-to-all-start.5 = ((bf16[8,64,512]{2,1,0:T(8,128)(2,1)}), bf16[8,64,512]{2,1,0:T(8,128)(2,1)S(1)}, u32[]{:S(2)}, u32[]{:S(2)}) async-start(bf16[8,64,512]{2,1,0:T(8,128)(2,1)} %fusion.19.refs_1_), calls=%async_computation.6 | async-start | bytes 1048576 | tf_op jit(solution)/shard_map/all_to_all | solution.py:700
  368.5 11.4 %collective-permute-done.33 = bf16[128,2048]{1,0:T(8,128)(2,1)} collective-permute-done((bf16[128,2048]{1,0:T(8,128)(2,1)S(1)}, bf16[128,2048]{1,0:T(8,128)(2,1)}, u32[]{:S(2)}, u32[]{:S(2)}) %collective-permute-start.33) | collective-permute-done | bytes 524320 | tf_op jit(solution)/shard_map/ppermute | solution.py:625
  392.9 6.1 %collective-permute-done.23 = bf16[128,2048]{1,0:T(8,128)(2,1)S(1)} collective-permute-done((bf16[128,2048]{1,0:T(8,128)(2,1)}, bf16[128,2048]{1,0:T(8,128)(2,1)S(1)}, u32[]{:S(2)}, u32[]{:S(2)}) %collective-permute-start.23) | collective-permute-done | bytes 524320 | tf_op jit(solution)/shard_map/ppermute | solution.py:718
  399.1 4.7 %collective-permute-done.22 = bf16[128,2048]{1,0:T(8,128)(2,1)} collective-permute-done((bf16[128,2048]{1,0:T(8,128)(2,1)}, bf16[128,2048]{1,0:T(8,128)(2,1)}, u32[]{:S(2)}, u32[]{:S(2)}) %collective-permute-start.22) | collective-permute-done | bytes 524320 | tf_op jit(solution)/shard_map/ppermute | solution.py:725
  410.7 3.7 collective-permute-done.31
  421.1 5.0 %collective-permute-done.27 = bf16[128,2048]{1,0:T(8,128)(2,1)} collective-permute-done((bf16[128,2048]{1,0:T(8,128)(2,1)S(1)}, bf16[128,2048]{1,0:T(8,128)(2,1)}, u32[]{:S(2)}, u32[]{:S(2)}) %collective-permute-start.27) | collective-permute-done | bytes 524320 | tf_op jit(solution)/shard_map/ppermute | solution.py:725
  (267 shorter events, 142.4 us)
Async XLA Ops:
  7.2 194.4 %all-gather.2.cloned.1.call-start = ((), (), s32[]{:S(2)}) async-start(), calls=%async_computation.8 | async-start | bytes 4718592 | tf_op jit(solution)/shard_map/all_gather | solution.py:666
  15.6 36.1 %collective-permute-start.5 = (bf16[688,1024]{1,0:T(8,128)(2,1)}, bf16[688,1024]{1,0:T(8,128)(2,1)S(1)}, u32[]{:S(2)}, u32[]{:S(2)}) collective-permute-start(bf16[688,1024]{1,0:T(8,128)(2,1)} %fusion.3.refs_0_), channel_id=1, source_target_pairs={{0,1},{1,0},{2,3},{3,2},{4,5},{5,4},{6,7},{7,6},{8,9},{9,8},{10,11... | collective-permute-start | bytes 4227080 | tf_op jit(solution)/shard_map/ppermute | solution.py:573
  16.1 37.6 %collective-permute-start = (bf16[688,1024]{1,0:T(8,128)(2,1)}, bf16[688,1024]{1,0:T(8,128)(2,1)}, u32[]{:S(2)}, u32[]{:S(2)}) collective-permute-start(bf16[688,1024]{1,0:T(8,128)(2,1)} %fusion.3.refs_0_), channel_id=1, source_target_pairs={{0,2},{1,3},{2,0},{3,1},{4,6},{5,7},{6,4},{7,5},{8,10},{9,11},{10,... | collective-permute-start | bytes 4227080 | tf_op jit(solution)/shard_map/ppermute | solution.py:572
  20.1 15.6 %collective-permute-start.1 = (bf16[128,2048]{1,0:T(8,128)(2,1)S(1)}, bf16[128,2048]{1,0:T(8,128)(2,1)S(1)}, u32[]{:S(2)}, u32[]{:S(2)}) collective-permute-start(bf16[128,2048]{1,0:T(8,128)(2,1)S(1)} %bitcast.157), channel_id=1, source_target_pairs={{0,8},{4,12},{8,16},{12,20},{16,24},{20,28},{24,0},{28,4},{1,9},{5... | collective-permute-start | bytes 1572872 | tf_op jit(solution)/shard_map/ppermute | solution.py:581
  53.7 21.2 %collective-permute-start.6 = (bf16[688,1024]{1,0:T(8,128)(2,1)}, bf16[688,1024]{1,0:T(8,128)(2,1)S(1)}, u32[]{:S(2)}, u32[]{:S(2)}) collective-permute-start(bf16[688,1024]{1,0:T(8,128)(2,1)} %after.23.refs_1_), channel_id=1, source_target_pairs={{0,1},{1,0},{2,3},{3,2},{4,5},{5,4},{6,7},{7,6},{8,9},{9,8},{10,11... | collective-permute-start | bytes 4227080 | tf_op jit(solution)/shard_map/ppermute | solution.py:587
  58.8 16.1 %collective-permute-start.8 = (bf16[128,2048]{1,0:T(8,128)(2,1)S(1)}, bf16[128,2048]{1,0:T(8,128)(2,1)S(1)}, u32[]{:S(2)}, u32[]{:S(2)}) collective-permute-start(bf16[128,2048]{1,0:T(8,128)(2,1)S(1)} %copy-done.24), channel_id=1, source_target_pairs={{0,8},{4,12},{8,16},{12,20},{16,24},{20,28},{24,0},{28,4},{1,9},{5... | collective-permute-start | bytes 1572872 | tf_op jit(solution)/shard_map/ppermute | solution.py:581
  58.8 16.1 %collective-permute-start.7 = (bf16[128,2048]{1,0:T(8,128)(2,1)S(1)}, bf16[128,2048]{1,0:T(8,128)(2,1)S(1)}, u32[]{:S(2)}, u32[]{:S(2)}) collective-permute-start(bf16[128,2048]{1,0:T(8,128)(2,1)S(1)} %copy-done.24), channel_id=1, source_target_pairs={{0,4},{4,0},{8,12},{12,8},{16,20},{20,16},{24,28},{28,24},{1,5},{5... | collective-permute-start | bytes 1572872 | tf_op jit(solution)/shard_map/ppermute | solution.py:576
  82.8 19.7 %collective-permute-start.9 = (bf16[128,2048]{1,0:T(8,128)(2,1)S(1)}, bf16[128,2048]{1,0:T(8,128)(2,1)S(1)}, u32[]{:S(2)}, u32[]{:S(2)}) collective-permute-start(bf16[128,2048]{1,0:T(8,128)(2,1)S(1)} %copy-done.13), channel_id=1, source_target_pairs={{0,4},{4,0},{8,12},{12,8},{16,20},{20,16},{24,28},{28,24},{1,5},{5... | collective-permute-start | bytes 1572872 | tf_op jit(solution)/shard_map/ppermute | solution.py:576
  86.6 40.4 %collective-permute-start.11 = (bf16[64,8192]{1,0:T(8,128)(2,1)}, bf16[64,8192]{1,0:T(8,128)(2,1)}, u32[]{:S(2)}, u32[]{:S(2)}) collective-permute-start(bf16[64,8192]{1,0:T(8,128)(2,1)} %after.28), channel_id=1, source_target_pairs={{0,2},{4,6},{9,11},{13,15},{18,16},{22,20},{27,25},{31,29}} | collective-permute-start | bytes 3145736 | tf_op jit(solution)/shard_map/ppermute | solution.py:613
  90.1 54.3 %collective-permute-start.12 = (bf16[64,8192]{1,0:T(8,128)(2,1)S(1)}, bf16[64,8192]{1,0:T(8,128)(2,1)}, u32[]{:S(2)}, u32[]{:S(2)}) collective-permute-start(bf16[64,8192]{1,0:T(8,128)(2,1)S(1)} %copy-done.19), channel_id=1, source_target_pairs={{0,3},{4,7},{9,10},{13,14},{18,17},{22,21},{27,24},{31,28}} | collective-permute-start | bytes 3145736 | tf_op jit(solution)/shard_map/ppermute | solution.py:613
  92.4 52.0 %collective-permute-start.10 = (bf16[64,8192]{1,0:T(8,128)(2,1)}, bf16[64,8192]{1,0:T(8,128)(2,1)}, u32[]{:S(2)}, u32[]{:S(2)}) collective-permute-start(bf16[64,8192]{1,0:T(8,128)(2,1)} %after.27), channel_id=1, source_target_pairs={{0,1},{4,5},{9,8},{13,12},{18,19},{22,23},{27,26},{31,30}} | collective-permute-start | bytes 3145736 | tf_op jit(solution)/shard_map/ppermute | solution.py:613
  116.1 23.9 %all-to-all-start = ((bf16[8,1,160,128]{3,2,1,0:T(8,128)(2,1)}), bf16[8,1,160,128]{3,2,1,0:T(8,128)(2,1)S(1)}, u32[]{:S(2)}, u32[]{:S(2)}) async-start(bf16[8,1,160,128]{3,2,1,0:T(8,128)(2,1)} %bitcast.170), calls=%async_computation | async-start | bytes 655360 | tf_op jit(solution)/shard_map/all_to_all | solution.py:597
  120.8 41.9 %collective-permute-start.15 = (bf16[512,2048]{1,0:T(8,128)(2,1)}, bf16[512,2048]{1,0:T(8,128)(2,1)}, u32[]{:S(2)}, u32[]{:S(2)}) collective-permute-start(bf16[512,2048]{1,0:T(8,128)(2,1)} %after.31), channel_id=1, source_target_pairs={{0,3},{4,7},{9,10},{13,14},{18,17},{22,21},{27,24},{31,28}} | collective-permute-start | bytes 6291464 | tf_op jit(solution)/shard_map/ppermute | solution.py:613
  124.4 45.0 %collective-permute-start.14 = (bf16[512,2048]{1,0:T(8,128)(2,1)}, bf16[512,2048]{1,0:T(8,128)(2,1)}, u32[]{:S(2)}, u32[]{:S(2)}) collective-permute-start(bf16[512,2048]{1,0:T(8,128)(2,1)} %after.31), channel_id=1, source_target_pairs={{0,2},{4,6},{9,11},{13,15},{18,16},{22,20},{27,25},{31,29}} | collective-permute-start | bytes 6291464 | tf_op jit(solution)/shard_map/ppermute | solution.py:613
  127.0 42.4 %collective-permute-start.13 = (bf16[512,2048]{1,0:T(8,128)(2,1)}, bf16[512,2048]{1,0:T(8,128)(2,1)}, u32[]{:S(2)}, u32[]{:S(2)}) collective-permute-start(bf16[512,2048]{1,0:T(8,128)(2,1)} %after.31), channel_id=1, source_target_pairs={{0,1},{4,5},{9,8},{13,12},{18,19},{22,23},{27,26},{31,30}} | collective-permute-start | bytes 6291464 | tf_op jit(solution)/shard_map/ppermute | solution.py:613
  140.8 21.2 %all-to-all-start.1 = ((bf16[8,1,160,128]{3,2,1,0:T(8,128)(2,1)}), bf16[8,1,160,128]{3,2,1,0:T(8,128)(2,1)S(1)}, u32[]{:S(2)}, u32[]{:S(2)}) async-start(bf16[8,1,160,128]{3,2,1,0:T(8,128)(2,1)} %broadcast_in_dim.77), calls=%async_computation.1 | async-start | bytes 655360 | tf_op jit(solution)/shard_map/all_to_all | solution.py:600
  144.2 152.4 %reduce-scatter.2.cloned.1.call-start = ((), (), s32[]{:S(2)}) async-start(), calls=%async_computation.7 | async-start | bytes 4718592 | tf_op jit(solution)/shard_map/reduce_scatter | solution.py:685
  252.4 15.6 %all-to-all-start.2 = ((bf16[8,1,160,128]{3,2,1,0:T(8,128)(2,1)}), bf16[8,1,160,128]{3,2,1,0:T(8,128)(2,1)S(1)}, u32[]{:S(2)}, u32[]{:S(2)}) async-start(bf16[8,1,160,128]{3,2,1,0:T(8,128)(2,1)} %bitcast.171), calls=%async_computation.3 | async-start | bytes 655360 | tf_op jit(solution)/shard_map/all_to_all | solution.py:597
  264.4 60.3 %collective-permute-start.19 = (bf16[8,64,512]{2,1,0:T(8,128)(2,1)S(1)}, bf16[8,64,512]{2,1,0:T(8,128)(2,1)}, u32[]{:S(2)}, u32[]{:S(2)}) collective-permute-start(bf16[8,64,512]{2,1,0:T(8,128)(2,1)S(1)} %get-tuple-element.128), channel_id=1, source_target_pairs={{0,1},{1,0},{2,3},{3,2},{4,5},{5,4},{6,7},{7,6},{8,9},{9,8},{10,11... | collective-permute-start | bytes 1572872 | tf_op jit(solution)/shard_map/ppermute | solution.py:625
  266.5 58.2 %collective-permute-start.20 = (bf16[8,64,512]{2,1,0:T(8,128)(2,1)S(1)}, bf16[8,64,512]{2,1,0:T(8,128)(2,1)}, u32[]{:S(2)}, u32[]{:S(2)}) collective-permute-start(bf16[8,64,512]{2,1,0:T(8,128)(2,1)S(1)} %get-tuple-element.129), channel_id=1, source_target_pairs={{0,2},{1,3},{2,0},{3,1},{4,6},{5,7},{6,4},{7,5},{8,10},{9,11},{10,... | collective-permute-start | bytes 1572872 | tf_op jit(solution)/shard_map/ppermute | solution.py:625
  266.5 58.2 %collective-permute-start.21 = (bf16[8,64,512]{2,1,0:T(8,128)(2,1)S(1)}, bf16[8,64,512]{2,1,0:T(8,128)(2,1)}, u32[]{:S(2)}, u32[]{:S(2)}) collective-permute-start(bf16[8,64,512]{2,1,0:T(8,128)(2,1)S(1)} %get-tuple-element.130), channel_id=1, source_target_pairs={{0,3},{1,2},{2,1},{3,0},{4,7},{5,6},{6,5},{7,4},{8,11},{9,10},{10,... | collective-permute-start | bytes 1572872 | tf_op jit(solution)/shard_map/ppermute | solution.py:625
  268.8 25.9 %all-to-all-start.3 = ((bf16[8,1,160,128]{3,2,1,0:T(8,128)(2,1)}), bf16[8,1,160,128]{3,2,1,0:T(8,128)(2,1)S(1)}, u32[]{:S(2)}, u32[]{:S(2)}) async-start(bf16[8,1,160,128]{3,2,1,0:T(8,128)(2,1)} %broadcast_in_dim.81), calls=%async_computation.4 | async-start | bytes 655360 | tf_op jit(solution)/shard_map/all_to_all | solution.py:600
  308.1 29.1 %collective-permute-start.16 = (bf16[128,2048]{1,0:T(8,128)(2,1)}, bf16[128,2048]{1,0:T(8,128)(2,1)S(1)}, u32[]{:S(2)}, u32[]{:S(2)}) collective-permute-start(bf16[128,2048]{1,0:T(8,128)(2,1)} %convolution_convert_fusion.1._), channel_id=1, source_target_pairs={{0,4},{4,0},{8,12},{12,8},{16,20},{20,16},{24,28},{28,24},{1,5},{5... | collective-permute-start | bytes 1572872 | tf_op jit(solution)/shard_map/ppermute | solution.py:715
  328.0 34.1 %all-to-all-start.4 = ((bf16[8,64,512]{2,1,0:T(8,128)(2,1)}), bf16[8,64,512]{2,1,0:T(8,128)(2,1)S(1)}, u32[]{:S(2)}, u32[]{:S(2)}) async-start(bf16[8,64,512]{2,1,0:T(8,128)(2,1)} %after.37), calls=%async_computation.5 | async-start | bytes 1048576 | tf_op jit(solution)/shard_map/all_to_all | solution.py:700
  333.4 23.9 %collective-permute-start.26 = (bf16[8,64,512]{2,1,0:T(8,128)(2,1)}, bf16[8,64,512]{2,1,0:T(8,128)(2,1)}, u32[]{:S(2)}, u32[]{:S(2)}) collective-permute-start(bf16[8,64,512]{2,1,0:T(8,128)(2,1)} %get-tuple-element.127), channel_id=1, source_target_pairs={{0,3},{1,2},{2,1},{3,0},{4,7},{5,6},{6,5},{7,4},{8,11},{9,10},{10,... | collective-permute-start | bytes 1572872 | tf_op jit(solution)/shard_map/ppermute | solution.py:625
  336.5 30.1 %collective-permute-start.32 = (bf16[128,2048]{1,0:T(8,128)(2,1)}, bf16[128,2048]{1,0:T(8,128)(2,1)}, u32[]{:S(2)}, u32[]{:S(2)}) collective-permute-start(bf16[128,2048]{1,0:T(8,128)(2,1)} %get-tuple-element.122), channel_id=1, source_target_pairs={{0,1},{1,0},{2,3},{3,2},{4,5},{5,4},{6,7},{7,6},{8,9},{9,8},{10,11... | collective-permute-start | bytes 1572872 | tf_op jit(solution)/shard_map/ppermute | solution.py:625
  337.2 31.3 %collective-permute-start.34 = (bf16[128,2048]{1,0:T(8,128)(2,1)}, bf16[128,2048]{1,0:T(8,128)(2,1)}, u32[]{:S(2)}, u32[]{:S(2)}) collective-permute-start(bf16[128,2048]{1,0:T(8,128)(2,1)} %get-tuple-element.123), channel_id=1, source_target_pairs={{0,3},{1,2},{2,1},{3,0},{4,7},{5,6},{6,5},{7,4},{8,11},{9,10},{10,... | collective-permute-start | bytes 1572872 | tf_op jit(solution)/shard_map/ppermute | solution.py:625
  338.3 41.5 %collective-permute-start.33 = (bf16[128,2048]{1,0:T(8,128)(2,1)S(1)}, bf16[128,2048]{1,0:T(8,128)(2,1)}, u32[]{:S(2)}, u32[]{:S(2)}) collective-permute-start(bf16[128,2048]{1,0:T(8,128)(2,1)S(1)} %get-tuple-element.124), channel_id=1, source_target_pairs={{0,2},{1,3},{2,0},{3,1},{4,6},{5,7},{6,4},{7,5},{8,10},{9,11},{10,... | collective-permute-start | bytes 1572872 | tf_op jit(solution)/shard_map/ppermute | solution.py:625
  347.0 39.9 %collective-permute-start.18 = (bf16[128,2048]{1,0:T(8,128)(2,1)S(1)}, bf16[128,2048]{1,0:T(8,128)(2,1)}, u32[]{:S(2)}, u32[]{:S(2)}) collective-permute-start(bf16[128,2048]{1,0:T(8,128)(2,1)S(1)} %copy-done.25), channel_id=1, source_target_pairs={{0,4},{4,0},{8,12},{12,8},{16,20},{20,16},{24,28},{28,24},{1,5},{5... | collective-permute-start | bytes 1572872 | tf_op jit(solution)/shard_map/ppermute | solution.py:718
  357.2 29.7 %collective-permute-start.17 = (bf16[128,2048]{1,0:T(8,128)(2,1)}, bf16[128,2048]{1,0:T(8,128)(2,1)}, u32[]{:S(2)}, u32[]{:S(2)}) collective-permute-start(bf16[128,2048]{1,0:T(8,128)(2,1)} %after.36), channel_id=1, source_target_pairs={{0,8},{4,12},{8,16},{12,20},{16,24},{20,28},{24,0},{28,4},{1,9},{5... | collective-permute-start | bytes 1572872 | tf_op jit(solution)/shard_map/ppermute | solution.py:725
  362.1 28.8 %all-to-all-start.5 = ((bf16[8,64,512]{2,1,0:T(8,128)(2,1)}), bf16[8,64,512]{2,1,0:T(8,128)(2,1)S(1)}, u32[]{:S(2)}, u32[]{:S(2)}) async-start(bf16[8,64,512]{2,1,0:T(8,128)(2,1)} %fusion.19.refs_1_), calls=%async_computation.6 | async-start | bytes 1048576 | tf_op jit(solution)/shard_map/all_to_all | solution.py:700
  385.7 35.4 %collective-permute-start.28 = (bf16[128,2048]{1,0:T(8,128)(2,1)}, bf16[128,2048]{1,0:T(8,128)(2,1)}, u32[]{:S(2)}, u32[]{:S(2)}) collective-permute-start(bf16[128,2048]{1,0:T(8,128)(2,1)} %get-tuple-element.55.refs_3_), channel_id=1, source_target_pairs={{0,4},{4,0},{8,12},{12,8},{16,20},{20,16},{24,28},{28,24},{1,5},{5... | collective-permute-start | bytes 1572872 | tf_op jit(solution)/shard_map/ppermute | solution.py:718
  (59 other events, 477.1 us)
Sparse Core Ops, SparseCore 0:
  77.2 86.3 all-gather.1
  199.3 97.2 reduce-scatter.1

commit v2 on v1

--- a/solution.py
+++ b/solution.py
@@ -85,16 +85,14 @@
 ROW_LOG, ROW_CONV, ROW_CONV_B, ROW_DT_B, ROW_SKIP = 0, 16, 20, 21, 22
 
 
-def assemble_kernel(slots_ref, *refs):
-    n = slots_ref.shape[0]
-    pieces, (w_ref, gain_ref, gains_ref, w_sem, gain_sem) = refs[:n], refs[n:]
+def assemble_kernel(pieces_ref, w_ref, gain_ref, gains_ref, w_sem, gain_sem):
+    n = pieces_ref.shape[0]
     deep = w_ref.shape[0] // n
     copies = []
-    for k, piece in enumerate(pieces):
-        slot = slots_ref[k]
-        at = pl.multiple_of(slot * deep, deep)
-        copies.append(pltpu.make_async_copy(piece.at[:deep], w_ref.at[pl.ds(at, deep)], w_sem.at[k]))
-        copies.append(pltpu.make_async_copy(piece.at[deep : deep + GROUP], gains_ref.at[slot], gain_sem.at[k]))
+    for k in range(n):
+        piece = pieces_ref.at[k]
+        copies.append(pltpu.make_async_copy(piece.at[:deep], w_ref.at[k * deep : (k + 1) * deep], w_sem.at[k]))
+        copies.append(pltpu.make_async_copy(piece.at[deep : deep + GROUP], gains_ref.at[k], gain_sem.at[k]))
     for copy in copies:
         copy.start()
     for copy in copies:
@@ -107,11 +105,11 @@
     gain_ref[...] = jnp.concatenate(parts, axis=1)
 
 
-def assemble(pieces, slots, deep):
-    n, columns = len(pieces), pieces[0].shape[1]
+def assemble(pieces, deep):
+    n, _, columns = pieces.shape
     return pl.pallas_call(
         assemble_kernel,
-        in_specs=[pl.BlockSpec(memory_space=pltpu.SMEM), *[ANY] * n],
+        in_specs=[ANY],
         out_specs=[pl.BlockSpec(memory_space=pltpu.VMEM)] * 2,
         out_shape=[jax.ShapeDtypeStruct((n * deep, columns), BF16), jax.ShapeDtypeStruct((1, n * deep), F32)],
         scratch_shapes=[
@@ -121,7 +119,7 @@
         ],
         compiler_params=pltpu.CompilerParams(vmem_limit_bytes=VMEM),
         name="assemble",
-    )(slots, *pieces)
+    )(pieces)
 
 
 def project_kernel(slots_ref, w_in_ref, gain_ref, w_xt_ref, table_ref, mask_ref, *refs):
@@ -241,8 +239,8 @@
     return (ahead == 0).astype(BF16), ahead[: GROUP * STATE]
 
 
-def forward_kernel(mixed_ref, act_ref, gate_ref, mask_ref, w_dtt_ref, table_ref, own_ref, _,
-                   branch_ref, y_ref, states_ref, _out, h_ref, stepd_ref, drive_ref, b_ref):
+def forward_kernel(mixed_ref, act_ref, gate_ref, mask_ref, w_dtt_ref, table_ref, own_ref,
+                   branch_ref, y_ref, states_ref, h_ref, stepd_ref, drive_ref, b_ref):
     @pl.when(pl.program_id(0) == 0)
     def _():
         h_ref[...] = jnp.zeros_like(h_ref)
@@ -278,23 +276,21 @@
     branch_ref[...] = (y_total * (gate * sigmoid(gate))).astype(BF16)
 
 
-def scan_forward(mixed, act, gate, mask, w_dtt, table, own, w_out):
+def scan_forward(mixed, act, gate, mask, w_dtt, table, own):
     count, width = act.shape
     return pl.pallas_call(
         forward_kernel,
         grid=(count // BLOCK,),
         in_specs=[
             pl.BlockSpec((1, MIXED, BLOCK), lambda i: (i, 0, 0)), rows_spec(width), rows_spec(width), rows_spec(8),
-            whole_spec(w_dtt.shape), whole_spec(table.shape), whole_spec(own.shape), ANY,
-        ],
-        out_specs=[rows_spec(width), rows_spec(width), pl.BlockSpec((BLOCK * STATE, width), lambda i: (i, 0)), ANY],
+            whole_spec(w_dtt.shape), whole_spec(table.shape), whole_spec(own.shape),
+        ],
+        out_specs=[rows_spec(width), rows_spec(width), pl.BlockSpec((BLOCK * STATE, width), lambda i: (i, 0))],
         out_shape=[
             jax.ShapeDtypeStruct((count, width), BF16),
             jax.ShapeDtypeStruct((count, width), F32),
             jax.ShapeDtypeStruct((count * STATE, width), BF16),
-            jax.ShapeDtypeStruct(w_out.shape, w_out.dtype),
-        ],
-        input_output_aliases={7: 3},
+        ],
         scratch_shapes=[
             pltpu.VMEM((STATE, width), F32),
             pltpu.VMEM((BLOCK, width), F32),
@@ -304,11 +300,11 @@
         compiler_params=pltpu.CompilerParams(vmem_limit_bytes=VMEM),
         cost_estimate=pl.CostEstimate(flops=8 * count * width * STATE * 16, bytes_accessed=64 << 20, transcendentals=0),
         name="scan_forward",
-    )(mixed, act, gate, mask, w_dtt, table, own, w_out)
+    )(mixed, act, gate, mask, w_dtt, table, own)
 
 
 def backward_kernel(mixed_ref, act_ref, gate_ref, d_branch_ref, mask_ref, states_ref, ahead_ref,
-                    w_dtt_ref, table_ref, own_ref, offset_ref,
+                    w_dtt_ref, table_ref, own_ref, offset_ref, _block, _gate,
                     d_mixed_ref, d_act_ref, sums_ref, dt_grad_ref,
                     p_ref, dy_ref, stepd_ref, c_ref, s1_ref, s2_ref, bg_ref, dyt_ref, sat_ref, d_b_ref, d_c_ref,
                     adj_a_ref, adj_b_ref, rq_a_ref, rq_b_ref):
@@ -405,7 +401,7 @@
     d_mixed_ref[0, :DT_RANK] = dot_nt(w_dtt_ref[...], d_pre).astype(BF16)
 
 
-def scan_backward(mixed, act, gate, d_branch, mask, states, w_dtt, table, own, offsets):
+def scan_backward(mixed, act, gate, d_branch, mask, states, w_dtt, table, own, offsets, *before):
     count, width = act.shape
     blocks = count // BLOCK
     last = blocks - 1
@@ -419,7 +415,7 @@
             mixed_spec, rows, rows, rows, rows_spec(8, lambda i: last - i),
             pl.BlockSpec((BLOCK * STATE, width), lambda i: (last - i, 0)),
             pl.BlockSpec((STATE, width), lambda i: (jnp.maximum((last - i) * BLOCK - 1, 0), 0)),
-            whole_spec(w_dtt.shape), whole_spec(table.shape), whole_spec(own.shape), whole_spec(offsets.shape),
+            whole_spec(w_dtt.shape), whole_spec(table.shape), whole_spec(own.shape), whole_spec(offsets.shape), ANY, ANY,
         ],
         out_specs=[mixed_spec, rows, whole_spec((24, width)), whole_spec((DT_RANK, width))],
         out_shape=[
@@ -448,13 +444,53 @@
         compiler_params=pltpu.CompilerParams(vmem_limit_bytes=VMEM),
         cost_estimate=pl.CostEstimate(flops=8 * count * width * STATE * 32, bytes_accessed=96 << 20, transcendentals=0),
         name="scan_backward",
-    )(mixed, act, gate, d_branch, mask, states, states, w_dtt, table, own, offsets)
+    )(mixed, act, gate, d_branch, mask, states, states, w_dtt, table, own, offsets, *before)
 
 
 def finish_kernel(mixed_ref, d_act_ref, conv_out_ref, conv_in_ref, ahead_ref, act_ref, d_gate_ref, mask_ref, w_xt_ref,
                   table_ref, d_proj_ref, x_grad_ref, sums_ref, line_ref, masked_ref):
-    first = pl.program_id(0) == 0
     rows, width = act_ref.shape
+    d_conv_in = conv_backward(
+        (mixed_ref, d_act_ref, conv_out_ref, conv_in_ref, ahead_ref, act_ref, mask_ref, w_xt_ref, table_ref,
+         x_grad_ref, sums_ref, line_ref, masked_ref), rows, width, pl.program_id(0) == 0
+    )
+    d_proj_ref[:, :width] = d_conv_in.astype(BF16)
+    d_proj_ref[:, width:] = d_gate_ref[...]
+
+
+def finish(mixed, d_act, conv_out, conv_in, act, d_gate, mask, w_xt, table):
+    count, width = act.shape
+    blocks = count // WIDE
+    last = blocks - 1
+
+    def rows(columns):
+        return rows_spec(columns, lambda i: last - i, WIDE)
+
+    per = WIDE // GROUP
+    return pl.pallas_call(
+        finish_kernel,
+        grid=(blocks,),
+        in_specs=[
+            pl.BlockSpec((WIDE // BLOCK, MIXED, BLOCK), lambda i: (last - i, 0, 0)), rows(width), rows(width), rows(width),
+            pl.BlockSpec((GROUP, width), lambda i: (jnp.maximum((last - i) * per - 1, 0), 0)),
+            rows(width), rows(width), rows(8), whole_spec(w_xt.shape), whole_spec(table.shape),
+        ],
+        out_specs=[rows(2 * width), whole_spec((MIXED, width)), whole_spec((8, width))],
+        out_shape=[
+            jax.ShapeDtypeStruct((count, 2 * width), BF16),
+            jax.ShapeDtypeStruct((MIXED, width), F32),
+            jax.ShapeDtypeStruct((8, width), F32),
+        ],
+        scratch_shapes=[pltpu.VMEM((WIDE + 8, width), F32), pltpu.VMEM((CONV - 1, WIDE + 8, width), F32)],
+        compiler_params=pltpu.CompilerParams(vmem_limit_bytes=VMEM),
+        cost_estimate=pl.CostEstimate(flops=1 << 31, bytes_accessed=12 << 20, transcendentals=0),
+        name="finish",
+    )(mixed, d_act, conv_out, conv_in, conv_in, act, d_gate, mask, w_xt, table)
+
+
+def conv_backward(refs, rows, width, first):
+    (mixed_ref, d_act_ref, conv_out_ref, conv_in_ref, ahead_ref, act_ref, mask_ref, w_xt_ref, table_ref,
+     x_grad_ref, sums_ref, line_ref, masked_ref) = refs
 
     @pl.when(first)
     def _():
@@ -485,68 +521,111 @@
             masked_ref[k, :rows] = masked
             masked = masked_ref[k, CONV - 1 - k : CONV - 1 - k + rows]
         d_conv_in = d_conv_in + table_ref[ROW_CONV + k : ROW_CONV + k + 1, :] * masked
-    d_proj_ref[:, :width] = d_conv_in.astype(BF16)
-    d_proj_ref[:, width:] = d_gate_ref[...]
-
-
-def finish(mixed, d_act, conv_out, conv_in, act, d_gate, mask, w_xt, table):
+    return d_conv_in
+
+
+def tail_kernel(where_ref, mixed_ref, d_act_ref, conv_out_ref, conv_in_ref, ahead_ref, act_ref, d_gate_ref, mask_ref,
+                w_xt_ref, table_ref, w_any, lowered_any, *refs):
+    mine, theirs, part_ref = refs[:4], refs[4:8], refs[8]
+    (x_grad_ref, sums_ref, line_ref, masked_ref, w_ref, lowered_ref, d_conv_ref, gain_ref,
+     sem_ref) = refs[9:]
+    step = pl.program_id(0)
+    rows, width = act_ref.shape
+    tokens, model = mine[0].shape
+    row, column = where_ref[0], where_ref[1]
+    block = pl.num_programs(0) - 1 - step
+    w_copy = pltpu.make_async_copy(w_any, w_ref, sem_ref.at[0])
+    lowered_copy = pltpu.make_async_copy(lowered_any, lowered_ref, sem_ref.at[1])
+
+    @pl.when(step == 0)
+    def _():
+        w_copy.start()
+        lowered_copy.start()
+        gain_ref[...] = jnp.zeros_like(gain_ref)
+
+    d_conv_in = conv_backward(
+        (mixed_ref, d_act_ref, conv_out_ref, conv_in_ref, ahead_ref, act_ref, mask_ref, w_xt_ref, table_ref,
+         x_grad_ref, sums_ref, line_ref, masked_ref), rows, width, step == 0
+    ).astype(BF16)
+    at = pl.multiple_of(block * rows, rows)
+    d_conv_ref[pl.ds(at, rows), :] = d_conv_in
+
+    @pl.when(step == 0)
+    def _():
+        w_copy.wait()
+        lowered_copy.wait()
+
+    d_proj = jnp.concatenate([d_conv_in, d_gate_ref[...]], axis=1)
+    out = dot_nt(d_proj, w_ref[...])
+    gain_ref[...] += jnp.sum(out * lowered_ref[pl.ds(at, rows), :].astype(F32), axis=0, keepdims=True)
+    halves = out[:tokens].astype(BF16), out[tokens:].astype(BF16)
+    k = lax.rem(row - block + 4, 4)
+    for j in range(4):
+        for c in range(2):
+
+            @pl.when(jnp.logical_and(k == j, column == c))
+            def _(j=j, c=c):
+                mine[j][...] = halves[c]
+                theirs[j][...] = halves[1 - c]
+
+    @pl.when(block == 0)
+    def _():
+        shards, places, each, _ = part_ref.shape
+        each = each - 8
+        many = shards * each
+
+        def one(s, carry):
+            lanes = pl.ds(pl.multiple_of(s * many, many), many)
+            chunk = dot_tn(lowered_ref[:, lanes], d_conv_ref[...]).astype(BF16)
+            gains = jnp.broadcast_to(gain_ref[:, lanes], (8, many)).astype(BF16)
+            for j in range(shards):
+                part_ref[j, s, :each] = chunk[j * each : (j + 1) * each]
+                part_ref[j, s, each:] = jnp.concatenate([gains] * (width // many), axis=1)
+            return carry
+
+        lax.fori_loop(0, places, one, 0)
+
+
+def tail(where, mixed, d_act, conv_out, conv_in, act, d_gate, mask, w_xt, table, w_rows, lowered, seqs, shards):
     count, width = act.shape
-    blocks = count // WIDE
+    model = lowered.shape[1]
+    tokens, many = count // seqs, model // seqs
+    blocks = count // (2 * tokens)
     last = blocks - 1
+    per = 2 * tokens // GROUP
 
     def rows(columns):
-        return rows_spec(columns, lambda i: last - i, WIDE)
-
-    per = WIDE // GROUP
-    return pl.pallas_call(
-        finish_kernel,
+        return pl.BlockSpec((2 * tokens, columns), lambda i: (last - i, 0))
+
+    shapes = [jax.ShapeDtypeStruct((tokens, model), BF16)] * 8
+    shapes += [jax.ShapeDtypeStruct((shards, seqs, many // shards + 8, width), BF16)]
+    shapes += [jax.ShapeDtypeStruct((MIXED, width), F32), jax.ShapeDtypeStruct((8, width), F32)]
+    out = pl.pallas_call(
+        tail_kernel,
         grid=(blocks,),
         in_specs=[
-            pl.BlockSpec((WIDE // BLOCK, MIXED, BLOCK), lambda i: (last - i, 0, 0)), rows(width), rows(width), rows(width),
+            pl.BlockSpec(memory_space=pltpu.SMEM),
+            pl.BlockSpec((2 * tokens // BLOCK, MIXED, BLOCK), lambda i: (last - i, 0, 0)),
+            rows(width), rows(width), rows(width),
             pl.BlockSpec((GROUP, width), lambda i: (jnp.maximum((last - i) * per - 1, 0), 0)),
-            rows(width), rows(width), rows(8), whole_spec(w_xt.shape), whole_spec(table.shape),
-        ],
-        out_specs=[rows(2 * width), whole_spec((MIXED, width)), whole_spec((8, width))],
-        out_shape=[
-            jax.ShapeDtypeStruct((count, 2 * width), BF16),
-            jax.ShapeDtypeStruct((MIXED, width), F32),
-            jax.ShapeDtypeStruct((8, width), F32),
-        ],
-        scratch_shapes=[pltpu.VMEM((WIDE + 8, width), F32), pltpu.VMEM((CONV - 1, WIDE + 8, width), F32)],
+            rows(width), rows(width), rows(8), whole_spec(w_xt.shape), whole_spec(table.shape), ANY, ANY,
+        ],
+        out_specs=[whole_spec(shape.shape) for shape in shapes],
+        out_shape=shapes,
+        scratch_shapes=[
+            pltpu.VMEM((2 * tokens + 8, width), F32),
+            pltpu.VMEM((CONV - 1, 2 * tokens + 8, width), F32),
+            pltpu.VMEM(w_rows.shape, BF16),
+            pltpu.VMEM(lowered.shape, BF16),
+            pltpu.VMEM((count, width), BF16),
+            pltpu.VMEM((1, model), F32),
+            pltpu.SemaphoreType.DMA((2,)),
+        ],
         compiler_params=pltpu.CompilerParams(vmem_limit_bytes=VMEM),
-        cost_estimate=pl.CostEstimate(flops=1 << 31, bytes_accessed=12 << 20, transcendentals=0),
-        name="finish",
-    )(mixed, d_act, conv_out, conv_in, conv_in, act, d_gate, mask, w_xt, table)
-
-
-def lower_kernel(where_ref, d_proj_ref, w_ref, _, *out_refs):
-    row, column = where_ref[0], where_ref[1]
-    tokens = out_refs[0].shape[0]
-    mine, theirs = out_refs[:4], out_refs[4:]
-    for i, k in enumerate((1, 2, 3, 0)):
-        at = lax.rem(row - k + 4, 4) * 2
-        parts = [d_proj_ref[pl.ds(pl.multiple_of((at + column) * tokens, tokens), tokens), :]]
-        if i:
-            parts.append(d_proj_ref[pl.ds(pl.multiple_of((at + 1 - column) * tokens, tokens), tokens), :])
-        out = dot_nt(jnp.concatenate(parts, axis=0), w_ref[...]).astype(BF16)
-        mine[i][...] = out[:tokens]
-        if i:
-            theirs[i - 1][...] = out[tokens:]
-
-
-def lower(where, d_proj, w_rows, first):
-    tokens, model = first.shape
-    vmem = pl.BlockSpec(memory_space=pltpu.VMEM)
-    out = pl.pallas_call(
-        lower_kernel,
-        in_specs=[pl.BlockSpec(memory_space=pltpu.SMEM), vmem, vmem, ANY],
-        out_specs=[vmem] * 7,
-        out_shape=[jax.ShapeDtypeStruct((tokens, model), BF16)] * 7,
-        compiler_params=pltpu.CompilerParams(vmem_limit_bytes=VMEM),
-        cost_estimate=pl.CostEstimate(flops=2 * d_proj.size * model, bytes_accessed=12 << 20, transcendentals=0),
-        name="lower",
-    )(where.astype(jnp.int32), d_proj, w_rows, first)
-    return out[:4], out[4:]
+        cost_estimate=pl.CostEstimate(flops=1 << 33, bytes_accessed=32 << 20, transcendentals=0),
+        name="tail",
+    )(where, mixed, d_act, conv_out, conv_in, conv_in, act, d_gate, mask, w_xt, table, w_rows, lowered)
+    return list(out[:4]), out[4:8], *out[8:]
 
 
 def line_ring(seqs):
@@ -557,20 +636,22 @@
     return [(i, i ^ bit) for i in range(size)]
 
 
-def gather_all(part, shard):
+def gather_all(part, owned, owner, early, middle):
     seqs, shards = lax.axis_size("seq"), lax.axis_size("fsdp")
     if (seqs, shards) != (8, 4):
-        whole, wide = lax.all_gather(part, "seq", axis=0), lax.all_gather(shard, "fsdp", axis=0)
-        return (
-            [whole[k] for k in range(seqs)], jnp.arange(seqs, dtype=jnp.int32),
-            [wide[k] for k in range(shards)], jnp.arange(shards, dtype=jnp.int32),
-        )
+        whole = lax.all_gather(part, "seq", axis=0)
+        owned = lax.dynamic_index_in_dim(lax.all_gather(owned, "fsdp"), owner, 0, False)
+        return [whole[k] for k in range(seqs)], jnp.arange(seqs, dtype=jnp.int32), lambda *_: owned
     place, here = lax.axis_index("seq"), lax.axis_index("fsdp")
     row, column = place // 2, place % 2
     swap, ring = pair_swap(seqs, 1), line_ring(seqs)
+    first, second = [], []
+    for s in range(seqs):
+        own = s * shards // seqs
+        first.append((s * shards + own, s * shards + (own ^ 2)))
+        second.append((s * shards + own, s * shards + (own ^ 1)))
+        second.append((s * shards + (own ^ 2), s * shards + (own ^ 3)))
     pieces, slots = [], []
-    far = lax.ppermute(shard, "fsdp", pair_swap(shards, 2))
-    beside = lax.ppermute(shard, "fsdp", pair_swap(shards, 1))
     for k in range(4):
         slot = (row - k + 4) % 4 * 2
         swapped = lax.ppermute(part, "seq", swap)
@@ -578,17 +659,16 @@
         slots += [slot + column, slot + 1 - column]
         if k == 3:
             break
-        part = lax.ppermute(part, "seq", ring)
-        if k == 0:
-            part = after(part, swapped)
-        elif k == 1:
-            part = after(part, swapped, beside)
-            far = after(far, part)
-            both = lax.ppermute(far, "fsdp", pair_swap(shards, 1))
-        else:
-            part = after(part, swapped, both)
-    w_slots = jnp.stack([here, here ^ 2, here ^ 1, here ^ 3]).astype(jnp.int32)
-    return pieces, jnp.stack(slots).astype(jnp.int32), [shard, far, beside, both], w_slots
+        others = (early, middle, ())[k]
+        part = after(lax.ppermute(part, "seq", ring), swapped, *others)
+    across = lax.ppermute(after(owned, pieces[-2]), ("seq", "fsdp"), first)
+
+    def rest(early, late):
+        same_core = jnp.where(here == owner, owned, after(across, early))
+        last = lax.ppermute(same_core, ("seq", "fsdp"), second)
+        return jnp.where((here ^ owner) % 2 == 0, same_core, after(last, late))
+
+    return pieces, jnp.stack(slots).astype(jnp.int32), rest
 
 
 def sum_over_seq(part):
@@ -600,30 +680,22 @@
     return lax.all_to_all(copies, "seq", split_axis=0, concat_axis=0, tiled=True).reshape(part.shape), total
 
 
-def from_owner(shares, owner):
-    seqs, shards = lax.axis_size("seq"), lax.axis_size("fsdp")
-    here = lax.axis_index("fsdp")
-    if (seqs, shards) != (8, 4):
-        every = jnp.stack([shares(j) for j in range(shards)])
-        every = lax.dynamic_index_in_dim(lax.all_gather(every, "fsdp"), owner, 0, False)
-        return [lax.dynamic_index_in_dim(every, here, 0, False)]
-    got = [jnp.where(here == owner, shares(here), 0)]
-    for j in range(1, shards):
-        pairs = [(s * shards + s * shards // seqs, s * shards + (s * shards // seqs ^ j)) for s in range(seqs)]
-        got.append(lax.ppermute(shares(here ^ j), ("seq", "fsdp"), pairs))
-    return got
-
-
 def scatter_shards(blocks, kind=BF16):
     shards = lax.axis_size("fsdp")
+    blocks = blocks if isinstance(blocks, list) else [blocks]
+
+    def block(j):
+        parts = [lax.dynamic_index_in_dim(each, j, 0, False).astype(kind) for each in blocks]
+        return jnp.concatenate(parts, axis=-2) if len(parts) > 1 else parts[0]
+
     if shards != 4 or lax.axis_size("seq") != 8:
-        return lax.psum_scatter(blocks, "fsdp", scatter_dimension=0)
+        return [lax.psum_scatter(jnp.stack([block(j) for j in range(shards)]), "fsdp", scatter_dimension=0)]
     here = lax.axis_index("fsdp")
-    total = lax.dynamic_index_in_dim(blocks, here, 0, False).astype(F32)
-    for j in range(1, shards):
-        theirs = lax.dynamic_index_in_dim(blocks, here ^ j, 0, False).astype(kind)
-        total = total + lax.ppermute(theirs, "fsdp", pair_swap(shards, j)).astype(F32)
-    return total
+    return [block(here)] + [lax.ppermute(block(here ^ j), "fsdp", pair_swap(shards, j)) for j in range(1, shards)]
+
+
+def add_up(parts):
+    return sum(part.astype(F32) for part in parts)
 
 
 def local(
@@ -660,76 +732,80 @@
         axis=1,
     )
     shard = jnp.concatenate([in_cols, gain_rows, small], axis=0)
-    pieces, slots, w_pieces, w_slots = gather_all(x_in[0], shard)
-    small = sum(jnp.where(w_slots[k] == owner, piece[deep + GROUP :], 0) for k, piece in enumerate(w_pieces))
+    mask = doc_masks(doc_lengths[0], count)
+    own, offsets = owns()
+    rows = model // (seqs * shards)
+    out_rows = lax.dynamic_slice_in_dim(out_weight, offset, width, 0)
+    w_pieces = lax.all_gather(shard, "fsdp", axis=0)
+    pieces, slots, w_out_of = gather_all(x_in[0], out_rows, owner, (shard, out_rows), (own, offsets, mask))
+    small = lax.dynamic_index_in_dim(w_pieces[:, deep + GROUP :], owner, 0, False)
     w_xt, w_dtt, table = small[:, :width], small[:DT_RANK, width:], small[DT_RANK:, width:].astype(F32)
-    cot_all = lax.all_gather(after(cotangent[0], pieces[-2]), "seq", axis=0, tiled=True)
-    rows = model // (seqs * shards)
-    start = place * shards * rows % deep
-    in_got = from_owner(
-        lambda j: after(lax.dynamic_slice_in_dim(in_weight, start + j * rows, rows, 0), pieces[2]), owner
-    )
-    out_rows = after(lax.dynamic_slice_in_dim(out_weight, offset, width, 0), pieces[-2])
-    out_got = from_owner(lambda j: out_rows, owner)
-    mask = doc_masks(doc_lengths[0], count)
-
-    own, offsets = owns()
-    w_rows, gain = assemble(w_pieces, w_slots, deep)
+    cot_all = lax.all_gather(after(cotangent[0], pieces[-4]), "seq", axis=0, tiled=True)
+
+    w_rows, gain = assemble(w_pieces, deep)
     lowered, conv_in, conv_out, act, gate, mixed = project(pieces, slots, w_rows, gain, w_xt, table, mask)
     mixed, share = sum_over_seq(mixed)
-    in_rows = sum(in_got[1:], after(in_got[0], share))
-    w_out = sum(out_got[1:], after(out_got[0], share))
-    mixed = after(mixed, in_rows)
-    branch, y_total, states, w_out = scan_forward(mixed, act, gate, mask, w_dtt, table, own, w_out)
+    branch, y_total, states = scan_forward(mixed, act, gate, mask, w_dtt, table, own)
+    w_out = w_out_of(share, branch)
     block_part = dot_nn(branch, w_out).astype(BF16)
     block_sum = lax.psum_scatter(block_part, "seq", scatter_dimension=0, tiled=True)
     block_out = (x_in[0].astype(F32) + block_sum.astype(F32)).astype(BF16)
 
     d_branch = dot_nt(cot_all, w_out)
-    d_gate = (d_branch * y_total * silu_slope(gate)).astype(BF16)
-    d_branch = after(d_branch, block_part, d_gate)
-    d_mixed, d_act, sums, dt_grad = scan_backward(
-        mixed, act, gate, d_branch, mask, states, w_dtt, table, own, offsets
-    )
-    out_grad = scatter_shards(dot_tn(branch, cot_all).reshape(shards, width // shards, model))
-
-    def shared(part):
-        return scatter_shards(part.reshape(seqs, shards, rows, width).transpose(1, 0, 2, 3)).astype(BF16)
+
+    def shared(part, *more):
+        blocks = [part.reshape(seqs, shards, rows, width), *more]
+        return scatter_shards([block.transpose(1, 0, 2, 3) for block in blocks])
 
     def spread(part):
         part = lax.all_to_all(part, "seq", split_axis=0, concat_axis=0, tiled=True)
         return part.transpose(1, 0, 2).reshape(rows, INNER).astype(F32)
 
-    gate_sum = shared(dot_tn(lowered, d_gate))
-    d_mixed, share = sum_over_seq(d_mixed)
-    d_mixed = after(d_mixed, block_sum)
-    gate_grad = spread(after(gate_sum, share))
-    d_proj, x_proj_grad, conv_sums = finish(d_mixed, d_act, conv_out, conv_in, act, d_gate, mask, w_xt, table)
-
-    small = jnp.concatenate([x_proj_grad, dt_grad, sums, conv_sums], axis=0)
+    d_gate = (d_branch * y_total * silu_slope(gate)).astype(BF16)
+    gate_got = shared(dot_tn(lowered, d_gate).astype(BF16))
+    d_mixed, d_act, sums, dt_grad = scan_backward(
+        mixed, act, gate, d_branch, mask, states, w_dtt, table, own, offsets, block_part, gate_got[0]
+    )
+    d_mixed, share = sum_over_seq(after(d_mixed, *gate_got[1:]))
+    out_part = dot_tn(after(branch, share), cot_all).astype(BF16)
+    out_sum = lax.psum_scatter(out_part.reshape(shards, width // shards, model), "fsdp", scatter_dimension=0)
+    out_grad = out_sum.astype(F32)
+    gate_sum = add_up([after(gate_got[0], share), *gate_got[1:]]).astype(BF16)
+    d_mixed = after(d_mixed, block_sum, gate_sum, out_part)
+    gate_grad = spread(gate_sum)
     if seqs == 8:
         row, column = place // 2, place % 2
         swap, ring = pair_swap(seqs, 1), line_ring(seqs)
-        first = (row + 3) % 4 * 2 + 1 - column
-        first = dot_nt(lax.dynamic_slice_in_dim(d_proj, first * tokens, tokens, 0), w_rows).astype(BF16)
-        swapped = [lax.ppermute(first, "seq", swap)]
-        mine, theirs = lower(jnp.stack([row, column]), d_proj, w_rows, first)
-        conv_sum = shared(dot_tn(lowered, after(d_proj, *theirs)[:, :width]))
-        swapped += [lax.ppermute(block, "seq", swap) for block in theirs]
-        total = mine[0].astype(F32) + swapped[0].astype(F32)
-        befores = (theirs, (gate_grad,), (conv_sum,))
+        mine, theirs, conv_part, x_proj_grad, conv_sums = tail(
+            jnp.stack([row, column]).astype(jnp.int32),
+            d_mixed, d_act, conv_out, conv_in, act, d_gate, mask, w_xt, table, w_rows, lowered, seqs, shards,
+        )
+        small = jnp.concatenate([x_proj_grad, dt_grad, sums, conv_sums], axis=0)
+        swapped = [lax.ppermute(block, "seq", swap) for block in theirs]
+        conv_sum = lax.psum_scatter(conv_part, "fsdp", scatter_dimension=0)
+        conv_sum = lax.all_to_all(conv_sum, "seq", split_axis=0, concat_axis=0, tiled=True)
+        total = mine[1].astype(F32) + swapped[1].astype(F32)
+        befores = ((), (gate_grad, out_sum), ())
         for k in range(3):
             total = after(total.astype(BF16), *befores[k])
+            if k == 1:
+                small = after(small, total)
+            n = (k + 2) % 4
+            arrived = lax.ppermute(total, "seq", ring).astype(F32)
             if k == 2:
-                small = after(small, total)
-            total = lax.ppermute(total, "seq", ring).astype(F32) + mine[k + 1].astype(F32) + swapped[k + 1].astype(F32)
+                mine[n] = after(mine[n], conv_sum)
+            total = arrived + mine[n].astype(F32) + swapped[n].astype(F32)
         d_low_own = total
     else:
-        conv_sum = shared(dot_tn(lowered, d_proj[:, :width]))
-        d_lowered = dot_nt(d_proj, w_rows).astype(BF16)
-        d_low_own = lax.psum_scatter(d_lowered, "seq", scatter_dimension=0, tiled=True).astype(F32)
-    conv_grad = spread(conv_sum)
-
+        d_proj, x_proj_grad, conv_sums = finish(d_mixed, d_act, conv_out, conv_in, act, d_gate, mask, w_xt, table)
+        small = jnp.concatenate([x_proj_grad, dt_grad, sums, conv_sums], axis=0)
+        d_lowered = dot_nt(d_proj, w_rows)
+        gain_part = jnp.sum(d_lowered * lowered.astype(F32), axis=0).reshape(seqs, 1, 1, shards * rows)
+        gain_part = jnp.broadcast_to(gain_part, (seqs, shards, 8, shards * rows))
+        gain_part = jnp.pad(gain_part, ((0, 0), (0, 0), (0, 0), (0, width - shards * rows)))
+        conv_sum = add_up(shared(dot_tn(lowered, d_proj[:, :width]), gain_part)).astype(BF16)
+        conv_sum = lax.all_to_all(conv_sum, "seq", split_axis=0, concat_axis=0, tiled=True)
+        d_low_own = lax.psum_scatter(d_lowered.astype(BF16), "seq", scatter_dimension=0, tiled=True).astype(F32)
     x_own = x_in[0].astype(F32)
     inv_own = lax.rsqrt(jnp.mean(x_own * x_own, axis=1, keepdims=True) + NORM_EPS)
     normed_own = x_own * inv_own
@@ -737,20 +813,23 @@
     x_grad = cotangent[0].astype(F32) + inv_own * (
         d_norm - normed_own * jnp.mean(d_norm * normed_own, axis=1, keepdims=True)
     )
+    small = small.reshape(-1, shards, width // shards).transpose(1, 0, 2)
+    small = lax.psum_scatter(small, "fsdp", scatter_dimension=0)
+    conv_sum = conv_sum.astype(F32)
+    conv_grad = conv_sum[:, :rows].transpose(1, 0, 2).reshape(rows, INNER)
     in_grad = jnp.concatenate([conv_grad, gate_grad], axis=1)
     gain_own = lax.dynamic_slice_in_dim(gain[0], (place * shards + lax.axis_index("fsdp")) * rows, rows, 0)
-    gain_grad = jnp.sum(in_grad * in_rows.astype(F32), axis=1) / gain_own
-    small = small.reshape(-1, shards, width // shards).transpose(1, 0, 2)
-    small = scatter_shards(small, F32)
+    gain_sum = jnp.sum(conv_sum[:, rows], axis=0)
+    gain_grad = lax.dynamic_slice_in_dim(gain_sum, lax.axis_index("fsdp") * rows, rows, 0) / gain_own
     at = MIXED + DT_RANK
-    tail = at + 24
+    end = at + 24
     return (
         block_out[None],
         x_grad[None],
         gain_grad,
         in_grad,
-        small[tail : tail + CONV].T,
-        small[tail + CONV],
+        small[end : end + CONV].T,
+        small[end + CONV],
         small[:MIXED].T,
         small[MIXED:at].T,
         small[at + STATE + 1],

time: 445 us -> 385 us (0.87); the launches traced: 438 us -> 383 us
  starting transfers between devices: 72.1 us -> 45.1 us
  waiting for transfers between devices: 137 us -> 117 us
  blocking collectives: 0 us -> 19.1 us
  other arithmetic: 44.6 us -> 26.3 us
  matrix products: 31 us -> 18.3 us
    ppermute x31 -> x15, waiting for transfers between devices: 77.9 us -> 40 us  [the longest x4 29.4 us: local(): swapped = [lax.ppermute(block, 'seq', swap) for block in theirs]]
    ppermute x31 -> x15, starting transfers between devices: 40.2 us -> 18.1 us  [the longest x4 5.54 us: local(): swapped = [lax.ppermute(block, 'seq', swap) for block in theirs]]
    all_to_all x0 -> x1, blocking collectives: none -> 19.1 us  [sum_over_seq(): lax.all_to_all(shares, 'seq', split_axis=0, concat_axis=0, tiled=True)]
    add x5 -> x0, other arithmetic: 13 us -> none  [the longest x1 5.16 us: local(): w_out = sum(out_got[1:], after(out_got[0], share))]
    all_to_all x2 -> x1, waiting for transfers between devices: 6.6 us -> 15.9 us  [sum_over_seq(): lax.all_to_all(shares, 'seq', split_axis=0, concat_axis=0, tiled=True)]
    dot_general x3 -> x2, matrix products: 16.1 us -> 8.6 us  [dot_tn(): lax.dot_general(a, b, (((0,), (0,)), ((), ())), preferred_element_type=F32)]
    ppermute x4, waiting for transfers between devices: 22.7 us -> 29.7 us  [gather_all(): swapped = lax.ppermute(part, 'seq', swap)]
    all_to_all x0 -> x1, starting transfers between devices: none -> 6.2 us  [local(): lax.all_to_all(conv_sum, 'seq', split_axis=0, concat_axis=0, tiled=True)]
  transfers between devices with their start and end apart: 43 -> 30, of which waited for: 19 -> 16; matrix products, arithmetic and copies ran while one was open for 22% -> 15% of each run, Pallas kernels for 22% -> 26%
where the time goes in v2:
time: 385 us; the launch traced here: 383 us
  waiting for transfers between devices  117 us (30%)
  Pallas kernels  99.4 us (26%)
  starting transfers between devices  45.1 us (12%)
  local copies, waits for them, and re-layouts  43 us (11%)
  other arithmetic  26.3 us (7%)
  blocking collectives  19.1 us (5%)
  matrix products  18.3 us (5%)
  between operations  14.8 us (4%)
    pallas_call x1, Pallas kernels, scan_backward(): pl.pallas_call(backward_kernel, grid=(blocks,), in_specs=[mixed_spec, row...  41.9 us
    ppermute x4, waiting for transfers between devices, gather_all(): swapped = lax.ppermute(part, 'seq', swap)  29.7 us
    ppermute x4, waiting for transfers between devices, local(): swapped = [lax.ppermute(block, 'seq', swap) for block in theirs]  29.4 us
    all_to_all x2, waiting for transfers between devices, sum_over_seq(): lax.all_to_all(copies, 'seq', split_axis=0, concat_axis=0, tiled=True)  22.8 us
    pallas_call x1, Pallas kernels, tail(): pl.pallas_call(tail_kernel, grid=(blocks,), in_specs=[pl.BlockSpec(memory...  21.9 us
    all_to_all x1, blocking collectives, sum_over_seq(): lax.all_to_all(shares, 'seq', split_axis=0, concat_axis=0, tiled=True)  19.1 us
    pallas_call x1, Pallas kernels, scan_forward(): pl.pallas_call(forward_kernel, grid=(count // BLOCK,), in_specs=[pl.Block...  18.4 us
    unnamed x102, local copies, waits for them, and re-layouts  17 us
  transfers between devices with their start and end apart: 30, of which 16 were waited for; matrix products, arithmetic and copies ran while one was open for 15% of the time, Pallas kernels for 26%

profile of v2, /device:TPU:0, one launch (start us, length us, event | category | flops | bytes accessed | tf_op | source)
XLA Modules:
  0.0 383.5 jit_solution(16414365736695744632)
XLA Ops:
  15.6 3.0 collective-permute-start
  20.6 3.2 constant_dynamic-slice_fusion.1.refs_3_.refs_0_
  24.6 5.9 %collective-permute-done.refs_1_ = bf16[128,2048]{1,0:T(8,128)(2,1)S(1)} collective-permute-done((bf16[128,2048]{1,0:T(8,128)(2,1)S(1)}, bf16[128,2048]{1,0:T(8,128)(2,1)S(1)}, u32[]{:S(2)}, u32[]{:S(2)}) %collective-permute-start) | collective-permute-done | bytes 524320 | tf_op jit(solution)/shard_map/ppermute | solution.py:657
  30.5 3.3 collective-permute-done.1.refs_0_
  40.5 6.9 %collective-permute-done.2.refs_1_.refs_3_ = bf16[128,2048]{1,0:T(8,128)(2,1)S(1)} collective-permute-done((bf16[128,2048]{1,0:T(8,128)(2,1)}, bf16[128,2048]{1,0:T(8,128)(2,1)S(1)}, u32[]{:S(2)}, u32[]{:S(2)}) %collective-permute-start.2) | collective-permute-done | bytes 524320 | tf_op jit(solution)/shard_map/ppermute | solution.py:657
  52.8 10.4 %collective-permute-done.4.refs_1_.refs_5_ = bf16[128,2048]{1,0:T(8,128)(2,1)S(1)} collective-permute-done((bf16[128,2048]{1,0:T(8,128)(2,1)S(1)}, bf16[128,2048]{1,0:T(8,128)(2,1)S(1)}, u32[]{:S(2)}, u32[]{:S(2)}) %collective-permute-start.4) | collective-permute-done | bytes 524320 | tf_op jit(solution)/shard_map/ppermute | solution.py:657
  66.5 3.7 collective-permute-start.7
  71.4 4.5 %assemble.1 = (bf16[2048,1024]{1,0:T(8,128)(2,1)}, f32[1,2048]{1,0:T(1,128)}) custom-call(bf16[4,688,1024]{2,1,0:T(8,128)(2,1)} %bitcast.112), custom_call_target="tpu_custom_call" | custom-call | tf_op jit(solution)/shard_map/assemble/pallas_call | solution.py:110
  78.6 6.5 %collective-permute-done.6.refs_7_ = bf16[128,2048]{1,0:T(8,128)(2,1)} collective-permute-done((bf16[128,2048]{1,0:T(8,128)(2,1)S(1)}, bf16[128,2048]{1,0:T(8,128)(2,1)}, u32[]{:S(2)}, u32[]{:S(2)}) %collective-permute-start.6) | collective-permute-done | bytes 524320 | tf_op jit(solution)/shard_map/ppermute | solution.py:657
  85.1 12.7 %project.1 = (bf16[1024,2048]{1,0:T(8,128)(2,1)}, bf16[1024,512]{1,0:T(8,128)(2,1)}, f32[1024,512]{1,0:T(8,128)}, bf16[1024,512]{1,0:T(8,128)(2,1)}, f32[1024,512]{1,0:T(8,128)}, /*index=5*/bf16[8,160,128]{2,1,0:T(8,128)(2,1)}) custom-call(s32[8]{0:T(128)} %stack.55.slots_ref, bf16[2048,1024]{1,0:T(8,128)(2,1)} %get-tuple-element.38.w_in_ref.w_any, ...), custom_call_target="tpu_custom_call" | custom-call | flops 4294967296 | bytes 20971520 | tf_op jit(solution)/shard_map/project/pallas_call | solution.py:184
  97.8 3.4 all-to-all-start
  101.3 15.9 %all-to-all-done = bf16[8,1,160,128]{3,2,1,0:T(8,128)(2,1)S(1)} async-done(((bf16[8,1,160,128]{3,2,1,0:T(8,128)(2,1)}), bf16[8,1,160,128]{3,2,1,0:T(8,128)(2,1)S(1)}, u32[]{:S(2)}, u32[]{:S(2)}) %all-to-all-start) | async-done | bytes 327712 | tf_op jit(solution)/shard_map/all_to_all | solution.py:677
  121.6 2.6 collective-permute-start.8
  125.0 4.0 %all-to-all-start.1 = ((bf16[8,1,160,128]{3,2,1,0:T(8,128)(2,1)}), bf16[8,1,160,128]{3,2,1,0:T(8,128)(2,1)S(1)}, u32[]{:S(2)}, u32[]{:S(2)}) async-start(bf16[8,1,160,128]{3,2,1,0:T(8,128)(2,1)} %broadcast_in_dim.61), calls=%async_computation.1 | async-start | bytes 655360 | tf_op jit(solution)/shard_map/all_to_all | solution.py:680
  129.7 15.3 %all-to-all-done.1 = bf16[8,1,160,128]{3,2,1,0:T(8,128)(2,1)S(1)} async-done(((bf16[8,1,160,128]{3,2,1,0:T(8,128)(2,1)}), bf16[8,1,160,128]{3,2,1,0:T(8,128)(2,1)S(1)}, u32[]{:S(2)}, u32[]{:S(2)}) %all-to-all-start.1) | async-done | bytes 327712 | tf_op jit(solution)/shard_map/all_to_all | solution.py:680
  145.8 18.4 %scan_forward.1 = (bf16[1024,512]{1,0:T(8,128)(2,1)}, f32[1024,512]{1,0:T(8,128)}, bf16[16384,512]{1,0:T(8,128)(2,1)}) custom-call(bf16[8,160,128]{2,1,0:T(8,128)(2,1)} %bitcast.119, bf16[1024,512]{1,0:T(8,128)(2,1)} %get-tuple-element.41.act_ref, f32[1024,512]{1,0:T(8,128)} %get-tuple-element.42.gate_ref, f32[1024,8]{1,0:T(8,128)} %copy.80.refs_4_.mask_ref, ...), custom_call_target="tpu_custom_call" | custom-call | flops 1073741824 | bytes 67108864 | tf_op jit(solution)/shard_map/scan_forward/pallas_call | solution.py:281
  165.4 4.3 %convolution_convert_fusion._block = bf16[1024,2048]{1,0:T(8,128)(2,1)} fusion(bf16[1024,512]{1,0:T(8,128)(2,1)S(1)} %copy-done.11, bf16[512,2048]{1,0:T(8,128)(2,1)S(1)} %broadcast_select_fusion, bf16[512,2048]{1,0:T(8,128)(2,1)} %after.21, pred[]{:T(512)S(6)} %eq.80), kind=kOutput, calls=%fused_computation.2 | convolution fusion | flops 2150629376 | bytes 9437185 | tf_op jit(solution)/shard_map/dot_general | solution.py:24
  170.1 5.4 %fusion.13.d_branch_ref = f32[1024,512]{1,0:T(8,128)S(1)} fusion(bf16[1024,2048]{1,0:T(8,128)(2,1)} %all-gather.4.cloned.1.call-done, bf16[512,2048]{1,0:T(8,128)(2,1)} %copy-done.23, bf16[512,2048]{1,0:T(8,128)(2,1)} %after.21, pred[]{:T(512)S(6)} %eq.80), kind=kOutput, calls=%fused_computation.34 | convolution fusion | flops 2148532224 | bytes 10485761 | tf_op jit(solution)/shard_map/dot_general | solution.py:32
  185.6 41.9 %scan_backward.1 = (bf16[8,160,128]{2,1,0:T(8,128)(2,1)}, f32[1024,512]{1,0:T(8,128)}, f32[24,512]{1,0:T(8,128)}, f32[128,512]{1,0:T(8,128)}) custom-call(bf16[8,160,128]{2,1,0:T(8,128)(2,1)} %bitcast.120, bf16[1024,512]{1,0:T(8,128)(2,1)} %get-tuple-element.41.act_ref, f32[1024,512]{1,0:T(8,128)} %get-tuple-element.42.gate_ref, f32[1024,512]{1,0:T(8,128)} %copy-done.4, ...), custom_call_target="tpu_custom_call" | custom-call | flops 2147483648 | bytes 100663296 | tf_op jit(solution)/shard_map/scan_backward/pallas_call | solution.py:411
  228.6 19.1 %all_to_all.30 = bf16[8,1,160,128]{3,2,1,0:T(8,128)(2,1)S(1)} all-to-all(bf16[8,1,160,128]{3,2,1,0:T(8,128)(2,1)} %bitcast.124), channel_id=1, replica_groups=mesh['seq'=8,'fsdp'=4] {'seq'}, dimensions={0} | all-to-all | bytes 655360 | tf_op jit(solution)/shard_map/all_to_all | solution.py:677
  248.4 6.2 %convolution_convert_fusion.1.refs_3_ = bf16[512,2048]{1,0:T(8,128)(2,1)} fusion(bf16[1024,512]{1,0:T(8,128)(2,1)} %after.25, bf16[1024,2048]{1,0:T(8,128)(2,1)} %all-gather.4.cloned.1.call-done), kind=kOutput, calls=%fused_computation.3 | convolution fusion | flops 2148532224 | bytes 7340032 | tf_op jit(solution)/shard_map/dot_general | solution.py:28
  256.1 3.9 %all-to-all-start.3 = ((bf16[8,1,160,128]{3,2,1,0:T(8,128)(2,1)}), bf16[8,1,160,128]{3,2,1,0:T(8,128)(2,1)S(1)}, u32[]{:S(2)}, u32[]{:S(2)}) async-start(bf16[8,1,160,128]{3,2,1,0:T(8,128)(2,1)} %broadcast_in_dim.63), calls=%async_computation.4 | async-start | bytes 655360 | tf_op jit(solution)/shard_map/all_to_all | solution.py:680
  263.0 7.4 %all-to-all-done.3 = bf16[8,1,160,128]{3,2,1,0:T(8,128)(2,1)S(1)} async-done(((bf16[8,1,160,128]{3,2,1,0:T(8,128)(2,1)}), bf16[8,1,160,128]{3,2,1,0:T(8,128)(2,1)S(1)}, u32[]{:S(2)}, u32[]{:S(2)}) %all-to-all-start.3) | async-done | bytes 327712 | tf_op jit(solution)/shard_map/all_to_all | solution.py:680
  271.2 21.9 %tail.1 = (bf16[128,2048]{1,0:T(8,128)(2,1)}, bf16[128,2048]{1,0:T(8,128)(2,1)}, bf16[128,2048]{1,0:T(8,128)(2,1)}, bf16[128,2048]{1,0:T(8,128)(2,1)}, bf16[128,...) custom-call(s32[2]{0:T(128)} %pad_add_fusion.where_ref, ...), custom_call_target="tpu_custom_call" | custom-call | flops 8589934592 | bytes 33554432 | tf_op jit(solution)/shard_map/tail/pallas_call | solution.py:603
  295.7 3.5 all-to-all-start.4
  301.2 12.1 %collective-permute-done.12 = bf16[128,2048]{1,0:T(8,128)(2,1)S(1)} collective-permute-done((bf16[128,2048]{1,0:T(8,128)(2,1)S(1)}, bf16[128,2048]{1,0:T(8,128)(2,1)S(1)}, u32[]{:S(2)}, u32[]{:S(2)}) %collective-permute-start.12) | collective-permute-done | bytes 524320 | tf_op jit(solution)/shard_map/ppermute | solution.py:784
  317.5 5.6 %collective-permute-done.14 = bf16[128,2048]{1,0:T(8,128)(2,1)S(1)} collective-permute-done((bf16[128,2048]{1,0:T(8,128)(2,1)S(1)}, bf16[128,2048]{1,0:T(8,128)(2,1)S(1)}, u32[]{:S(2)}, u32[]{:S(2)}) %collective-permute-start.14) | collective-permute-done | bytes 524320 | tf_op jit(solution)/shard_map/ppermute | solution.py:784
  332.1 11.8 %collective-permute-done.16 = bf16[128,2048]{1,0:T(8,128)(2,1)} collective-permute-done((bf16[128,2048]{1,0:T(8,128)(2,1)}, bf16[128,2048]{1,0:T(8,128)(2,1)}, u32[]{:S(2)}, u32[]{:S(2)}) %collective-permute-start.16) | collective-permute-done | bytes 524320 | tf_op jit(solution)/shard_map/ppermute | solution.py:784
  346.2 6.2 %all-to-all-start.5 = ((bf16[8,72,512]{2,1,0:T(8,128)(2,1)}), bf16[8,72,512]{2,1,0:T(8,128)(2,1)S(1)}, u32[]{:S(2)}, u32[]{:S(2)}) async-start(bf16[8,72,512]{2,1,0:T(8,128)(2,1)} %bitcast.129), calls=%async_computation.8 | async-start | bytes 1179648 | tf_op jit(solution)/shard_map/all_to_all | solution.py:786
  352.4 3.3 reduce-scatter.11.cloned.1.call-done
  362.6 5.6 %all-to-all-done.5.refs_1_ = bf16[8,72,512]{2,1,0:T(8,128)(2,1)S(1)} async-done(((bf16[8,72,512]{2,1,0:T(8,128)(2,1)}), bf16[8,72,512]{2,1,0:T(8,128)(2,1)S(1)}, u32[]{:S(2)}, u32[]{:S(2)}) %all-to-all-start.5) | async-done | bytes 589856 | tf_op jit(solution)/shard_map/all_to_all | solution.py:786
  373.8 2.8 fusion.10
  (231 shorter events, 88.0 us)
Async XLA Ops:
  7.2 64.2 %all-gather.6.cloned.1.call-start = ((), (), s32[]{:S(2)}) async-start(), calls=%async_computation.15 | async-start | bytes 7045120 | tf_op jit(solution)/shard_map/all_gather | solution.py:739
  15.6 154.5 %all-gather.4.cloned.1.call-start = ((), (), s32[]{:S(2)}) async-start(), calls=%async_computation.11 | async-start | bytes 4718592 | tf_op jit(solution)/shard_map/all_gather | solution.py:743
  15.6 14.9 %collective-permute-start = (bf16[128,2048]{1,0:T(8,128)(2,1)S(1)}, bf16[128,2048]{1,0:T(8,128)(2,1)S(1)}, u32[]{:S(2)}, u32[]{:S(2)}) collective-permute-start(bf16[128,2048]{1,0:T(8,128)(2,1)S(1)} %bitcast.116), channel_id=1, source_target_pairs={{0,4},{4,0},{8,12},{12,8},{16,20},{20,16},{24,28},{28,24},{1,5},{5... | collective-permute-start | bytes 1572872 | tf_op jit(solution)/shard_map/ppermute | solution.py:657
  18.6 15.2 %collective-permute-start.1 = (bf16[128,2048]{1,0:T(8,128)(2,1)S(1)}, bf16[128,2048]{1,0:T(8,128)(2,1)S(1)}, u32[]{:S(2)}, u32[]{:S(2)}) collective-permute-start(bf16[128,2048]{1,0:T(8,128)(2,1)S(1)} %bitcast.117), channel_id=1, source_target_pairs={{0,8},{4,12},{8,16},{12,20},{16,24},{20,28},{24,0},{28,4},{1,9},{5... | collective-permute-start | bytes 1572872 | tf_op jit(solution)/shard_map/ppermute | solution.py:663
  34.7 12.8 %collective-permute-start.2 = (bf16[128,2048]{1,0:T(8,128)(2,1)}, bf16[128,2048]{1,0:T(8,128)(2,1)S(1)}, u32[]{:S(2)}, u32[]{:S(2)}) collective-permute-start(bf16[128,2048]{1,0:T(8,128)(2,1)} %after.16.refs_2_), channel_id=1, source_target_pairs={{0,4},{4,0},{8,12},{12,8},{16,20},{20,16},{24,28},{28,24},{1,5},{5... | collective-permute-start | bytes 1572872 | tf_op jit(solution)/shard_map/ppermute | solution.py:657
  35.2 14.5 %collective-permute-start.3 = (bf16[128,2048]{1,0:T(8,128)(2,1)}, bf16[128,2048]{1,0:T(8,128)(2,1)S(1)}, u32[]{:S(2)}, u32[]{:S(2)}) collective-permute-start(bf16[128,2048]{1,0:T(8,128)(2,1)} %after.16.refs_2_), channel_id=1, source_target_pairs={{0,8},{4,12},{8,16},{12,20},{16,24},{20,28},{24,0},{28,4},{1,9},{5... | collective-permute-start | bytes 1572872 | tf_op jit(solution)/shard_map/ppermute | solution.py:663
  51.6 11.6 %collective-permute-start.4 = (bf16[128,2048]{1,0:T(8,128)(2,1)S(1)}, bf16[128,2048]{1,0:T(8,128)(2,1)S(1)}, u32[]{:S(2)}, u32[]{:S(2)}) collective-permute-start(bf16[128,2048]{1,0:T(8,128)(2,1)S(1)} %copy-done.25), channel_id=1, source_target_pairs={{0,4},{4,0},{8,12},{12,8},{16,20},{20,16},{24,28},{28,24},{1,5},{5... | collective-permute-start | bytes 1572872 | tf_op jit(solution)/shard_map/ppermute | solution.py:657
  52.8 12.9 %collective-permute-start.5 = (bf16[128,2048]{1,0:T(8,128)(2,1)S(1)}, bf16[128,2048]{1,0:T(8,128)(2,1)S(1)}, u32[]{:S(2)}, u32[]{:S(2)}) collective-permute-start(bf16[128,2048]{1,0:T(8,128)(2,1)S(1)} %copy-done.25), channel_id=1, source_target_pairs={{0,8},{4,12},{8,16},{12,20},{16,24},{20,28},{24,0},{28,4},{1,9},{5... | collective-permute-start | bytes 1572872 | tf_op jit(solution)/shard_map/ppermute | solution.py:663
  66.5 51.4 %collective-permute-start.7 = (bf16[512,2048]{1,0:T(8,128)(2,1)}, bf16[512,2048]{1,0:T(8,128)(2,1)S(1)}, u32[]{:S(2)}, u32[]{:S(2)}) collective-permute-start(bf16[512,2048]{1,0:T(8,128)(2,1)} %after.19), channel_id=1, source_target_pairs={{0,2},{4,6},{9,11},{13,15},{18,16},{22,20},{27,25},{31,29}} | collective-permute-start | bytes 6291464 | tf_op jit(solution)/shard_map/ppermute | solution.py:664
  70.2 15.0 %collective-permute-start.6 = (bf16[128,2048]{1,0:T(8,128)(2,1)S(1)}, bf16[128,2048]{1,0:T(8,128)(2,1)}, u32[]{:S(2)}, u32[]{:S(2)}) collective-permute-start(bf16[128,2048]{1,0:T(8,128)(2,1)S(1)} %copy-done.22), channel_id=1, source_target_pairs={{0,4},{4,0},{8,12},{12,8},{16,20},{20,16},{24,28},{28,24},{1,5},{5... | collective-permute-start | bytes 1572872 | tf_op jit(solution)/shard_map/ppermute | solution.py:657
  97.8 19.3 %all-to-all-start = ((bf16[8,1,160,128]{3,2,1,0:T(8,128)(2,1)}), bf16[8,1,160,128]{3,2,1,0:T(8,128)(2,1)S(1)}, u32[]{:S(2)}, u32[]{:S(2)}) async-start(bf16[8,1,160,128]{3,2,1,0:T(8,128)(2,1)} %bitcast.131), calls=%async_computation | async-start | bytes 655360 | tf_op jit(solution)/shard_map/all_to_all | solution.py:677
  121.6 48.1 %copy-start.23 = (bf16[512,2048]{1,0:T(8,128)(2,1)}, bf16[512,2048]{1,0:T(8,128)(2,1)S(1)}, u32[]{:S(2)}) copy-start(bf16[512,2048]{1,0:T(8,128)(2,1)S(1)} %broadcast_select_fusion) | copy-start | bytes 6291460
  121.6 42.6 %collective-permute-start.8 = (bf16[512,2048]{1,0:T(8,128)(2,1)S(1)}, bf16[512,2048]{1,0:T(8,128)(2,1)}, u32[]{:S(2)}, u32[]{:S(2)}) collective-permute-start(bf16[512,2048]{1,0:T(8,128)(2,1)S(1)} %broadcast_select_fusion), channel_id=1, source_target_pairs={{0,1},{2,3},{4,5},{6,7},{9,8},{11,10},{13,12},{15,14},{18,19},{16,... | collective-permute-start | bytes 6291464 | tf_op jit(solution)/shard_map/ppermute | solution.py:668
  125.0 20.0 %all-to-all-start.1 = ((bf16[8,1,160,128]{3,2,1,0:T(8,128)(2,1)}), bf16[8,1,160,128]{3,2,1,0:T(8,128)(2,1)S(1)}, u32[]{:S(2)}, u32[]{:S(2)}) async-start(bf16[8,1,160,128]{3,2,1,0:T(8,128)(2,1)} %broadcast_in_dim.61), calls=%async_computation.1 | async-start | bytes 655360 | tf_op jit(solution)/shard_map/all_to_all | solution.py:680
  129.0 141.5 %reduce-scatter.5.cloned.1.call-start = ((), (), s32[]{:S(2)}) async-start(), calls=%async_computation.10 | async-start | bytes 4718592 | tf_op jit(solution)/shard_map/reduce_scatter | solution.py:751
  169.8 156.8 %reduce-scatter.7.cloned.1.call-start = ((), (), s32[]{:S(2)}) async-start(), calls=%async_computation.12 | async-start | bytes 2621440 | tf_op jit(solution)/shard_map/reduce_scatter | solution.py:771
  182.3 45.2 %collective-permute-start.9 = (bf16[8,64,512]{2,1,0:T(8,128)(2,1)S(1)}, bf16[8,64,512]{2,1,0:T(8,128)(2,1)S(1)}, u32[]{:S(2)}, u32[]{:S(2)}) collective-permute-start(bf16[8,64,512]{2,1,0:T(8,128)(2,1)S(1)} %get-tuple-element.120), channel_id=1, source_target_pairs={{0,1},{1,0},{2,3},{3,2},{4,5},{5,4},{6,7},{7,6},{8,9},{9,8},{10,11... | collective-permute-start | bytes 1572872 | tf_op jit(solution)/shard_map/ppermute | solution.py:694
  183.9 43.6 %collective-permute-start.10 = (bf16[8,64,512]{2,1,0:T(8,128)(2,1)S(1)}, bf16[8,64,512]{2,1,0:T(8,128)(2,1)S(1)}, u32[]{:S(2)}, u32[]{:S(2)}) collective-permute-start(bf16[8,64,512]{2,1,0:T(8,128)(2,1)S(1)} %get-tuple-element.119), channel_id=1, source_target_pairs={{0,2},{1,3},{2,0},{3,1},{4,6},{5,7},{6,4},{7,5},{8,10},{9,11},{10,... | collective-permute-start | bytes 1572872 | tf_op jit(solution)/shard_map/ppermute | solution.py:694
  185.6 42.0 %collective-permute-start.11 = (bf16[8,64,512]{2,1,0:T(8,128)(2,1)S(1)}, bf16[8,64,512]{2,1,0:T(8,128)(2,1)S(1)}, u32[]{:S(2)}, u32[]{:S(2)}) collective-permute-start(bf16[8,64,512]{2,1,0:T(8,128)(2,1)S(1)} %get-tuple-element.118), channel_id=1, source_target_pairs={{0,3},{1,2},{2,1},{3,0},{4,7},{5,6},{6,5},{7,4},{8,11},{9,10},{10,... | collective-permute-start | bytes 1572872 | tf_op jit(solution)/shard_map/ppermute | solution.py:694
  256.1 14.3 %all-to-all-start.3 = ((bf16[8,1,160,128]{3,2,1,0:T(8,128)(2,1)}), bf16[8,1,160,128]{3,2,1,0:T(8,128)(2,1)S(1)}, u32[]{:S(2)}, u32[]{:S(2)}) async-start(bf16[8,1,160,128]{3,2,1,0:T(8,128)(2,1)} %broadcast_in_dim.63), calls=%async_computation.4 | async-start | bytes 655360 | tf_op jit(solution)/shard_map/all_to_all | solution.py:680
  260.0 86.2 %reduce-scatter.9.cloned.1.call-start = ((), (), s32[]{:S(2)}) async-start(), calls=%async_computation.13 | async-start | bytes 2949120 | tf_op jit(solution)/shard_map/reduce_scatter | solution.py:785
  293.1 20.1 %copy-start.34 = (bf16[128,2048]{1,0:T(8,128)(2,1)S(1)}, bf16[128,2048]{1,0:T(8,128)(2,1)}, u32[]{:S(2)}) copy-start(bf16[128,2048]{1,0:T(8,128)(2,1)} %get-tuple-element.51) | copy-start | bytes 1572868
  294.1 19.1 %collective-permute-start.12 = (bf16[128,2048]{1,0:T(8,128)(2,1)S(1)}, bf16[128,2048]{1,0:T(8,128)(2,1)S(1)}, u32[]{:S(2)}, u32[]{:S(2)}) collective-permute-start(bf16[128,2048]{1,0:T(8,128)(2,1)S(1)} %copy-done.46), channel_id=1, source_target_pairs={{0,4},{4,0},{8,12},{12,8},{16,20},{20,16},{24,28},{28,24},{1,5},{5... | collective-permute-start | bytes 1572872 | tf_op jit(solution)/shard_map/ppermute | solution.py:784
  295.7 19.7 %all-to-all-start.4 = ((bf16[8,64,512]{2,1,0:T(8,128)(2,1)}), bf16[8,64,512]{2,1,0:T(8,128)(2,1)S(1)}, u32[]{:S(2)}, u32[]{:S(2)}) async-start(bf16[8,64,512]{2,1,0:T(8,128)(2,1)} %add_convert_fusion.3.refs_2_), calls=%async_computation.5 | async-start | bytes 1048576 | tf_op jit(solution)/shard_map/all_to_all | solution.py:761
  299.2 56.5 %reduce-scatter.11.cloned.1.call-start = ((), (), s32[]{:S(2)}) async-start(), calls=%async_computation.14 | async-start | bytes 819200 | tf_op jit(solution)/shard_map/reduce_scatter | solution.py:817
  299.2 23.8 %collective-permute-start.14 = (bf16[128,2048]{1,0:T(8,128)(2,1)S(1)}, bf16[128,2048]{1,0:T(8,128)(2,1)S(1)}, u32[]{:S(2)}, u32[]{:S(2)}) collective-permute-start(bf16[128,2048]{1,0:T(8,128)(2,1)S(1)} %copy-done.45), channel_id=1, source_target_pairs={{0,4},{4,0},{8,12},{12,8},{16,20},{20,16},{24,28},{28,24},{1,5},{5... | collective-permute-start | bytes 1572872 | tf_op jit(solution)/shard_map/ppermute | solution.py:784
  314.2 11.4 %collective-permute-start.13 = (bf16[128,2048]{1,0:T(8,128)(2,1)}, bf16[128,2048]{1,0:T(8,128)(2,1)S(1)}, u32[]{:S(2)}, u32[]{:S(2)}) collective-permute-start(bf16[128,2048]{1,0:T(8,128)(2,1)} %after.27), channel_id=1, source_target_pairs={{0,8},{4,12},{8,16},{12,20},{16,24},{20,28},{24,0},{28,4},{1,9},{5... | collective-permute-start | bytes 1572872 | tf_op jit(solution)/shard_map/ppermute | solution.py:794
  328.9 15.0 %collective-permute-start.16 = (bf16[128,2048]{1,0:T(8,128)(2,1)}, bf16[128,2048]{1,0:T(8,128)(2,1)}, u32[]{:S(2)}, u32[]{:S(2)}) collective-permute-start(bf16[128,2048]{1,0:T(8,128)(2,1)} %get-tuple-element.56), channel_id=1, source_target_pairs={{0,4},{4,0},{8,12},{12,8},{16,20},{20,16},{24,28},{28,24},{1,5},{5... | collective-permute-start | bytes 1572872 | tf_op jit(solution)/shard_map/ppermute | solution.py:784
  330.4 13.5 %collective-permute-start.15 = (bf16[128,2048]{1,0:T(8,128)(2,1)S(1)}, bf16[128,2048]{1,0:T(8,128)(2,1)}, u32[]{:S(2)}, u32[]{:S(2)}) collective-permute-start(bf16[128,2048]{1,0:T(8,128)(2,1)S(1)} %copy-done.7), channel_id=1, source_target_pairs={{0,8},{4,12},{8,16},{12,20},{16,24},{20,28},{24,0},{28,4},{1,9},{5... | collective-permute-start | bytes 1572872 | tf_op jit(solution)/shard_map/ppermute | solution.py:794
  331.5 37.6 %collective-permute-start.18 = (bf16[128,2048]{1,0:T(8,128)(2,1)}, bf16[128,2048]{1,0:T(8,128)(2,1)S(1)}, u32[]{:S(2)}, u32[]{:S(2)}) collective-permute-start(bf16[128,2048]{1,0:T(8,128)(2,1)} %get-tuple-element.59), channel_id=1, source_target_pairs={{0,4},{4,0},{8,12},{12,8},{16,20},{20,16},{24,28},{28,24},{1,5},{5... | collective-permute-start | bytes 1572872 | tf_op jit(solution)/shard_map/ppermute | solution.py:784
  346.2 23.0 %collective-permute-start.17 = (bf16[128,2048]{1,0:T(8,128)(2,1)}, bf16[128,2048]{1,0:T(8,128)(2,1)}, u32[]{:S(2)}, u32[]{:S(2)}) collective-permute-start(bf16[128,2048]{1,0:T(8,128)(2,1)} %after.29), channel_id=1, source_target_pairs={{0,8},{4,12},{8,16},{12,20},{16,24},{20,28},{24,0},{28,4},{1,9},{5... | collective-permute-start | bytes 1572872 | tf_op jit(solution)/shard_map/ppermute | solution.py:794
  346.2 22.0 %all-to-all-start.5 = ((bf16[8,72,512]{2,1,0:T(8,128)(2,1)}), bf16[8,72,512]{2,1,0:T(8,128)(2,1)S(1)}, u32[]{:S(2)}, u32[]{:S(2)}) async-start(bf16[8,72,512]{2,1,0:T(8,128)(2,1)} %bitcast.129), calls=%async_computation.8 | async-start | bytes 1179648 | tf_op jit(solution)/shard_map/all_to_all | solution.py:786
  (47 other events, 158.6 us)
Sparse Core Ops, SparseCore 0:
  15.7 45.3 all-gather.5
  63.2 81.0 all-gather.3
  169.9 91.1 reduce-scatter.4
  264.2 30.3 reduce-scatter.6
  297.0 33.0 reduce-scatter.8
  333.2 22.4 reduce-scatter.10

commit v3 on v2

--- a/solution.py
+++ b/solution.py
@@ -714,7 +714,7 @@
     lanes = min(2 * width, deep)
     small = jnp.concatenate(
         [
-            dt_weight.T, a_log.T, conv_weight.T, conv_bias[None], dt_bias[None], skip_weight[None],
+            dt_weight.T, a_log.T, conv_weight.T, jnp.stack([conv_bias, dt_bias, skip_weight]),
             jnp.zeros((MIXED - DT_RANK - STATE - CONV - 3, held), BF16),
         ],
         axis=0,

time: 385 us -> 385 us (level)
  no operation moved by 1% of the time
where the time goes in v3:
time: 385 us; the launch traced here: 383 us
  waiting for transfers between devices  117 us (30%)
  Pallas kernels  99.4 us (26%)
  starting transfers between devices  45.1 us (12%)
  local copies, waits for them, and re-layouts  43 us (11%)
  other arithmetic  26.3 us (7%)
  blocking collectives  19.1 us (5%)
  matrix products  18.3 us (5%)
  between operations  14.8 us (4%)
    pallas_call x1, Pallas kernels, scan_backward(): pl.pallas_call(backward_kernel, grid=(blocks,), in_specs=[mixed_spec, row...  41.9 us
    ppermute x4, waiting for transfers between devices, gather_all(): swapped = lax.ppermute(part, 'seq', swap)  29.7 us
    ppermute x4, waiting for transfers between devices, local(): swapped = [lax.ppermute(block, 'seq', swap) for block in theirs]  29.4 us
    all_to_all x2, waiting for transfers between devices, sum_over_seq(): lax.all_to_all(copies, 'seq', split_axis=0, concat_axis=0, tiled=True)  22.8 us
    pallas_call x1, Pallas kernels, tail(): pl.pallas_call(tail_kernel, grid=(blocks,), in_specs=[pl.BlockSpec(memory...  21.9 us
    all_to_all x1, blocking collectives, sum_over_seq(): lax.all_to_all(shares, 'seq', split_axis=0, concat_axis=0, tiled=True)  19.1 us
    pallas_call x1, Pallas kernels, scan_forward(): pl.pallas_call(forward_kernel, grid=(count // BLOCK,), in_specs=[pl.Block...  18.4 us
    unnamed x102, local copies, waits for them, and re-layouts  17 us
  transfers between devices with their start and end apart: 30, of which 16 were waited for; matrix products, arithmetic and copies ran while one was open for 15% of the time, Pallas kernels for 26%

profile of v3, /device:TPU:0, one launch (start us, length us, event | category | flops | bytes accessed | tf_op | source)
XLA Modules:
  0.0 383.5 jit_solution(16414365736695744632)
XLA Ops:
  15.6 3.0 collective-permute-start
  20.6 3.2 constant_dynamic-slice_fusion.1.refs_3_.refs_0_
  24.6 5.9 %collective-permute-done.refs_1_ = bf16[128,2048]{1,0:T(8,128)(2,1)S(1)} collective-permute-done((bf16[128,2048]{1,0:T(8,128)(2,1)S(1)}, bf16[128,2048]{1,0:T(8,128)(2,1)S(1)}, u32[]{:S(2)}, u32[]{:S(2)}) %collective-permute-start) | collective-permute-done | bytes 524320 | tf_op jit(solution)/shard_map/ppermute | solution.py:657
  30.5 3.3 collective-permute-done.1.refs_0_
  40.5 6.9 %collective-permute-done.2.refs_1_.refs_3_ = bf16[128,2048]{1,0:T(8,128)(2,1)S(1)} collective-permute-done((bf16[128,2048]{1,0:T(8,128)(2,1)}, bf16[128,2048]{1,0:T(8,128)(2,1)S(1)}, u32[]{:S(2)}, u32[]{:S(2)}) %collective-permute-start.2) | collective-permute-done | bytes 524320 | tf_op jit(solution)/shard_map/ppermute | solution.py:657
  52.8 10.4 %collective-permute-done.4.refs_1_.refs_5_ = bf16[128,2048]{1,0:T(8,128)(2,1)S(1)} collective-permute-done((bf16[128,2048]{1,0:T(8,128)(2,1)S(1)}, bf16[128,2048]{1,0:T(8,128)(2,1)S(1)}, u32[]{:S(2)}, u32[]{:S(2)}) %collective-permute-start.4) | collective-permute-done | bytes 524320 | tf_op jit(solution)/shard_map/ppermute | solution.py:657
  66.5 3.7 collective-permute-start.7
  71.4 4.5 %assemble.1 = (bf16[2048,1024]{1,0:T(8,128)(2,1)}, f32[1,2048]{1,0:T(1,128)}) custom-call(bf16[4,688,1024]{2,1,0:T(8,128)(2,1)} %bitcast.112), custom_call_target="tpu_custom_call" | custom-call | tf_op jit(solution)/shard_map/assemble/pallas_call | solution.py:110
  78.6 6.5 %collective-permute-done.6.refs_7_ = bf16[128,2048]{1,0:T(8,128)(2,1)} collective-permute-done((bf16[128,2048]{1,0:T(8,128)(2,1)S(1)}, bf16[128,2048]{1,0:T(8,128)(2,1)}, u32[]{:S(2)}, u32[]{:S(2)}) %collective-permute-start.6) | collective-permute-done | bytes 524320 | tf_op jit(solution)/shard_map/ppermute | solution.py:657
  85.1 12.7 %project.1 = (bf16[1024,2048]{1,0:T(8,128)(2,1)}, bf16[1024,512]{1,0:T(8,128)(2,1)}, f32[1024,512]{1,0:T(8,128)}, bf16[1024,512]{1,0:T(8,128)(2,1)}, f32[1024,512]{1,0:T(8,128)}, /*index=5*/bf16[8,160,128]{2,1,0:T(8,128)(2,1)}) custom-call(s32[8]{0:T(128)} %stack.64.slots_ref, bf16[2048,1024]{1,0:T(8,128)(2,1)} %get-tuple-element.38.w_in_ref.w_any, ...), custom_call_target="tpu_custom_call" | custom-call | flops 4294967296 | bytes 20971520 | tf_op jit(solution)/shard_map/project/pallas_call | solution.py:184
  97.8 3.4 all-to-all-start
  101.3 15.9 %all-to-all-done = bf16[8,1,160,128]{3,2,1,0:T(8,128)(2,1)S(1)} async-done(((bf16[8,1,160,128]{3,2,1,0:T(8,128)(2,1)}), bf16[8,1,160,128]{3,2,1,0:T(8,128)(2,1)S(1)}, u32[]{:S(2)}, u32[]{:S(2)}) %all-to-all-start) | async-done | bytes 327712 | tf_op jit(solution)/shard_map/all_to_all | solution.py:677
  121.6 2.6 collective-permute-start.8
  125.0 4.0 %all-to-all-start.1 = ((bf16[8,1,160,128]{3,2,1,0:T(8,128)(2,1)}), bf16[8,1,160,128]{3,2,1,0:T(8,128)(2,1)S(1)}, u32[]{:S(2)}, u32[]{:S(2)}) async-start(bf16[8,1,160,128]{3,2,1,0:T(8,128)(2,1)} %broadcast_in_dim.28), calls=%async_computation.1 | async-start | bytes 655360 | tf_op jit(solution)/shard_map/all_to_all | solution.py:680
  129.7 15.3 %all-to-all-done.1 = bf16[8,1,160,128]{3,2,1,0:T(8,128)(2,1)S(1)} async-done(((bf16[8,1,160,128]{3,2,1,0:T(8,128)(2,1)}), bf16[8,1,160,128]{3,2,1,0:T(8,128)(2,1)S(1)}, u32[]{:S(2)}, u32[]{:S(2)}) %all-to-all-start.1) | async-done | bytes 327712 | tf_op jit(solution)/shard_map/all_to_all | solution.py:680
  145.8 18.4 %scan_forward.1 = (bf16[1024,512]{1,0:T(8,128)(2,1)}, f32[1024,512]{1,0:T(8,128)}, bf16[16384,512]{1,0:T(8,128)(2,1)}) custom-call(bf16[8,160,128]{2,1,0:T(8,128)(2,1)} %bitcast.119, bf16[1024,512]{1,0:T(8,128)(2,1)} %get-tuple-element.41.act_ref, f32[1024,512]{1,0:T(8,128)} %get-tuple-element.42.gate_ref, f32[1024,8]{1,0:T(8,128)} %copy.80.refs_4_.mask_ref, ...), custom_call_target="tpu_custom_call" | custom-call | flops 1073741824 | bytes 67108864 | tf_op jit(solution)/shard_map/scan_forward/pallas_call | solution.py:281
  165.4 4.3 %convolution_convert_fusion._block = bf16[1024,2048]{1,0:T(8,128)(2,1)} fusion(bf16[1024,512]{1,0:T(8,128)(2,1)S(1)} %copy-done.11, bf16[512,2048]{1,0:T(8,128)(2,1)S(1)} %broadcast_select_fusion, bf16[512,2048]{1,0:T(8,128)(2,1)} %after.21, pred[]{:T(512)S(6)} %eq.80), kind=kOutput, calls=%fused_computation.2 | convolution fusion | flops 2150629376 | bytes 9437185 | tf_op jit(solution)/shard_map/dot_general | solution.py:24
  170.1 5.4 %fusion.13.d_branch_ref = f32[1024,512]{1,0:T(8,128)S(1)} fusion(bf16[1024,2048]{1,0:T(8,128)(2,1)} %all-gather.4.cloned.1.call-done, bf16[512,2048]{1,0:T(8,128)(2,1)} %copy-done.23, bf16[512,2048]{1,0:T(8,128)(2,1)} %after.21, pred[]{:T(512)S(6)} %eq.80), kind=kOutput, calls=%fused_computation.34 | convolution fusion | flops 2148532224 | bytes 10485761 | tf_op jit(solution)/shard_map/dot_general | solution.py:32
  185.6 41.9 %scan_backward.1 = (bf16[8,160,128]{2,1,0:T(8,128)(2,1)}, f32[1024,512]{1,0:T(8,128)}, f32[24,512]{1,0:T(8,128)}, f32[128,512]{1,0:T(8,128)}) custom-call(bf16[8,160,128]{2,1,0:T(8,128)(2,1)} %bitcast.120, bf16[1024,512]{1,0:T(8,128)(2,1)} %get-tuple-element.41.act_ref, f32[1024,512]{1,0:T(8,128)} %get-tuple-element.42.gate_ref, f32[1024,512]{1,0:T(8,128)} %copy-done.4, ...), custom_call_target="tpu_custom_call" | custom-call | flops 2147483648 | bytes 100663296 | tf_op jit(solution)/shard_map/scan_backward/pallas_call | solution.py:411
  228.6 19.1 %all_to_all.30 = bf16[8,1,160,128]{3,2,1,0:T(8,128)(2,1)S(1)} all-to-all(bf16[8,1,160,128]{3,2,1,0:T(8,128)(2,1)} %bitcast.124), channel_id=1, replica_groups=mesh['seq'=8,'fsdp'=4] {'seq'}, dimensions={0} | all-to-all | bytes 655360 | tf_op jit(solution)/shard_map/all_to_all | solution.py:677
  248.4 6.2 %convolution_convert_fusion.1.refs_3_ = bf16[512,2048]{1,0:T(8,128)(2,1)} fusion(bf16[1024,512]{1,0:T(8,128)(2,1)} %after.25, bf16[1024,2048]{1,0:T(8,128)(2,1)} %all-gather.4.cloned.1.call-done), kind=kOutput, calls=%fused_computation.3 | convolution fusion | flops 2148532224 | bytes 7340032 | tf_op jit(solution)/shard_map/dot_general | solution.py:28
  256.1 3.9 %all-to-all-start.3 = ((bf16[8,1,160,128]{3,2,1,0:T(8,128)(2,1)}), bf16[8,1,160,128]{3,2,1,0:T(8,128)(2,1)S(1)}, u32[]{:S(2)}, u32[]{:S(2)}) async-start(bf16[8,1,160,128]{3,2,1,0:T(8,128)(2,1)} %broadcast_in_dim.51), calls=%async_computation.4 | async-start | bytes 655360 | tf_op jit(solution)/shard_map/all_to_all | solution.py:680
  263.0 7.4 %all-to-all-done.3 = bf16[8,1,160,128]{3,2,1,0:T(8,128)(2,1)S(1)} async-done(((bf16[8,1,160,128]{3,2,1,0:T(8,128)(2,1)}), bf16[8,1,160,128]{3,2,1,0:T(8,128)(2,1)S(1)}, u32[]{:S(2)}, u32[]{:S(2)}) %all-to-all-start.3) | async-done | bytes 327712 | tf_op jit(solution)/shard_map/all_to_all | solution.py:680
  271.2 21.9 %tail.1 = (bf16[128,2048]{1,0:T(8,128)(2,1)}, bf16[128,2048]{1,0:T(8,128)(2,1)}, bf16[128,2048]{1,0:T(8,128)(2,1)}, bf16[128,2048]{1,0:T(8,128)(2,1)}, bf16[128,...) custom-call(s32[2]{0:T(128)} %pad_add_fusion.where_ref, ...), custom_call_target="tpu_custom_call" | custom-call | flops 8589934592 | bytes 33554432 | tf_op jit(solution)/shard_map/tail/pallas_call | solution.py:603
  295.7 3.5 all-to-all-start.4
  301.2 12.1 %collective-permute-done.12 = bf16[128,2048]{1,0:T(8,128)(2,1)S(1)} collective-permute-done((bf16[128,2048]{1,0:T(8,128)(2,1)S(1)}, bf16[128,2048]{1,0:T(8,128)(2,1)S(1)}, u32[]{:S(2)}, u32[]{:S(2)}) %collective-permute-start.12) | collective-permute-done | bytes 524320 | tf_op jit(solution)/shard_map/ppermute | solution.py:784
  317.5 5.6 %collective-permute-done.14 = bf16[128,2048]{1,0:T(8,128)(2,1)S(1)} collective-permute-done((bf16[128,2048]{1,0:T(8,128)(2,1)S(1)}, bf16[128,2048]{1,0:T(8,128)(2,1)S(1)}, u32[]{:S(2)}, u32[]{:S(2)}) %collective-permute-start.14) | collective-permute-done | bytes 524320 | tf_op jit(solution)/shard_map/ppermute | solution.py:784
  332.1 11.8 %collective-permute-done.16 = bf16[128,2048]{1,0:T(8,128)(2,1)} collective-permute-done((bf16[128,2048]{1,0:T(8,128)(2,1)}, bf16[128,2048]{1,0:T(8,128)(2,1)}, u32[]{:S(2)}, u32[]{:S(2)}) %collective-permute-start.16) | collective-permute-done | bytes 524320 | tf_op jit(solution)/shard_map/ppermute | solution.py:784
  346.2 6.2 %all-to-all-start.5 = ((bf16[8,72,512]{2,1,0:T(8,128)(2,1)}), bf16[8,72,512]{2,1,0:T(8,128)(2,1)S(1)}, u32[]{:S(2)}, u32[]{:S(2)}) async-start(bf16[8,72,512]{2,1,0:T(8,128)(2,1)} %bitcast.129), calls=%async_computation.8 | async-start | bytes 1179648 | tf_op jit(solution)/shard_map/all_to_all | solution.py:786
  352.4 3.3 reduce-scatter.11.cloned.1.call-done
  362.6 5.6 %all-to-all-done.5.refs_1_ = bf16[8,72,512]{2,1,0:T(8,128)(2,1)S(1)} async-done(((bf16[8,72,512]{2,1,0:T(8,128)(2,1)}), bf16[8,72,512]{2,1,0:T(8,128)(2,1)S(1)}, u32[]{:S(2)}, u32[]{:S(2)}) %all-to-all-start.5) | async-done | bytes 589856 | tf_op jit(solution)/shard_map/all_to_all | solution.py:786
  373.8 2.8 fusion.10
  (231 shorter events, 88.0 us)
Async XLA Ops:
  7.2 64.2 %all-gather.6.cloned.1.call-start = ((), (), s32[]{:S(2)}) async-start(), calls=%async_computation.15 | async-start | bytes 7045120 | tf_op jit(solution)/shard_map/all_gather | solution.py:739
  15.6 154.5 %all-gather.4.cloned.1.call-start = ((), (), s32[]{:S(2)}) async-start(), calls=%async_computation.11 | async-start | bytes 4718592 | tf_op jit(solution)/shard_map/all_gather | solution.py:743
  15.6 14.9 %collective-permute-start = (bf16[128,2048]{1,0:T(8,128)(2,1)S(1)}, bf16[128,2048]{1,0:T(8,128)(2,1)S(1)}, u32[]{:S(2)}, u32[]{:S(2)}) collective-permute-start(bf16[128,2048]{1,0:T(8,128)(2,1)S(1)} %bitcast.116), channel_id=1, source_target_pairs={{0,4},{4,0},{8,12},{12,8},{16,20},{20,16},{24,28},{28,24},{1,5},{5... | collective-permute-start | bytes 1572872 | tf_op jit(solution)/shard_map/ppermute | solution.py:657
  18.6 15.2 %collective-permute-start.1 = (bf16[128,2048]{1,0:T(8,128)(2,1)S(1)}, bf16[128,2048]{1,0:T(8,128)(2,1)S(1)}, u32[]{:S(2)}, u32[]{:S(2)}) collective-permute-start(bf16[128,2048]{1,0:T(8,128)(2,1)S(1)} %bitcast.117), channel_id=1, source_target_pairs={{0,8},{4,12},{8,16},{12,20},{16,24},{20,28},{24,0},{28,4},{1,9},{5... | collective-permute-start | bytes 1572872 | tf_op jit(solution)/shard_map/ppermute | solution.py:663
  34.7 12.8 %collective-permute-start.2 = (bf16[128,2048]{1,0:T(8,128)(2,1)}, bf16[128,2048]{1,0:T(8,128)(2,1)S(1)}, u32[]{:S(2)}, u32[]{:S(2)}) collective-permute-start(bf16[128,2048]{1,0:T(8,128)(2,1)} %after.16.refs_2_), channel_id=1, source_target_pairs={{0,4},{4,0},{8,12},{12,8},{16,20},{20,16},{24,28},{28,24},{1,5},{5... | collective-permute-start | bytes 1572872 | tf_op jit(solution)/shard_map/ppermute | solution.py:657
  35.2 14.5 %collective-permute-start.3 = (bf16[128,2048]{1,0:T(8,128)(2,1)}, bf16[128,2048]{1,0:T(8,128)(2,1)S(1)}, u32[]{:S(2)}, u32[]{:S(2)}) collective-permute-start(bf16[128,2048]{1,0:T(8,128)(2,1)} %after.16.refs_2_), channel_id=1, source_target_pairs={{0,8},{4,12},{8,16},{12,20},{16,24},{20,28},{24,0},{28,4},{1,9},{5... | collective-permute-start | bytes 1572872 | tf_op jit(solution)/shard_map/ppermute | solution.py:663
  51.6 11.6 %collective-permute-start.4 = (bf16[128,2048]{1,0:T(8,128)(2,1)S(1)}, bf16[128,2048]{1,0:T(8,128)(2,1)S(1)}, u32[]{:S(2)}, u32[]{:S(2)}) collective-permute-start(bf16[128,2048]{1,0:T(8,128)(2,1)S(1)} %copy-done.25), channel_id=1, source_target_pairs={{0,4},{4,0},{8,12},{12,8},{16,20},{20,16},{24,28},{28,24},{1,5},{5... | collective-permute-start | bytes 1572872 | tf_op jit(solution)/shard_map/ppermute | solution.py:657
  52.8 12.9 %collective-permute-start.5 = (bf16[128,2048]{1,0:T(8,128)(2,1)S(1)}, bf16[128,2048]{1,0:T(8,128)(2,1)S(1)}, u32[]{:S(2)}, u32[]{:S(2)}) collective-permute-start(bf16[128,2048]{1,0:T(8,128)(2,1)S(1)} %copy-done.25), channel_id=1, source_target_pairs={{0,8},{4,12},{8,16},{12,20},{16,24},{20,28},{24,0},{28,4},{1,9},{5... | collective-permute-start | bytes 1572872 | tf_op jit(solution)/shard_map/ppermute | solution.py:663
  66.5 51.4 %collective-permute-start.7 = (bf16[512,2048]{1,0:T(8,128)(2,1)}, bf16[512,2048]{1,0:T(8,128)(2,1)S(1)}, u32[]{:S(2)}, u32[]{:S(2)}) collective-permute-start(bf16[512,2048]{1,0:T(8,128)(2,1)} %after.19), channel_id=1, source_target_pairs={{0,2},{4,6},{9,11},{13,15},{18,16},{22,20},{27,25},{31,29}} | collective-permute-start | bytes 6291464 | tf_op jit(solution)/shard_map/ppermute | solution.py:664
  70.2 15.0 %collective-permute-start.6 = (bf16[128,2048]{1,0:T(8,128)(2,1)S(1)}, bf16[128,2048]{1,0:T(8,128)(2,1)}, u32[]{:S(2)}, u32[]{:S(2)}) collective-permute-start(bf16[128,2048]{1,0:T(8,128)(2,1)S(1)} %copy-done.22), channel_id=1, source_target_pairs={{0,4},{4,0},{8,12},{12,8},{16,20},{20,16},{24,28},{28,24},{1,5},{5... | collective-permute-start | bytes 1572872 | tf_op jit(solution)/shard_map/ppermute | solution.py:657
  97.8 19.3 %all-to-all-start = ((bf16[8,1,160,128]{3,2,1,0:T(8,128)(2,1)}), bf16[8,1,160,128]{3,2,1,0:T(8,128)(2,1)S(1)}, u32[]{:S(2)}, u32[]{:S(2)}) async-start(bf16[8,1,160,128]{3,2,1,0:T(8,128)(2,1)} %bitcast.131), calls=%async_computation | async-start | bytes 655360 | tf_op jit(solution)/shard_map/all_to_all | solution.py:677
  121.6 48.1 %copy-start.23 = (bf16[512,2048]{1,0:T(8,128)(2,1)}, bf16[512,2048]{1,0:T(8,128)(2,1)S(1)}, u32[]{:S(2)}) copy-start(bf16[512,2048]{1,0:T(8,128)(2,1)S(1)} %broadcast_select_fusion) | copy-start | bytes 6291460
  121.6 42.6 %collective-permute-start.8 = (bf16[512,2048]{1,0:T(8,128)(2,1)S(1)}, bf16[512,2048]{1,0:T(8,128)(2,1)}, u32[]{:S(2)}, u32[]{:S(2)}) collective-permute-start(bf16[512,2048]{1,0:T(8,128)(2,1)S(1)} %broadcast_select_fusion), channel_id=1, source_target_pairs={{0,1},{2,3},{4,5},{6,7},{9,8},{11,10},{13,12},{15,14},{18,19},{16,... | collective-permute-start | bytes 6291464 | tf_op jit(solution)/shard_map/ppermute | solution.py:668
  125.0 20.0 %all-to-all-start.1 = ((bf16[8,1,160,128]{3,2,1,0:T(8,128)(2,1)}), bf16[8,1,160,128]{3,2,1,0:T(8,128)(2,1)S(1)}, u32[]{:S(2)}, u32[]{:S(2)}) async-start(bf16[8,1,160,128]{3,2,1,0:T(8,128)(2,1)} %broadcast_in_dim.28), calls=%async_computation.1 | async-start | bytes 655360 | tf_op jit(solution)/shard_map/all_to_all | solution.py:680
  129.0 141.5 %reduce-scatter.5.cloned.1.call-start = ((), (), s32[]{:S(2)}) async-start(), calls=%async_computation.10 | async-start | bytes 4718592 | tf_op jit(solution)/shard_map/reduce_scatter | solution.py:751
  169.8 156.8 %reduce-scatter.7.cloned.1.call-start = ((), (), s32[]{:S(2)}) async-start(), calls=%async_computation.12 | async-start | bytes 2621440 | tf_op jit(solution)/shard_map/reduce_scatter | solution.py:771
  182.3 45.2 %collective-permute-start.9 = (bf16[8,64,512]{2,1,0:T(8,128)(2,1)S(1)}, bf16[8,64,512]{2,1,0:T(8,128)(2,1)S(1)}, u32[]{:S(2)}, u32[]{:S(2)}) collective-permute-start(bf16[8,64,512]{2,1,0:T(8,128)(2,1)S(1)} %get-tuple-element.120), channel_id=1, source_target_pairs={{0,1},{1,0},{2,3},{3,2},{4,5},{5,4},{6,7},{7,6},{8,9},{9,8},{10,11... | collective-permute-start | bytes 1572872 | tf_op jit(solution)/shard_map/ppermute | solution.py:694
  183.9 43.6 %collective-permute-start.10 = (bf16[8,64,512]{2,1,0:T(8,128)(2,1)S(1)}, bf16[8,64,512]{2,1,0:T(8,128)(2,1)S(1)}, u32[]{:S(2)}, u32[]{:S(2)}) collective-permute-start(bf16[8,64,512]{2,1,0:T(8,128)(2,1)S(1)} %get-tuple-element.119), channel_id=1, source_target_pairs={{0,2},{1,3},{2,0},{3,1},{4,6},{5,7},{6,4},{7,5},{8,10},{9,11},{10,... | collective-permute-start | bytes 1572872 | tf_op jit(solution)/shard_map/ppermute | solution.py:694
  185.6 42.0 %collective-permute-start.11 = (bf16[8,64,512]{2,1,0:T(8,128)(2,1)S(1)}, bf16[8,64,512]{2,1,0:T(8,128)(2,1)S(1)}, u32[]{:S(2)}, u32[]{:S(2)}) collective-permute-start(bf16[8,64,512]{2,1,0:T(8,128)(2,1)S(1)} %get-tuple-element.118), channel_id=1, source_target_pairs={{0,3},{1,2},{2,1},{3,0},{4,7},{5,6},{6,5},{7,4},{8,11},{9,10},{10,... | collective-permute-start | bytes 1572872 | tf_op jit(solution)/shard_map/ppermute | solution.py:694
  256.1 14.3 %all-to-all-start.3 = ((bf16[8,1,160,128]{3,2,1,0:T(8,128)(2,1)}), bf16[8,1,160,128]{3,2,1,0:T(8,128)(2,1)S(1)}, u32[]{:S(2)}, u32[]{:S(2)}) async-start(bf16[8,1,160,128]{3,2,1,0:T(8,128)(2,1)} %broadcast_in_dim.51), calls=%async_computation.4 | async-start | bytes 655360 | tf_op jit(solution)/shard_map/all_to_all | solution.py:680
  260.0 86.2 %reduce-scatter.9.cloned.1.call-start = ((), (), s32[]{:S(2)}) async-start(), calls=%async_computation.13 | async-start | bytes 2949120 | tf_op jit(solution)/shard_map/reduce_scatter | solution.py:785
  293.1 20.1 %copy-start.34 = (bf16[128,2048]{1,0:T(8,128)(2,1)S(1)}, bf16[128,2048]{1,0:T(8,128)(2,1)}, u32[]{:S(2)}) copy-start(bf16[128,2048]{1,0:T(8,128)(2,1)} %get-tuple-element.51) | copy-start | bytes 1572868
  294.1 19.1 %collective-permute-start.12 = (bf16[128,2048]{1,0:T(8,128)(2,1)S(1)}, bf16[128,2048]{1,0:T(8,128)(2,1)S(1)}, u32[]{:S(2)}, u32[]{:S(2)}) collective-permute-start(bf16[128,2048]{1,0:T(8,128)(2,1)S(1)} %copy-done.46), channel_id=1, source_target_pairs={{0,4},{4,0},{8,12},{12,8},{16,20},{20,16},{24,28},{28,24},{1,5},{5... | collective-permute-start | bytes 1572872 | tf_op jit(solution)/shard_map/ppermute | solution.py:784
  295.7 19.7 %all-to-all-start.4 = ((bf16[8,64,512]{2,1,0:T(8,128)(2,1)}), bf16[8,64,512]{2,1,0:T(8,128)(2,1)S(1)}, u32[]{:S(2)}, u32[]{:S(2)}) async-start(bf16[8,64,512]{2,1,0:T(8,128)(2,1)} %add_convert_fusion.3.refs_2_), calls=%async_computation.5 | async-start | bytes 1048576 | tf_op jit(solution)/shard_map/all_to_all | solution.py:761
  299.2 56.5 %reduce-scatter.11.cloned.1.call-start = ((), (), s32[]{:S(2)}) async-start(), calls=%async_computation.14 | async-start | bytes 819200 | tf_op jit(solution)/shard_map/reduce_scatter | solution.py:817
  299.2 23.8 %collective-permute-start.14 = (bf16[128,2048]{1,0:T(8,128)(2,1)S(1)}, bf16[128,2048]{1,0:T(8,128)(2,1)S(1)}, u32[]{:S(2)}, u32[]{:S(2)}) collective-permute-start(bf16[128,2048]{1,0:T(8,128)(2,1)S(1)} %copy-done.45), channel_id=1, source_target_pairs={{0,4},{4,0},{8,12},{12,8},{16,20},{20,16},{24,28},{28,24},{1,5},{5... | collective-permute-start | bytes 1572872 | tf_op jit(solution)/shard_map/ppermute | solution.py:784
  314.2 11.4 %collective-permute-start.13 = (bf16[128,2048]{1,0:T(8,128)(2,1)}, bf16[128,2048]{1,0:T(8,128)(2,1)S(1)}, u32[]{:S(2)}, u32[]{:S(2)}) collective-permute-start(bf16[128,2048]{1,0:T(8,128)(2,1)} %after.27), channel_id=1, source_target_pairs={{0,8},{4,12},{8,16},{12,20},{16,24},{20,28},{24,0},{28,4},{1,9},{5... | collective-permute-start | bytes 1572872 | tf_op jit(solution)/shard_map/ppermute | solution.py:794
  328.9 15.0 %collective-permute-start.16 = (bf16[128,2048]{1,0:T(8,128)(2,1)}, bf16[128,2048]{1,0:T(8,128)(2,1)}, u32[]{:S(2)}, u32[]{:S(2)}) collective-permute-start(bf16[128,2048]{1,0:T(8,128)(2,1)} %get-tuple-element.56), channel_id=1, source_target_pairs={{0,4},{4,0},{8,12},{12,8},{16,20},{20,16},{24,28},{28,24},{1,5},{5... | collective-permute-start | bytes 1572872 | tf_op jit(solution)/shard_map/ppermute | solution.py:784
  330.4 13.5 %collective-permute-start.15 = (bf16[128,2048]{1,0:T(8,128)(2,1)S(1)}, bf16[128,2048]{1,0:T(8,128)(2,1)}, u32[]{:S(2)}, u32[]{:S(2)}) collective-permute-start(bf16[128,2048]{1,0:T(8,128)(2,1)S(1)} %copy-done.7), channel_id=1, source_target_pairs={{0,8},{4,12},{8,16},{12,20},{16,24},{20,28},{24,0},{28,4},{1,9},{5... | collective-permute-start | bytes 1572872 | tf_op jit(solution)/shard_map/ppermute | solution.py:794
  331.5 37.6 %collective-permute-start.18 = (bf16[128,2048]{1,0:T(8,128)(2,1)}, bf16[128,2048]{1,0:T(8,128)(2,1)S(1)}, u32[]{:S(2)}, u32[]{:S(2)}) collective-permute-start(bf16[128,2048]{1,0:T(8,128)(2,1)} %get-tuple-element.59), channel_id=1, source_target_pairs={{0,4},{4,0},{8,12},{12,8},{16,20},{20,16},{24,28},{28,24},{1,5},{5... | collective-permute-start | bytes 1572872 | tf_op jit(solution)/shard_map/ppermute | solution.py:784
  346.2 23.0 %collective-permute-start.17 = (bf16[128,2048]{1,0:T(8,128)(2,1)}, bf16[128,2048]{1,0:T(8,128)(2,1)}, u32[]{:S(2)}, u32[]{:S(2)}) collective-permute-start(bf16[128,2048]{1,0:T(8,128)(2,1)} %after.29), channel_id=1, source_target_pairs={{0,8},{4,12},{8,16},{12,20},{16,24},{20,28},{24,0},{28,4},{1,9},{5... | collective-permute-start | bytes 1572872 | tf_op jit(solution)/shard_map/ppermute | solution.py:794
  346.2 22.0 %all-to-all-start.5 = ((bf16[8,72,512]{2,1,0:T(8,128)(2,1)}), bf16[8,72,512]{2,1,0:T(8,128)(2,1)S(1)}, u32[]{:S(2)}, u32[]{:S(2)}) async-start(bf16[8,72,512]{2,1,0:T(8,128)(2,1)} %bitcast.129), calls=%async_computation.8 | async-start | bytes 1179648 | tf_op jit(solution)/shard_map/all_to_all | solution.py:786
  (47 other events, 158.6 us)
Sparse Core Ops, SparseCore 0:
  15.7 45.3 all-gather.5
  63.2 81.0 all-gather.3
  169.9 91.1 reduce-scatter.4
  264.2 30.3 reduce-scatter.6
  297.0 33.0 reduce-scatter.8
  333.2 22.4 reduce-scatter.10
